TPU v7x, 256 devices: a whole 4x4x8 slice. The times are simulated.
256 devices in a mesh: dp: 64 (over y_lo, x, z), tensor: 4 (over y_hi, core).
Axes of the slice: x: 4, y: 4 (y_hi: 2, y_lo: 2; y = y_hi * 2 + y_lo), z: 8, core: 2. Of those that a mesh axis runs over, the one named last changes fastest.
Arguments:
- block_out: bfloat16 [65536, 3072], P(('dp', 'tensor')), may hold values from -70 to 70
- gate: float32 [64, 3072], P('dp'), may hold values from -4 to 4
- out_grad: bfloat16 [65536, 3072], P('dp', 'tensor'), may hold values from -8 to 8
- zero_weight: float32 [3072, 3072], P('dp', 'tensor'), may hold values from -0.109375 to 0.109375
- first_moment: float32 [3072, 3072], P('dp', 'tensor'), may hold values from -0.00012 to 0.00012
- second_moment: float32 [3072, 3072], P('dp', 'tensor'), may hold values from 1e-11 to 1e-09
Outputs:
- stream_grad: bfloat16 [65536, 3072], P(('dp', 'tensor'))
- branch_grad: bfloat16 [65536, 3072], P(('dp', 'tensor'))
- zero_step: float32 [3072, 3072], P('dp', 'tensor')
All inputs are finite; a program needn't handle non-finite values.
Results may differ from a plain program's by a relative error of at most 0.015.
Values may be sent and summed in bfloat16 or wider, within the bound.
No kernel may reach another device: no remote copies, remote signals or barrier semaphores. Data moves between devices by JAX's collectives and lax.ppermute only.
A program may use at most 128 MiB of HBM per device.

v0:
```python
import jax
import jax.numpy as jnp
from jax import lax
from jax.sharding import PartitionSpec as P

beta_one = 0.9
beta_two = 0.999
bias_one = 1.0 - 0.9**10
bias_two = 1.0 - 0.999**10
epsilon = 1e-08
decay_rate = 0.1
max_norm = 1.0


def body(block_out, gate, out_grad, zero_weight, first_moment, second_moment):
    full_weight = lax.all_gather(zero_weight.astype(jnp.bfloat16), "dp", axis=0, tiled=True)
    stream = lax.psum_scatter(
        lax.dot_general(
            out_grad, full_weight, (((1,), (1,)), ((), ())), preferred_element_type=jnp.float32
        ).astype(jnp.bfloat16),
        "tensor",
        scatter_dimension=0,
        tiled=True,
    ).astype(jnp.float32)
    local_grad = lax.dot_general(
        lax.all_gather(block_out, "tensor", axis=0, tiled=True),
        out_grad,
        (((0,), (0,)), ((), ())),
        preferred_element_type=jnp.float32,
    )
    owner_grad = lax.psum_scatter(local_grad, "dp", scatter_dimension=0, tiled=True)
    norm_sq = lax.psum(jnp.sum(owner_grad * owner_grad), ("dp", "tensor"))
    factor = jnp.minimum(1.0, max_norm / (jnp.sqrt(norm_sq) + 1e-06))
    clipped = factor * owner_grad
    first = beta_one * first_moment + (1.0 - beta_one) * clipped
    second = beta_two * second_moment + (1.0 - beta_two) * clipped * clipped
    update = first / bias_one / (jnp.sqrt(second / bias_two) + epsilon) + decay_rate * zero_weight
    stream_out = stream.astype(jnp.bfloat16)
    branch_out = (gate * stream).astype(jnp.bfloat16)
    return (stream_out, branch_out, update)


def solution(mesh):
    placed = (
        P(("dp", "tensor"), None),
        P("dp", None),
        P("dp", "tensor"),
        P("dp", "tensor"),
        P("dp", "tensor"),
        P("dp", "tensor"),
    )
    return jax.shard_map(
        body,
        mesh=mesh,
        in_specs=placed,
        out_specs=(P(("dp", "tensor"), None), P(("dp", "tensor"), None), P("dp", "tensor")),
        check_vma=False,
    )
```

profile of v0, /device:TPU:1, one launch (start us, length us, event | category | flops | bytes accessed | tf_op | source)
XLA Modules:
  0.0 875.8 jit_solution(13060087053466533779)
XLA Ops:
  7.2 0.0 copy-start
  7.2 0.0 all-gather.5.cloned.1.call-start
  7.2 0.7 all-gather.5.cloned.1.call-update
  7.9 0.0 reduce-scatter.5.cloned.1.call-start
  8.0 59.1 %all-gather.5.cloned.1.call-done = bf16[1024,3072]{1,0:T(8,128)(2,1)} async-done(((bf16[256,3072]{1,0:T(8,128)(2,1)}), bf16[1024,3072]{1,0:T(8,128)(2,1)}) %all-gather.5.cloned.1.call-update) | async-done | bytes 6291472 | tf_op jit(solution)/shard_map/all_gather | solution.py:26
  67.1 0.0 copy-done
  67.1 10.2 %fusion.6 = f32[3072,768]{1,0:T(8,128)} fusion(bf16[1024,3072]{1,0:T(8,128)(2,1)} %all-gather.5.cloned.1.call-done, bf16[1024,768]{1,0:T(8,128)(2,1)S(1)} %copy-done), kind=kOutput, calls=%fused_computation.10 | convolution fusion | flops 4831838208 | bytes 17301504 | tf_op jit(solution)/shard_map/dot_general | solution.py:25
  77.3 0.0 copy-start.1
  77.3 0.0 copy-start.2
  77.3 0.0 copy-start.3
  77.3 0.0 reduce-scatter.5.cloned.1.call-update
  77.3 0.0 all-gather.3.cloned.1.call-start
  77.4 287.2 %reduce-scatter.5.cloned.1.call-done = f32[48,768]{1,0:T(8,128)} async-done(((f32[3072,768]{1,0:T(8,128)}), f32[48,768]{1,0:T(8,128)}) %reduce-scatter.5.cloned.1.call-update) | async-done | bytes 147472 | tf_op jit(solution)/shard_map/reduce_scatter | solution.py:31
  364.6 1.6 multiply_reduce_fusion
  366.1 120.5 %psum.7 = f32[]{:T(128)} all-reduce(f32[]{:T(128)} %multiply_reduce_fusion), channel_id=1, replica_groups=mesh['dp'=64,'tensor'=4] {'dp','tensor'}, use_global_device_ids=true, to_apply=%region_3.0 | all-reduce | flops 1 | bytes 8 | tf_op jit(solution)/shard_map/psum | solution.py:32
  487.3 0.0 copy-done.1
  487.4 0.0 copy-done.2
  487.4 0.0 copy-done.3
  487.4 1.7 fusion.5
  489.1 0.0 all-gather.3.cloned.1.call-update
  489.1 0.0 reduce-scatter.3.cloned.1.call-start
  489.1 257.7 %all-gather.3.cloned.1.call-done = bf16[3072,768]{1,0:T(8,128)(2,1)} async-done(((bf16[48,768]{1,0:T(8,128)(2,1)}), bf16[3072,768]{1,0:T(8,128)(2,1)}) %all-gather.3.cloned.1.call-update) | async-done | bytes 4718608 | tf_op jit(solution)/shard_map/all_gather | solution.py:16
  746.9 9.3 %convolution_convert_fusion = bf16[1024,3072]{1,0:T(8,128)(2,1)} fusion(bf16[1024,768]{1,0:T(8,128)(2,1)S(1)} %copy-done, bf16[3072,768]{1,0:T(8,128)(2,1)} %all-gather.3.cloned.1.call-done), kind=kOutput, calls=%fused_computation | convolution fusion | flops 4834983936 | bytes 12582912 | tf_op jit(solution)/shard_map/dot_general | solution.py:18
  756.2 0.0 copy-start.4
  756.2 0.0 reduce-scatter.3.cloned.1.call-update
  756.2 110.1 %reduce-scatter.3.cloned.1.call-done = bf16[256,3072]{1,0:T(8,128)(2,1)} async-done(((bf16[1024,3072]{1,0:T(8,128)(2,1)}), bf16[256,3072]{1,0:T(8,128)(2,1)}) %reduce-scatter.3.cloned.1.call-update) | async-done | bytes 1572880 | tf_op jit(solution)/shard_map/reduce_scatter | solution.py:17
  866.3 0.0 copy-done.4
  866.3 2.9 multiply_convert_fusion
Async XLA Ops:
  7.2 59.9 %copy-start = (bf16[1024,768]{1,0:T(8,128)(2,1)S(1)}, bf16[1024,768]{1,0:T(8,128)(2,1)}, u32[]{:S(2)}) copy-start(bf16[1024,768]{1,0:T(8,128)(2,1)} %param.8) | copy-start | bytes 4718596
  7.2 59.9 %all-gather.5.cloned.1.call-start = ((), (), s32[]{:S(2)}) async-start(), calls=%async_computation.4 | async-start | bytes 7864320 | tf_op jit(solution)/shard_map/all_gather | solution.py:26
  7.9 356.7 %reduce-scatter.5.cloned.1.call-start = ((), (), s32[]{:S(2)}) async-start(), calls=%async_computation.5 | async-start | bytes 9584640 | tf_op jit(solution)/shard_map/reduce_scatter | solution.py:31
  77.3 410.0 %copy-start.1 = (f32[48,768]{1,0:T(8,128)S(1)}, f32[48,768]{1,0:T(8,128)}, u32[]{:S(2)}) copy-start(f32[48,768]{1,0:T(8,128)} %param.9) | copy-start | bytes 442372
  77.3 410.0 %copy-start.2 = (f32[48,768]{1,0:T(8,128)S(1)}, f32[48,768]{1,0:T(8,128)}, u32[]{:S(2)}) copy-start(f32[48,768]{1,0:T(8,128)} %param.11) | copy-start | bytes 442372
  77.3 410.0 %copy-start.3 = (f32[48,768]{1,0:T(8,128)S(1)}, f32[48,768]{1,0:T(8,128)}, u32[]{:S(2)}) copy-start(f32[48,768]{1,0:T(8,128)} %param.10) | copy-start | bytes 442372
  77.3 669.5 %all-gather.3.cloned.1.call-start = ((), (), s32[]{:S(2)}) async-start(), calls=%async_computation.2 | async-start | bytes 4792320 | tf_op jit(solution)/shard_map/all_gather | solution.py:16
  489.1 377.2 %reduce-scatter.3.cloned.1.call-start = ((), (), s32[]{:S(2)}) async-start(), calls=%async_computation.3 | async-start | bytes 7864320 | tf_op jit(solution)/shard_map/reduce_scatter | solution.py:17
  756.2 110.1 %copy-start.4 = (f32[1,3072]{1,0:T(1,128)S(1)}, f32[1,3072]{1,0:T(1,128)}, u32[]{:S(2)}) copy-start(f32[1,3072]{1,0:T(1,128)} %param.7) | copy-start | bytes 36868
Sparse Core Ops, SparseCore 0:
  9.8 57.2 all-gather.4
  77.5 287.0 reduce-scatter.4
  489.2 257.6 all-gather.2
  756.3 109.9 reduce-scatter.2
where the time goes:
time: 876 us
  waiting for transfers between devices  715 us (82%)
  blocking collectives  120 us (14%)
  matrix products  19.5 us (2%)
  between operations  14.5 us (2%)
    reduce_scatter x1, waiting for transfers between devices, body(): lax.psum_scatter(local_grad, 'dp', scatter_dimension=0, tiled=True)  287 us
    all_gather x1, waiting for transfers between devices, body(): lax.all_gather(zero_weight.astype(jnp.bfloat16), 'dp', axis=0, tiled=True)  258 us
    psum x1, blocking collectives, body(): norm_sq = lax.psum(jnp.sum(owner_grad * owner_grad), ('dp', 'tensor'))  120 us
    reduce_scatter x1, waiting for transfers between devices, body(): lax.psum_scatter(lax.dot_general(out_grad, full_weight, (((1,), (1,)), ((...  110 us
    all_gather x1, waiting for transfers between devices, body(): lax.all_gather(block_out, 'tensor', axis=0, tiled=True)  59.1 us
  transfers between devices with their start and end apart: 4, of which 4 were waited for; matrix products, arithmetic and copies ran while one was open for 0% of the time, Pallas kernels for 0%

commit v1 on v0

v1 whole, which is shorter than its diff:
```python
import jax
import jax.numpy as jnp
from jax import lax
from jax.experimental import pallas as pl
from jax.experimental.pallas import tpu as pltpu
from jax.sharding import Mesh, PartitionSpec as P

beta_one = 0.9
beta_two = 0.999
bias_one = 1.0 - 0.9**10
bias_two = 1.0 - 0.999**10
epsilon = 1e-08
decay_rate = 0.1
max_norm = 1.0

AXES = ("yl", "x", "z", "yh", "c")
SIZES = (2, 4, 8, 2, 2)
NZ = 8
NXY = 8
OWN = 48
WIDTH = 768
HALF = 384
D = 3072
TOK = 256
F32 = jnp.float32
BF16 = jnp.bfloat16


def index_of(yl, x, z, yh, c):
    return (((yl * 4 + x) * 8 + z) * 2 + yh) * 2 + c


def pairs(move):
    out = []
    for yl in range(2):
        for x in range(4):
            for z in range(8):
                for yh in range(2):
                    for c in range(2):
                        out.append((index_of(yl, x, z, yh, c), index_of(*move(yl, x, z, yh, c))))
    return out


SWAP_CORE = pairs(lambda yl, x, z, yh, c: (yl, x, z, yh, 1 - c))
SWAP_YH = pairs(lambda yl, x, z, yh, c: (yl, x, z, 1 - yh, c))
Z_UP = pairs(lambda yl, x, z, yh, c: (yl, x, (z + 1) % 8, yh, c))
Z_DOWN = pairs(lambda yl, x, z, yh, c: (yl, x, (z - 1) % 8, yh, c))


def send(value, perm):
    return lax.ppermute(value, AXES, perm)


def gather(value, axes, n):
    return lax.all_to_all(jnp.broadcast_to(value[None], (n,) + value.shape), axes, 0, 0, tiled=True)


def gather_ring_z(block, zi):
    half = NXY // 2
    full = jnp.zeros((NXY, NZ) + block.shape[1:], block.dtype)

    def put(full, piece, offset, first=0):
        at = lax.rem(zi + offset + NZ, NZ)
        return lax.dynamic_update_slice(full, piece[:, None], (first, at, 0, 0))

    full = put(full, block, 0)
    up, down = block, block
    for step in range(1, 4):
        up, down = send(up, Z_UP), send(down, Z_DOWN)
        full = put(put(full, up, -step), down, step)
    up, down = send(up[:half], Z_UP), send(down[half:], Z_DOWN)
    return put(put(full, up, 4), down, 4, half)


def scatter_ring_z(parts, zi):
    half = NXY // 2

    def chunk(offset):
        at = lax.rem(zi + offset + NZ, NZ)
        return lax.dynamic_slice_in_dim(parts, at, 1, 1)[:, 0]

    far = chunk(4)
    up, down = send(far[:half], Z_UP), send(far[half:], Z_DOWN)
    here_up, here_down = chunk(3).astype(F32), chunk(-3).astype(F32)
    here_up = jnp.concatenate([here_up[:half] + up.astype(F32), here_up[half:]]).astype(BF16)
    here_down = jnp.concatenate([here_down[:half], here_down[half:] + down.astype(F32)]).astype(BF16)
    for offset in (2, 1):
        up, down = send(here_up, Z_UP), send(here_down, Z_DOWN)
        here_up = (chunk(offset).astype(F32) + up.astype(F32)).astype(BF16)
        here_down = (chunk(-offset).astype(F32) + down.astype(F32)).astype(BF16)
    up, down = send(here_up, Z_UP), send(here_down, Z_DOWN)
    return chunk(0).astype(F32) + up.astype(F32) + down.astype(F32)


def grad_kernel(b0, b1, b2, b3, og, out_a, out_b):
    total = None
    for k, block in enumerate((b0, b1, b2, b3)):
        term = lax.dot_general(
            block[...], og[k * TOK : (k + 1) * TOK, :], (((0,), (0,)), ((), ())), preferred_element_type=F32
        )
        total = term if total is None else total + term
    out_a[...] = total[:, :HALF].astype(BF16)
    out_b[...] = total[:, HALF:].astype(BF16)


def weight_grad(blocks, og):
    tile = 512
    return pl.pallas_call(
        grad_kernel,
        grid=(D // tile,),
        in_specs=[pl.BlockSpec((TOK, tile), lambda i: (0, i))] * 4 + [pl.BlockSpec((4 * TOK, WIDTH), lambda i: (0, 0))],
        out_specs=[pl.BlockSpec((tile, HALF), lambda i: (i, 0))] * 2,
        out_shape=[jax.ShapeDtypeStruct((D, HALF), BF16)] * 2,
        compiler_params=pltpu.CompilerParams(vmem_limit_bytes=40 * 1024 * 1024),
        cost_estimate=pl.CostEstimate(flops=2 * 4 * TOK * WIDTH * D, bytes_accessed=13 * 1024 * 1024, transcendentals=0),
        name="weight_grad",
    )(*blocks, og)


def stream_kernel(og, wa, wb, out):
    total = lax.dot_general(og[:, :HALF], wa[...], (((1,), (1,)), ((), ())), preferred_element_type=F32)
    total += lax.dot_general(og[:, HALF:], wb[...], (((1,), (1,)), ((), ())), preferred_element_type=F32)
    out[...] = total.astype(BF16)


def stream_part(og, wa, wb):
    tile = 768
    return pl.pallas_call(
        stream_kernel,
        grid=(D // tile,),
        in_specs=[
            pl.BlockSpec((TOK, WIDTH), lambda i: (0, 0)),
            pl.BlockSpec((tile, HALF), lambda i: (i, 0)),
            pl.BlockSpec((tile, HALF), lambda i: (i, 0)),
        ],
        out_specs=pl.BlockSpec((TOK, tile), lambda i: (0, i)),
        out_shape=jax.ShapeDtypeStruct((TOK, D), BF16),
        compiler_params=pltpu.CompilerParams(vmem_limit_bytes=40 * 1024 * 1024),
        cost_estimate=pl.CostEstimate(flops=2 * TOK * WIDTH * D, bytes_accessed=7 * 1024 * 1024, transcendentals=0),
        name="stream_part",
    )(og, wa, wb)


def body(block_out, gate, out_grad, zero_weight, first_moment, second_moment):
    zi = lax.axis_index("z")
    ti = lax.axis_index("yh") * 2 + lax.axis_index("c")

    order = [lax.dynamic_slice_in_dim(out_grad, lax.bitwise_xor(ti, k) * TOK, TOK, 0) for k in range(4)]

    with jax.named_scope("block_out"):
        far = send(block_out, SWAP_YH)
        near = send(block_out, SWAP_CORE)
        far_near = send(far, SWAP_CORE)

    weight = zero_weight.astype(BF16)
    with jax.named_scope("weight_gather"):
        rows_a = gather(weight[:, :HALF], ("z",), NZ)
        rows_b = gather(weight[:, HALF:], ("yl", "x"), NXY).reshape(NXY, OWN, HALF)
        weight_a = gather(rows_a, ("yl", "x"), NXY).reshape(D, HALF)
        weight_b = gather_ring_z(rows_b, zi).reshape(D, HALF)

    with jax.named_scope("weight_grad"):
        grad_a, grad_b = weight_grad((block_out, near, far, far_near), jnp.concatenate(order))
        grad_a = grad_a.reshape(NXY, NZ, OWN, HALF)
        grad_b = grad_b.reshape(NXY, NZ, OWN, HALF)

    with jax.named_scope("grad_scatter"):
        got_a = lax.all_to_all(grad_a, ("yl", "x"), 0, 0, tiled=True)
        sum_b = scatter_ring_z(grad_b, zi).astype(BF16)
        sum_a = jnp.sum(got_a.astype(F32), axis=0).astype(BF16)
        got_a = lax.all_to_all(sum_a, ("z",), 0, 0, tiled=True)
        got_b = lax.all_to_all(sum_b, ("yl", "x"), 0, 0, tiled=True)
        own_a = jnp.sum(got_a.astype(F32), axis=0)
        own_b = jnp.sum(got_b.astype(F32), axis=0)
        owner_grad = jnp.concatenate([own_a, own_b], axis=1)

    with jax.named_scope("stream"):
        p3 = stream_part(order[3], weight_a, weight_b)
        r3 = send(p3, SWAP_CORE)
        p2 = stream_part(order[2], weight_a, weight_b)
        s2 = (p2.astype(F32) + r3.astype(F32)).astype(BF16)
        q2 = send(s2, SWAP_YH)
        p1 = stream_part(order[1], weight_a, weight_b)
        r1 = send(p1, SWAP_CORE)
        p0 = stream_part(order[0], weight_a, weight_b)
        stream = p0.astype(F32) + r1.astype(F32) + q2.astype(F32)
        stream_out = stream.astype(BF16)
        branch_out = (gate * stream).astype(BF16)

    with jax.named_scope("norm"):
        local = jnp.sum(owner_grad * owner_grad)
        local = gather(jnp.full((8, 128), local, F32), ("yl", "x", "yh", "c"), 32)
        local = jnp.sum(local, axis=0)
        norm_sq = jnp.sum(gather(local, ("z",), NZ), axis=0)[:1, :1]

    factor = jnp.minimum(1.0, max_norm / (jnp.sqrt(norm_sq) + 1e-06))
    clipped = factor * owner_grad
    first = beta_one * first_moment + (1.0 - beta_one) * clipped
    second = beta_two * second_moment + (1.0 - beta_two) * clipped * clipped
    update = first / bias_one / (jnp.sqrt(second / bias_two) + epsilon) + decay_rate * zero_weight
    return (stream_out, branch_out, update)


def solution(mesh):
    fine = Mesh(mesh.devices.reshape(SIZES), AXES)
    dp, tensor = ("yl", "x", "z"), ("yh", "c")
    placed = (P(AXES, None), P(dp, None), P(dp, tensor), P(dp, tensor), P(dp, tensor), P(dp, tensor))
    return jax.shard_map(
        body,
        mesh=fine,
        in_specs=placed,
        out_specs=(P(AXES, None), P(AXES, None), P(dp, tensor)),
        check_vma=False,
    )
```

time: 876 us -> 274 us (0.31)
  waiting for transfers between devices: 715 us -> 120 us
  blocking collectives: 120 us -> 38.7 us
  starting transfers between devices: 0.16 us -> 58.8 us
  matrix products: 19.5 us -> 0 us
  local copies, waits for them, and re-layouts: 0.02 us -> 18.7 us
  Pallas kernels: 0 us -> 17.4 us
  between operations: 14.5 us -> 1.73 us
  other arithmetic: 6.15 us -> 17.1 us
    reduce_scatter x2 -> x0, waiting for transfers between devices: 397 us -> none  [the longest x1 287 us: body(): lax.psum_scatter(local_grad, 'dp', scatter_dimension=0, tiled=True)]
    all_gather x2 -> x0, waiting for transfers between devices: 317 us -> none  [the longest x1 258 us: body(): lax.all_gather(zero_weight.astype(jnp.bfloat16), 'dp', axis=0, tiled=True)]
    psum x1 -> x0, blocking collectives: 120 us -> none  [body(): norm_sq = lax.psum(jnp.sum(owner_grad * owner_grad), ('dp', 'tensor'))]
    ppermute x0 -> x22, waiting for transfers between devices: none -> 96.6 us  [send(): return lax.ppermute(value, AXES, perm)]
    all_to_all x0 -> x3, blocking collectives: none -> 38.7 us  [gather(): lax.all_to_all(jnp.broadcast_to(value[None], (n,) + value.shape), axes, 0...]
    ppermute x0 -> x22, starting transfers between devices: none -> 37.5 us  [send(): return lax.ppermute(value, AXES, perm)]
    all_to_all x0 -> x5, waiting for transfers between devices: none -> 23.4 us  [the longest x2 10.4 us: gather(): lax.all_to_all(jnp.broadcast_to(value[None], (n,) + value.shape), axes, 0...]
    all_to_all x0 -> x5, starting transfers between devices: none -> 21.3 us  [the longest x2 7.04 us: gather(): lax.all_to_all(jnp.broadcast_to(value[None], (n,) + value.shape), axes, 0...]
  transfers between devices with their start and end apart: 4 -> 27, of which waited for: 4 -> 14; matrix products, arithmetic and copies ran while one was open for 0% -> 8% of each run, Pallas kernels for 0% -> 3%
where the time goes in v1:
time: 274 us; the launch traced here: 272 us
  waiting for transfers between devices  120 us (44%)
  starting transfers between devices  58.8 us (21%)
  blocking collectives  38.7 us (14%)
  local copies, waits for them, and re-layouts  18.7 us (7%)
  Pallas kernels  17.4 us (6%)
  other arithmetic  17.1 us (6%)
    ppermute x22, waiting for transfers between devices, send(): return lax.ppermute(value, AXES, perm)  96.6 us
    all_to_all x3, blocking collectives, gather(): lax.all_to_all(jnp.broadcast_to(value[None], (n,) + value.shape), axes, 0...  38.7 us
    ppermute x22, starting transfers between devices, send(): return lax.ppermute(value, AXES, perm)  37.5 us
    all_to_all x2, waiting for transfers between devices, gather(): lax.all_to_all(jnp.broadcast_to(value[None], (n,) + value.shape), axes, 0...  10.4 us
    pallas_call x4, Pallas kernels, stream_part(): pl.pallas_call(stream_kernel, grid=(D // tile,), in_specs=[pl.BlockSpec((...  9.86 us
    all_to_all x1, waiting for transfers between devices, body(): got_a = lax.all_to_all(sum_a, ('z',), 0, 0, tiled=True)  9.64 us
    unnamed x24, local copies, waits for them, and re-layouts  7.68 us
    pallas_call x1, Pallas kernels, weight_grad(): pl.pallas_call(grad_kernel, grid=(D // tile,), in_specs=[pl.BlockSpec((TO...  7.49 us
  transfers between devices with their start and end apart: 27, of which 14 were waited for; matrix products, arithmetic and copies ran while one was open for 8% of the time, Pallas kernels for 3%

profile of v1, /device:TPU:1, one launch (start us, length us, event | category | flops | bytes accessed | tf_op | source)
XLA Modules:
  0.0 272.5 jit_solution(3581932696666602648)
XLA Ops:
  0.6 3.8 %collective-permute-start.12 = (bf16[256,3072]{1,0:T(8,128)(2,1)}, bf16[256,3072]{1,0:T(8,128)(2,1)S(1)}, u32[]{:S(2)}, u32[]{:S(2)}) collective-permute-start(bf16[256,3072]{1,0:T(8,128)(2,1)} %b0.1), channel_id=1, source_target_pairs={{0,2},{1,3},{2,0},{3,1},{4,6},{5,7},{6,4},{7,5},{8,10},{9,11},{10,... | collective-permute-start | bytes 4718600 | tf_op jit(solution)/shard_map/block_out/ppermute | solution.py:51
  5.4 32.4 %collective-permute-done.12.b2 = bf16[256,3072]{1,0:T(8,128)(2,1)S(1)} collective-permute-done((bf16[256,3072]{1,0:T(8,128)(2,1)}, bf16[256,3072]{1,0:T(8,128)(2,1)S(1)}, u32[]{:S(2)}, u32[]{:S(2)}) %collective-permute-start.12) | collective-permute-done | bytes 1572896 | tf_op jit(solution)/shard_map/block_out/ppermute | solution.py:51
  44.6 7.5 %weight_grad.1 = (bf16[3072,384]{1,0:T(8,128)(2,1)S(1)}, bf16[3072,384]{1,0:T(8,128)(2,1)S(1)}) custom-call(bf16[256,3072]{1,0:T(8,128)(2,1)S(1)} %copy-done.5, bf16[256,3072]{1,0:T(8,128)(2,1)} %collective-permute-done.11.b1, bf16[256,3072]{1,0:T(8,128)(2,1)S(1)} %copy-done.7, bf16[256,3072]{1,0:T(8,128)(2,1)} %collective-permute-done.13.b3, ...), custom_call_target="tpu_custom_call" | custom-call | flops 4831838208 | bytes 13631488 | tf_op jit(solution)/shard_map/weight_grad/weight_grad/pallas_call | solution.py:108
  56.0 3.9 %collective-permute-start.18 = (bf16[4,48,384]{2,1,0:T(8,128)(2,1)}, bf16[4,48,384]{2,1,0:T(8,128)(2,1)}, u32[]{:S(2)}, u32[]{:S(2)}) collective-permute-start(bf16[4,48,384]{2,1,0:T(8,128)(2,1)} %get-tuple-element.16), channel_id=1, source_target_pairs={{0,28},{1,29},{2,30},{3,31},{4,0},{5,1},{6,2},{7,3},{8,4},{9,5},{1... | collective-permute-start | bytes 442376 | tf_op jit(solution)/shard_map/grad_scatter/ppermute | solution.py:51
  60.7 5.0 %all-to-all-start.3 = ((bf16[8,8,48,384]{3,2,1,0:T(8,128)(2,1)}), bf16[8,8,48,384]{3,2,1,0:T(8,128)(2,1)}, u32[]{:S(2)}, u32[]{:S(2)}) async-start(bf16[8,8,48,384]{3,2,1,0:T(8,128)(2,1)} %bitcast.109), calls=%async_computation.3 | async-start | bytes 4718592 | tf_op jit(solution)/shard_map/grad_scatter/all_to_all | solution.py:168
  71.6 4.7 %collective-permute-done.19 = bf16[8,48,384]{2,1,0:T(8,128)(2,1)} collective-permute-done((bf16[8,48,384]{2,1,0:T(8,128)(2,1)}, bf16[8,48,384]{2,1,0:T(8,128)(2,1)}, u32[]{:S(2)}, u32[]{:S(2)}) %collective-permute-start.19) | collective-permute-done | bytes 294944 | tf_op jit(solution)/shard_map/grad_scatter/ppermute | solution.py:51
  76.3 3.8 %collective-permute-done.15 = bf16[8,48,384]{2,1,0:T(8,128)(2,1)} collective-permute-done((bf16[8,48,384]{2,1,0:T(8,128)(2,1)}, bf16[8,48,384]{2,1,0:T(8,128)(2,1)}, u32[]{:S(2)}, u32[]{:S(2)}) %collective-permute-start.15) | collective-permute-done | bytes 294944 | tf_op jit(solution)/shard_map/grad_scatter/ppermute | solution.py:51
  82.1 2.7 collective-permute-start.20
  84.8 4.9 %collective-permute-done.16 = bf16[8,48,384]{2,1,0:T(8,128)(2,1)} collective-permute-done((bf16[8,48,384]{2,1,0:T(8,128)(2,1)}, bf16[8,48,384]{2,1,0:T(8,128)(2,1)}, u32[]{:S(2)}, u32[]{:S(2)}) %collective-permute-start.16) | collective-permute-done | bytes 294944 | tf_op jit(solution)/shard_map/grad_scatter/ppermute | solution.py:51
  91.7 2.7 collective-permute-start.21
  94.4 4.4 %collective-permute-done.17 = bf16[8,48,384]{2,1,0:T(8,128)(2,1)} collective-permute-done((bf16[8,48,384]{2,1,0:T(8,128)(2,1)}, bf16[8,48,384]{2,1,0:T(8,128)(2,1)}, u32[]{:S(2)}, u32[]{:S(2)}) %collective-permute-start.17) | collective-permute-done | bytes 294944 | tf_op jit(solution)/shard_map/grad_scatter/ppermute | solution.py:51
  100.7 4.4 %all-to-all-start.5 = ((bf16[8,48,384]{2,1,0:T(8,128)(2,1)}), bf16[8,48,384]{2,1,0:T(8,128)(2,1)S(1)}, u32[]{:S(2)}, u32[]{:S(2)}) async-start(bf16[8,48,384]{2,1,0:T(8,128)(2,1)} %fusion.6), calls=%async_computation.5 | async-start | bytes 589824 | tf_op jit(solution)/shard_map/grad_scatter/all_to_all | solution.py:172
  105.1 2.9 %reduce_sum.57 = bf16[8,48,384]{2,1,0:T(8,128)(2,1)} reduce(bf16[8,8,48,384]{3,2,1,0:T(8,128)(2,1)} %all-to-all-done.3, bf16[]{:T(256)} %constant.62.clone.1), dimensions={0}, to_apply=%region_0.0 | reduce | flops 1032192 | bytes 2654210 | tf_op jit(solution)/shard_map/grad_scatter/reduce_sum | solution.py:170
  108.0 3.4 %all-to-all-done.5 = bf16[8,48,384]{2,1,0:T(8,128)(2,1)S(1)} async-done(((bf16[8,48,384]{2,1,0:T(8,128)(2,1)}), bf16[8,48,384]{2,1,0:T(8,128)(2,1)S(1)}, u32[]{:S(2)}, u32[]{:S(2)}) %all-to-all-start.5) | async-done | bytes 294944 | tf_op jit(solution)/shard_map/grad_scatter/all_to_all | solution.py:172
  111.4 4.9 %all-to-all-start.4 = ((bf16[8,48,384]{2,1,0:T(8,128)(2,1)}), bf16[8,48,384]{2,1,0:T(8,128)(2,1)S(1)}, u32[]{:S(2)}, u32[]{:S(2)}) async-start(bf16[8,48,384]{2,1,0:T(8,128)(2,1)} %reduce_sum.57), calls=%async_computation.4 | async-start | bytes 589824 | tf_op jit(solution)/shard_map/grad_scatter/all_to_all | solution.py:171
  116.3 9.6 %all-to-all-done.4 = bf16[8,48,384]{2,1,0:T(8,128)(2,1)S(1)} async-done(((bf16[8,48,384]{2,1,0:T(8,128)(2,1)}), bf16[8,48,384]{2,1,0:T(8,128)(2,1)S(1)}, u32[]{:S(2)}, u32[]{:S(2)}) %all-to-all-start.4) | async-done | bytes 294944 | tf_op jit(solution)/shard_map/grad_scatter/all_to_all | solution.py:171
  127.3 19.8 %all_to_all.40 = f32[32,8,128]{2,1,0:T(8,128)S(1)} all-to-all(f32[32,8,128]{2,1,0:T(8,128)S(1)} %broadcast_in_dim.70), channel_id=1, replica_groups=mesh['yl'=2,'x'=4,'z'=8,'yh'=2,'c'=2] {'yl','x','yh','c'}, dimensions={0} | all-to-all | bytes 262144 | tf_op jit(solution)/shard_map/norm/all_to_all | solution.py:55
  147.2 9.2 %all_to_all.41 = f32[8,8,128]{2,1,0:T(8,128)S(1)} all-to-all(f32[8,8,128]{2,1,0:T(8,128)S(1)} %broadcast_in_dim.71), channel_id=1, replica_groups=mesh['yl'=2,'x'=4,'z'=8,'yh'=2,'c'=2] {'z'}, dimensions={0} | all-to-all | bytes 65536 | tf_op jit(solution)/shard_map/norm/all_to_all | solution.py:55
  158.6 9.7 %all_to_all.42 = bf16[8,48,384]{2,1,0:T(8,128)(2,1)} all-to-all(bf16[8,48,384]{2,1,0:T(8,128)(2,1)S(1)} %broadcast_in_dim.60), channel_id=1, replica_groups=mesh['yl'=2,'x'=4,'z'=8,'yh'=2,'c'=2] {'yl','x'}, dimensions={0} | all-to-all | bytes 589824 | tf_op jit(solution)/shard_map/weight_gather/all_to_all | solution.py:55
  169.0 3.4 %all-to-all-start = ((bf16[8,48,384]{2,1,0:T(8,128)(2,1)}), bf16[8,48,384]{2,1,0:T(8,128)(2,1)S(1)}, u32[]{:S(2)}, u32[]{:S(2)}) async-start(bf16[8,48,384]{2,1,0:T(8,128)(2,1)} %broadcast_in_dim.57), calls=%async_computation | async-start | bytes 589824 | tf_op jit(solution)/shard_map/weight_gather/all_to_all | solution.py:55
  175.1 6.9 %all-to-all-done = bf16[8,48,384]{2,1,0:T(8,128)(2,1)S(1)} async-done(((bf16[8,48,384]{2,1,0:T(8,128)(2,1)}), bf16[8,48,384]{2,1,0:T(8,128)(2,1)S(1)}, u32[]{:S(2)}, u32[]{:S(2)}) %all-to-all-start) | async-done | bytes 294944 | tf_op jit(solution)/shard_map/weight_gather/all_to_all | solution.py:55
  183.7 3.6 %all-to-all-start.1 = ((bf16[8,8,48,384]{3,2,1,0:T(8,128)(2,1)}), bf16[8,8,48,384]{3,2,1,0:T(8,128)(2,1)S(1)}, u32[]{:S(2)}, u32[]{:S(2)}) async-start(bf16[8,8,48,384]{3,2,1,0:T(8,128)(2,1)} %broadcast_in_dim.58), calls=%async_computation.1 | async-start | bytes 4718592 | tf_op jit(solution)/shard_map/weight_gather/all_to_all | solution.py:55
  195.7 3.0 %collective-permute-start.5 = (bf16[8,48,384]{2,1,0:T(8,128)(2,1)S(1)}, bf16[8,48,384]{2,1,0:T(8,128)(2,1)S(1)}, u32[]{:S(2)}, u32[]{:S(2)}) collective-permute-start(bf16[8,48,384]{2,1,0:T(8,128)(2,1)S(1)} %collective-permute-done.3), channel_id=1, source_target_pairs={{0,28},{1,29},{2,30},{3,31},{4,0},{5,1},{6,2},{7,3},{8,4},{9,5},{1... | collective-permute-start | bytes 884744 | tf_op jit(solution)/shard_map/weight_gather/ppermute | solution.py:51
  198.8 6.2 %collective-permute-done.4 = bf16[8,48,384]{2,1,0:T(8,128)(2,1)S(1)} collective-permute-done((bf16[8,48,384]{2,1,0:T(8,128)(2,1)S(1)}, bf16[8,48,384]{2,1,0:T(8,128)(2,1)S(1)}, u32[]{:S(2)}, u32[]{:S(2)}) %collective-permute-start.4) | collective-permute-done | bytes 294944 | tf_op jit(solution)/shard_map/weight_gather/ppermute | solution.py:51
  205.1 2.9 %collective-permute-start.7 = (bf16[4,48,384]{2,1,0:T(8,128)(2,1)S(1)}, bf16[4,48,384]{2,1,0:T(8,128)(2,1)S(1)}, u32[]{:S(2)}, u32[]{:S(2)}) collective-permute-start(bf16[4,48,384]{2,1,0:T(8,128)(2,1)S(1)} %slice.83), channel_id=1, source_target_pairs={{0,28},{1,29},{2,30},{3,31},{4,0},{5,1},{6,2},{7,3},{8,4},{9,5},{1... | collective-permute-start | bytes 442376 | tf_op jit(solution)/shard_map/weight_gather/ppermute | solution.py:51
  208.1 4.0 %collective-permute-done.6 = bf16[4,48,384]{2,1,0:T(8,128)(2,1)S(1)} collective-permute-done((bf16[4,48,384]{2,1,0:T(8,128)(2,1)S(1)}, bf16[4,48,384]{2,1,0:T(8,128)(2,1)S(1)}, u32[]{:S(2)}, u32[]{:S(2)}) %collective-permute-start.6) | collective-permute-done | bytes 147488 | tf_op jit(solution)/shard_map/weight_gather/ppermute | solution.py:51
  213.7 3.5 %all-to-all-done.1 = bf16[8,8,48,384]{3,2,1,0:T(8,128)(2,1)S(1)} async-done(((bf16[8,8,48,384]{3,2,1,0:T(8,128)(2,1)}), bf16[8,8,48,384]{3,2,1,0:T(8,128)(2,1)S(1)}, u32[]{:S(2)}, u32[]{:S(2)}) %all-to-all-start.1) | async-done | bytes 2359328 | tf_op jit(solution)/shard_map/weight_gather/all_to_all | solution.py:55
  219.8 2.5 stream_part.7
  222.2 4.9 %collective-permute-start.9 = (bf16[256,3072]{1,0:T(8,128)(2,1)S(1)}, bf16[256,3072]{1,0:T(8,128)(2,1)S(1)}, u32[]{:S(2)}, u32[]{:S(2)}) collective-permute-start(bf16[256,3072]{1,0:T(8,128)(2,1)S(1)} %stream_part.7), channel_id=1, source_target_pairs={{0,1},{1,0},{2,3},{3,2},{4,5},{5,4},{6,7},{7,6},{8,9},{9,8},{10,11... | collective-permute-start | bytes 4718600 | tf_op jit(solution)/shard_map/stream/ppermute | solution.py:51
  234.4 2.5 stream_part.4
  236.9 33.0 %collective-permute-done.10 = bf16[256,3072]{1,0:T(8,128)(2,1)S(1)} collective-permute-done((bf16[256,3072]{1,0:T(8,128)(2,1)S(1)}, bf16[256,3072]{1,0:T(8,128)(2,1)S(1)}, u32[]{:S(2)}, u32[]{:S(2)}) %collective-permute-start.10) | collective-permute-done | bytes 1572896 | tf_op jit(solution)/shard_map/stream/ppermute | solution.py:51
  269.9 2.6 multiply_convert_fusion
  (93 shorter events, 52.0 us)
Async XLA Ops:
  0.6 37.2 %collective-permute-start.12 = (bf16[256,3072]{1,0:T(8,128)(2,1)}, bf16[256,3072]{1,0:T(8,128)(2,1)S(1)}, u32[]{:S(2)}, u32[]{:S(2)}) collective-permute-start(bf16[256,3072]{1,0:T(8,128)(2,1)} %b0.1), channel_id=1, source_target_pairs={{0,2},{1,3},{2,0},{3,1},{4,6},{5,7},{6,4},{7,5},{8,10},{9,11},{10,... | collective-permute-start | bytes 4718600 | tf_op jit(solution)/shard_map/block_out/ppermute | solution.py:51
  4.5 37.9 %collective-permute-start.11 = (bf16[256,3072]{1,0:T(8,128)(2,1)}, bf16[256,3072]{1,0:T(8,128)(2,1)}, u32[]{:S(2)}, u32[]{:S(2)}) collective-permute-start(bf16[256,3072]{1,0:T(8,128)(2,1)} %b0.1), channel_id=1, source_target_pairs={{0,1},{1,0},{2,3},{3,2},{4,5},{5,4},{6,7},{7,6},{8,9},{9,8},{10,11... | collective-permute-start | bytes 4718600 | tf_op jit(solution)/shard_map/block_out/ppermute | solution.py:51
  37.8 3.8 %copy-start.6 = (bf16[256,3072]{1,0:T(8,128)(2,1)}, bf16[256,3072]{1,0:T(8,128)(2,1)S(1)}, u32[]{:S(2)}) copy-start(bf16[256,3072]{1,0:T(8,128)(2,1)S(1)} %collective-permute-done.12.b2) | copy-start | bytes 4718596
  37.8 5.4 %collective-permute-start.13 = (bf16[256,3072]{1,0:T(8,128)(2,1)S(1)}, bf16[256,3072]{1,0:T(8,128)(2,1)}, u32[]{:S(2)}, u32[]{:S(2)}) collective-permute-start(bf16[256,3072]{1,0:T(8,128)(2,1)S(1)} %collective-permute-done.12.b2), channel_id=1, source_target_pairs={{0,1},{1,0},{2,3},{3,2},{4,5},{5,4},{6,7},{7,6},{8,9},{9,8},{10,11... | collective-permute-start | bytes 4718600 | tf_op jit(solution)/shard_map/block_out/ppermute | solution.py:51
  54.3 12.3 %collective-permute-start.14 = (bf16[4,48,384]{2,1,0:T(8,128)(2,1)}, bf16[4,48,384]{2,1,0:T(8,128)(2,1)}, u32[]{:S(2)}, u32[]{:S(2)}) collective-permute-start(bf16[4,48,384]{2,1,0:T(8,128)(2,1)} %get-tuple-element.15), channel_id=1, source_target_pairs={{0,4},{1,5},{2,6},{3,7},{4,8},{5,9},{6,10},{7,11},{8,12},{9,13},{1... | collective-permute-start | bytes 442376 | tf_op jit(solution)/shard_map/grad_scatter/ppermute | solution.py:51
  56.0 10.7 %collective-permute-start.18 = (bf16[4,48,384]{2,1,0:T(8,128)(2,1)}, bf16[4,48,384]{2,1,0:T(8,128)(2,1)}, u32[]{:S(2)}, u32[]{:S(2)}) collective-permute-start(bf16[4,48,384]{2,1,0:T(8,128)(2,1)} %get-tuple-element.16), channel_id=1, source_target_pairs={{0,28},{1,29},{2,30},{3,31},{4,0},{5,1},{6,2},{7,3},{8,4},{9,5},{1... | collective-permute-start | bytes 442376 | tf_op jit(solution)/shard_map/grad_scatter/ppermute | solution.py:51
  60.7 40.0 %all-to-all-start.3 = ((bf16[8,8,48,384]{3,2,1,0:T(8,128)(2,1)}), bf16[8,8,48,384]{3,2,1,0:T(8,128)(2,1)}, u32[]{:S(2)}, u32[]{:S(2)}) async-start(bf16[8,8,48,384]{3,2,1,0:T(8,128)(2,1)} %bitcast.109), calls=%async_computation.3 | async-start | bytes 4718592 | tf_op jit(solution)/shard_map/grad_scatter/all_to_all | solution.py:168
  68.5 7.9 %collective-permute-start.19 = (bf16[8,48,384]{2,1,0:T(8,128)(2,1)}, bf16[8,48,384]{2,1,0:T(8,128)(2,1)}, u32[]{:S(2)}, u32[]{:S(2)}) collective-permute-start(bf16[8,48,384]{2,1,0:T(8,128)(2,1)} %pad_maximum_fusion.2), channel_id=1, source_target_pairs={{0,28},{1,29},{2,30},{3,31},{4,0},{5,1},{6,2},{7,3},{8,4},{9,5},{1... | collective-permute-start | bytes 884744 | tf_op jit(solution)/shard_map/grad_scatter/ppermute | solution.py:51
  71.6 8.5 %collective-permute-start.15 = (bf16[8,48,384]{2,1,0:T(8,128)(2,1)}, bf16[8,48,384]{2,1,0:T(8,128)(2,1)}, u32[]{:S(2)}, u32[]{:S(2)}) collective-permute-start(bf16[8,48,384]{2,1,0:T(8,128)(2,1)} %pad_maximum_fusion.1), channel_id=1, source_target_pairs={{0,4},{1,5},{2,6},{3,7},{4,8},{5,9},{6,10},{7,11},{8,12},{9,13},{1... | collective-permute-start | bytes 884744 | tf_op jit(solution)/shard_map/grad_scatter/ppermute | solution.py:51
  82.1 7.6 %collective-permute-start.16 = (bf16[8,48,384]{2,1,0:T(8,128)(2,1)}, bf16[8,48,384]{2,1,0:T(8,128)(2,1)}, u32[]{:S(2)}, u32[]{:S(2)}) collective-permute-start(bf16[8,48,384]{2,1,0:T(8,128)(2,1)} %get-tuple-element.11), channel_id=1, source_target_pairs={{0,4},{1,5},{2,6},{3,7},{4,8},{5,9},{6,10},{7,11},{8,12},{9,13},{1... | collective-permute-start | bytes 884744 | tf_op jit(solution)/shard_map/grad_scatter/ppermute | solution.py:51
  82.1 7.6 %collective-permute-start.20 = (bf16[8,48,384]{2,1,0:T(8,128)(2,1)}, bf16[8,48,384]{2,1,0:T(8,128)(2,1)}, u32[]{:S(2)}, u32[]{:S(2)}) collective-permute-start(bf16[8,48,384]{2,1,0:T(8,128)(2,1)} %get-tuple-element.12), channel_id=1, source_target_pairs={{0,28},{1,29},{2,30},{3,31},{4,0},{5,1},{6,2},{7,3},{8,4},{9,5},{1... | collective-permute-start | bytes 884744 | tf_op jit(solution)/shard_map/grad_scatter/ppermute | solution.py:51
  91.7 7.1 %collective-permute-start.17 = (bf16[8,48,384]{2,1,0:T(8,128)(2,1)}, bf16[8,48,384]{2,1,0:T(8,128)(2,1)}, u32[]{:S(2)}, u32[]{:S(2)}) collective-permute-start(bf16[8,48,384]{2,1,0:T(8,128)(2,1)} %get-tuple-element.9), channel_id=1, source_target_pairs={{0,4},{1,5},{2,6},{3,7},{4,8},{5,9},{6,10},{7,11},{8,12},{9,13},{1... | collective-permute-start | bytes 884744 | tf_op jit(solution)/shard_map/grad_scatter/ppermute | solution.py:51
  91.7 7.1 %collective-permute-start.21 = (bf16[8,48,384]{2,1,0:T(8,128)(2,1)}, bf16[8,48,384]{2,1,0:T(8,128)(2,1)}, u32[]{:S(2)}, u32[]{:S(2)}) collective-permute-start(bf16[8,48,384]{2,1,0:T(8,128)(2,1)} %get-tuple-element.10), channel_id=1, source_target_pairs={{0,28},{1,29},{2,30},{3,31},{4,0},{5,1},{6,2},{7,3},{8,4},{9,5},{1... | collective-permute-start | bytes 884744 | tf_op jit(solution)/shard_map/grad_scatter/ppermute | solution.py:51
  100.7 10.7 %all-to-all-start.5 = ((bf16[8,48,384]{2,1,0:T(8,128)(2,1)}), bf16[8,48,384]{2,1,0:T(8,128)(2,1)S(1)}, u32[]{:S(2)}, u32[]{:S(2)}) async-start(bf16[8,48,384]{2,1,0:T(8,128)(2,1)} %fusion.6), calls=%async_computation.5 | async-start | bytes 589824 | tf_op jit(solution)/shard_map/grad_scatter/all_to_all | solution.py:172
  105.1 52.6 %copy-start.8 = (f32[48,768]{1,0:T(8,128)S(1)}, f32[48,768]{1,0:T(8,128)}, u32[]{:S(2)}) copy-start(f32[48,768]{1,0:T(8,128)} %param.9) | copy-start | bytes 442372
  105.1 52.6 %copy-start.9 = (f32[48,768]{1,0:T(8,128)S(1)}, f32[48,768]{1,0:T(8,128)}, u32[]{:S(2)}) copy-start(f32[48,768]{1,0:T(8,128)} %param.11) | copy-start | bytes 442372
  105.1 52.6 %copy-start.10 = (f32[48,768]{1,0:T(8,128)S(1)}, f32[48,768]{1,0:T(8,128)}, u32[]{:S(2)}) copy-start(f32[48,768]{1,0:T(8,128)} %param.10) | copy-start | bytes 442372
  111.4 14.6 %all-to-all-start.4 = ((bf16[8,48,384]{2,1,0:T(8,128)(2,1)}), bf16[8,48,384]{2,1,0:T(8,128)(2,1)S(1)}, u32[]{:S(2)}, u32[]{:S(2)}) async-start(bf16[8,48,384]{2,1,0:T(8,128)(2,1)} %reduce_sum.57), calls=%async_computation.4 | async-start | bytes 589824 | tf_op jit(solution)/shard_map/grad_scatter/all_to_all | solution.py:171
  169.0 13.1 %all-to-all-start = ((bf16[8,48,384]{2,1,0:T(8,128)(2,1)}), bf16[8,48,384]{2,1,0:T(8,128)(2,1)S(1)}, u32[]{:S(2)}, u32[]{:S(2)}) async-start(bf16[8,48,384]{2,1,0:T(8,128)(2,1)} %broadcast_in_dim.57), calls=%async_computation | async-start | bytes 589824 | tf_op jit(solution)/shard_map/weight_gather/all_to_all | solution.py:55
  172.4 16.2 %collective-permute-start = (bf16[8,48,384]{2,1,0:T(8,128)(2,1)}, bf16[8,48,384]{2,1,0:T(8,128)(2,1)}, u32[]{:S(2)}, u32[]{:S(2)}) collective-permute-start(bf16[8,48,384]{2,1,0:T(8,128)(2,1)} %all_to_all.42), channel_id=1, source_target_pairs={{0,4},{1,5},{2,6},{3,7},{4,8},{5,9},{6,10},{7,11},{8,12},{9,13},{1... | collective-permute-start | bytes 884744 | tf_op jit(solution)/shard_map/weight_gather/ppermute | solution.py:51
  173.7 15.2 %collective-permute-start.1 = (bf16[8,48,384]{2,1,0:T(8,128)(2,1)}, bf16[8,48,384]{2,1,0:T(8,128)(2,1)}, u32[]{:S(2)}, u32[]{:S(2)}) collective-permute-start(bf16[8,48,384]{2,1,0:T(8,128)(2,1)} %all_to_all.42), channel_id=1, source_target_pairs={{0,28},{1,29},{2,30},{3,31},{4,0},{5,1},{6,2},{7,3},{8,4},{9,5},{1... | collective-permute-start | bytes 884744 | tf_op jit(solution)/shard_map/weight_gather/ppermute | solution.py:51
  183.7 33.4 %all-to-all-start.1 = ((bf16[8,8,48,384]{3,2,1,0:T(8,128)(2,1)}), bf16[8,8,48,384]{3,2,1,0:T(8,128)(2,1)S(1)}, u32[]{:S(2)}, u32[]{:S(2)}) async-start(bf16[8,8,48,384]{3,2,1,0:T(8,128)(2,1)} %broadcast_in_dim.58), calls=%async_computation.1 | async-start | bytes 4718592 | tf_op jit(solution)/shard_map/weight_gather/all_to_all | solution.py:55
  188.6 7.1 %collective-permute-start.2 = (bf16[8,48,384]{2,1,0:T(8,128)(2,1)}, bf16[8,48,384]{2,1,0:T(8,128)(2,1)S(1)}, u32[]{:S(2)}, u32[]{:S(2)}) collective-permute-start(bf16[8,48,384]{2,1,0:T(8,128)(2,1)} %collective-permute-done), channel_id=1, source_target_pairs={{0,4},{1,5},{2,6},{3,7},{4,8},{5,9},{6,10},{7,11},{8,12},{9,13},{1... | collective-permute-start | bytes 884744 | tf_op jit(solution)/shard_map/weight_gather/ppermute | solution.py:51
  188.9 6.8 %collective-permute-start.3 = (bf16[8,48,384]{2,1,0:T(8,128)(2,1)}, bf16[8,48,384]{2,1,0:T(8,128)(2,1)S(1)}, u32[]{:S(2)}, u32[]{:S(2)}) collective-permute-start(bf16[8,48,384]{2,1,0:T(8,128)(2,1)} %collective-permute-done.1), channel_id=1, source_target_pairs={{0,28},{1,29},{2,30},{3,31},{4,0},{5,1},{6,2},{7,3},{8,4},{9,5},{1... | collective-permute-start | bytes 884744 | tf_op jit(solution)/shard_map/weight_gather/ppermute | solution.py:51
  195.7 9.3 %collective-permute-start.4 = (bf16[8,48,384]{2,1,0:T(8,128)(2,1)S(1)}, bf16[8,48,384]{2,1,0:T(8,128)(2,1)S(1)}, u32[]{:S(2)}, u32[]{:S(2)}) collective-permute-start(bf16[8,48,384]{2,1,0:T(8,128)(2,1)S(1)} %collective-permute-done.2), channel_id=1, source_target_pairs={{0,4},{1,5},{2,6},{3,7},{4,8},{5,9},{6,10},{7,11},{8,12},{9,13},{1... | collective-permute-start | bytes 884744 | tf_op jit(solution)/shard_map/weight_gather/ppermute | solution.py:51
  195.7 9.4 %collective-permute-start.5 = (bf16[8,48,384]{2,1,0:T(8,128)(2,1)S(1)}, bf16[8,48,384]{2,1,0:T(8,128)(2,1)S(1)}, u32[]{:S(2)}, u32[]{:S(2)}) collective-permute-start(bf16[8,48,384]{2,1,0:T(8,128)(2,1)S(1)} %collective-permute-done.3), channel_id=1, source_target_pairs={{0,28},{1,29},{2,30},{3,31},{4,0},{5,1},{6,2},{7,3},{8,4},{9,5},{1... | collective-permute-start | bytes 884744 | tf_op jit(solution)/shard_map/weight_gather/ppermute | solution.py:51
  205.0 7.2 %collective-permute-start.6 = (bf16[4,48,384]{2,1,0:T(8,128)(2,1)S(1)}, bf16[4,48,384]{2,1,0:T(8,128)(2,1)S(1)}, u32[]{:S(2)}, u32[]{:S(2)}) collective-permute-start(bf16[4,48,384]{2,1,0:T(8,128)(2,1)S(1)} %slice.82), channel_id=1, source_target_pairs={{0,4},{1,5},{2,6},{3,7},{4,8},{5,9},{6,10},{7,11},{8,12},{9,13},{1... | collective-permute-start | bytes 442376 | tf_op jit(solution)/shard_map/weight_gather/ppermute | solution.py:51
  205.1 7.1 %collective-permute-start.7 = (bf16[4,48,384]{2,1,0:T(8,128)(2,1)S(1)}, bf16[4,48,384]{2,1,0:T(8,128)(2,1)S(1)}, u32[]{:S(2)}, u32[]{:S(2)}) collective-permute-start(bf16[4,48,384]{2,1,0:T(8,128)(2,1)S(1)} %slice.83), channel_id=1, source_target_pairs={{0,28},{1,29},{2,30},{3,31},{4,0},{5,1},{6,2},{7,3},{8,4},{9,5},{1... | collective-permute-start | bytes 442376 | tf_op jit(solution)/shard_map/weight_gather/ppermute | solution.py:51
  222.2 10.0 %collective-permute-start.9 = (bf16[256,3072]{1,0:T(8,128)(2,1)S(1)}, bf16[256,3072]{1,0:T(8,128)(2,1)S(1)}, u32[]{:S(2)}, u32[]{:S(2)}) collective-permute-start(bf16[256,3072]{1,0:T(8,128)(2,1)S(1)} %stream_part.7), channel_id=1, source_target_pairs={{0,1},{1,0},{2,3},{3,2},{4,5},{5,4},{6,7},{7,6},{8,9},{9,8},{10,11... | collective-permute-start | bytes 4718600 | tf_op jit(solution)/shard_map/stream/ppermute | solution.py:51
  229.6 7.3 %collective-permute-start.8 = (bf16[256,3072]{1,0:T(8,128)(2,1)S(1)}, bf16[256,3072]{1,0:T(8,128)(2,1)S(1)}, u32[]{:S(2)}, u32[]{:S(2)}) collective-permute-start(bf16[256,3072]{1,0:T(8,128)(2,1)S(1)} %stream_part.5), channel_id=1, source_target_pairs={{0,1},{1,0},{2,3},{3,2},{4,5},{5,4},{6,7},{7,6},{8,9},{9,8},{10,11... | collective-permute-start | bytes 4718600 | tf_op jit(solution)/shard_map/stream/ppermute | solution.py:51
  232.8 37.1 %copy-start.11 = (f32[1,3072]{1,0:T(1,128)S(1)}, f32[1,3072]{1,0:T(1,128)}, u32[]{:S(2)}) copy-start(f32[1,3072]{1,0:T(1,128)} %param.7) | copy-start | bytes 36868
  232.8 37.1 %collective-permute-start.10 = (bf16[256,3072]{1,0:T(8,128)(2,1)S(1)}, bf16[256,3072]{1,0:T(8,128)(2,1)S(1)}, u32[]{:S(2)}, u32[]{:S(2)}) collective-permute-start(bf16[256,3072]{1,0:T(8,128)(2,1)S(1)} %add_convert_fusion), channel_id=1, source_target_pairs={{0,2},{1,3},{2,0},{3,1},{4,6},{5,7},{6,4},{7,5},{8,10},{9,11},{10,... | collective-permute-start | bytes 4718600 | tf_op jit(solution)/shard_map/stream/ppermute | solution.py:51
  (7 other events, 9.4 us)

commit v2 on v0

v2 whole, which is shorter than its diff:
```python
import jax
import jax.numpy as jnp
from jax import lax
from jax.experimental import pallas as pl
from jax.experimental.pallas import tpu as pltpu
from jax.sharding import Mesh, PartitionSpec as P

beta_one = 0.9
beta_two = 0.999
bias_one = 1.0 - 0.9**10
bias_two = 1.0 - 0.999**10
epsilon = 1e-08
decay_rate = 0.1
max_norm = 1.0

AXES = ("yl", "x", "z", "yh", "c")
SIZES = (2, 4, 8, 2, 2)
NZ = 8
OWN = 48
WIDTH = 768
D = 3072
TOK = 256
F32 = jnp.float32
BF16 = jnp.bfloat16


def index_of(yl, x, z, yh, c):
    return (((yl * 4 + x) * 8 + z) * 2 + yh) * 2 + c


def pairs(move):
    out = []
    for yl in range(2):
        for x in range(4):
            for z in range(8):
                for yh in range(2):
                    for c in range(2):
                        out.append((index_of(yl, x, z, yh, c), index_of(*move(yl, x, z, yh, c))))
    return out


SWAP_CORE = pairs(lambda yl, x, z, yh, c: (yl, x, z, yh, 1 - c))
SWAP_YH = pairs(lambda yl, x, z, yh, c: (yl, x, z, 1 - yh, c))
SWAP_YL = pairs(lambda yl, x, z, yh, c: (1 - yl, x, z, yh, c))
X_UP = pairs(lambda yl, x, z, yh, c: (yl, (x + 1) % 4, z, yh, c))
X_DOWN = pairs(lambda yl, x, z, yh, c: (yl, (x - 1) % 4, z, yh, c))
X_FAR = pairs(lambda yl, x, z, yh, c: (yl, (x + 2) % 4, z, yh, c))
Z_UP = pairs(lambda yl, x, z, yh, c: (yl, x, (z + 1) % 8, yh, c))
Z_DOWN = pairs(lambda yl, x, z, yh, c: (yl, x, (z - 1) % 8, yh, c))


def send(value, perm):
    return lax.ppermute(value, AXES, perm)


def gather(value, axes, n):
    copies = jnp.broadcast_to(value[None], (n,) + value.shape)
    return lax.all_to_all(copies, axes, 0, 0, tiled=True)


def after(value, *earlier):
    return lax.optimization_barrier((value,) + earlier)[0]


def add(*terms):
    total = terms[0].astype(F32)
    for term in terms[1:]:
        total = total + term.astype(F32)
    return total


VMEM_LIMIT = 28 * 1024 * 1024


def grad_kernel(b0, b1, b2, b3, og, out, blocks):
    for k, block in enumerate((b0, b1, b2, b3)):
        blocks[k * TOK : (k + 1) * TOK, :] = block[...]
    total = lax.dot_general(blocks[...], og[...], (((0,), (0,)), ((), ())), preferred_element_type=F32)
    out[...] = total.astype(BF16)


def weight_grad(blocks, og):
    tile = 768
    return pl.pallas_call(
        grad_kernel,
        grid=(D // tile,),
        in_specs=[pl.BlockSpec((TOK, tile), lambda i: (0, i))] * 4 + [pl.BlockSpec((4 * TOK, WIDTH), lambda i: (0, 0))],
        out_specs=pl.BlockSpec((tile, WIDTH), lambda i: (i, 0)),
        scratch_shapes=[pltpu.VMEM((4 * TOK, tile), BF16)],
        out_shape=jax.ShapeDtypeStruct((D, WIDTH), BF16),
        compiler_params=pltpu.CompilerParams(vmem_limit_bytes=VMEM_LIMIT),
        cost_estimate=pl.CostEstimate(flops=8 * TOK * WIDTH * D, bytes_accessed=16 * 1024 * 1024, transcendentals=0),
        name="weight_grad",
    )(*blocks, og)


def stream_kernel(here, og, *refs):
    blocks, far_low, far_high, (p0, p1, p2, p3, rows) = refs[:7], refs[7], refs[8], refs[9:]
    step = pl.program_id(0)
    yl = lax.rem(step // 2 - here[0] + 2, 2)
    for k in range(2):
        x = lax.rem(lax.rem(step, 2) * 2 + k - here[1] + 4, 4)
        for z, block in zip((0, 1, 2, 3, 5, 6, 7), blocks):
            rows[k, lax.rem(here[2] + z, NZ)] = block[x, yl]
        far = jnp.where(x < 2, far_low[jnp.minimum(x, 1), yl], far_high[jnp.maximum(x - 2, 0), yl])
        rows[k, lax.rem(here[2] + 4, NZ)] = far
    full = rows[...].reshape(2 * NZ * OWN, WIDTH)
    for k, out in enumerate((p0, p1, p2, p3)):
        out[...] = lax.dot_general(
            og[k * TOK : (k + 1) * TOK, :], full, (((1,), (1,)), ((), ())), preferred_element_type=F32
        ).astype(BF16)


def stream_parts(here, og, blocks, far):
    tile = 2 * NZ * OWN
    whole = [pl.BlockSpec((n, 2, OWN, WIDTH), lambda i, here: (0, 0, 0, 0)) for n in (4, 4, 4, 4, 4, 4, 4, 2, 2)]
    return pl.pallas_call(
        stream_kernel,
        grid_spec=pltpu.PrefetchScalarGridSpec(
            num_scalar_prefetch=1,
            grid=(4,),
            in_specs=[pl.BlockSpec((4 * TOK, WIDTH), lambda i, here: (0, 0))] + whole,
            out_specs=[pl.BlockSpec((TOK, tile), lambda i, here: (0, i))] * 4,
            scratch_shapes=[pltpu.VMEM((2, NZ, OWN, WIDTH), BF16)],
        ),
        out_shape=[jax.ShapeDtypeStruct((TOK, D), BF16)] * 4,
        compiler_params=pltpu.CompilerParams(vmem_limit_bytes=VMEM_LIMIT),
        cost_estimate=pl.CostEstimate(flops=8 * TOK * WIDTH * D, bytes_accessed=16 * 1024 * 1024, transcendentals=0),
        name="stream_parts",
    )(here, og, *blocks, *far)


def body(block_out, gate, out_grad, zero_weight, first_moment, second_moment):
    here = jnp.stack([lax.axis_index("yl"), lax.axis_index("x"), lax.axis_index("z")]).astype(jnp.int32)
    ti = lax.axis_index("yh") * 2 + lax.axis_index("c")

    order = [lax.dynamic_slice_in_dim(out_grad, lax.bitwise_xor(ti, k) * TOK, TOK, 0) for k in range(4)]
    out_grad = jnp.concatenate(order)

    with jax.named_scope("start"):
        near = send(block_out, SWAP_CORE)
        weight = zero_weight.astype(BF16)
        other = send(weight, SWAP_YL)
        block_out, other, near = lax.optimization_barrier((block_out, other, near))
        far = send(block_out, SWAP_YH)
        rows = jnp.stack([weight, other])
        x_up, x_down, x_far = send(rows, X_UP), send(rows, X_DOWN), send(rows, X_FAR)
        rows = jnp.stack([rows, x_down, x_far, x_up])

    with jax.named_scope("weight_gather"):
        up, down = send(rows, Z_UP), send(rows, Z_DOWN)
        up, down, far, out_grad = lax.optimization_barrier((up, down, far, out_grad))
        up2, down2 = send(up, Z_UP), send(down, Z_DOWN)

    with jax.named_scope("weight_grad"):
        far_near = send(far, SWAP_CORE)
        grad = weight_grad((block_out, near, far, far_near), out_grad)
        up2, down2 = lax.optimization_barrier((grad, up2, down2))[1:]

    with jax.named_scope("grad_scatter"):
        got = lax.all_to_all(grad.reshape(8, NZ, OWN, WIDTH), ("yl", "x"), 0, 0, tiled=True)

    with jax.named_scope("weight_gather"):
        up3, down3 = send(up2, Z_UP), send(down2, Z_DOWN)
        up3, down3 = lax.optimization_barrier((up3, down3))
        up4, down4 = send(up3[:2], Z_UP), send(down3[2:], Z_DOWN)

    with jax.named_scope("stream"):
        blocks = (rows, down, down2, down3, up3, up2, up)
        p0, p1, p2, p3 = stream_parts(here, out_grad, blocks, (up4, down4))
        r3, r1 = send(p3, SWAP_CORE), send(p1, SWAP_CORE)
        s2 = add(p2, r3).astype(BF16)
        s2, r1 = lax.optimization_barrier((s2, r1))
        q2 = send(s2, SWAP_YH)

    with jax.named_scope("grad_scatter"):
        total = add(*got).astype(BF16)
        owner_grad = add(*lax.all_to_all(total, ("z",), 0, 0, tiled=True))

    with jax.named_scope("norm"):
        local = jnp.sum(owner_grad * owner_grad)
        local = jnp.sum(gather(jnp.full((1, 128), local, F32), ("x", "z"), 32).reshape(32, 128), axis=0, keepdims=True)
        local, q2 = lax.optimization_barrier((local, q2))
        norm_sq = jnp.sum(gather(local, ("yl", "yh", "c"), 8), axis=0)[:1, :1]

    with jax.named_scope("stream"):
        stream = add(p0, r1, q2)
        stream_out = stream.astype(BF16)
        branch_out = (gate * stream).astype(BF16)

    factor = jnp.minimum(1.0, max_norm / (jnp.sqrt(norm_sq) + 1e-06))
    clipped = factor * owner_grad
    first = beta_one * first_moment + (1.0 - beta_one) * clipped
    second = beta_two * second_moment + (1.0 - beta_two) * clipped * clipped
    update = first / bias_one / (jnp.sqrt(second / bias_two) + epsilon) + decay_rate * zero_weight
    return (stream_out, branch_out, update)


def solution(mesh):
    fine = Mesh(mesh.devices.reshape(SIZES), AXES)
    dp, tensor = ("yl", "x", "z"), ("yh", "c")
    placed = (P(AXES, None), P(dp, None), P(dp, tensor), P(dp, tensor), P(dp, tensor), P(dp, tensor))
    return jax.shard_map(
        body,
        mesh=fine,
        in_specs=placed,
        out_specs=(P(AXES, None), P(AXES, None), P(dp, tensor)),
        check_vma=False,
    )
```

time: 876 us -> 192 us (0.22)
  waiting for transfers between devices: 715 us -> 51.5 us
  blocking collectives: 120 us -> 50.2 us
  starting transfers between devices: 0.16 us -> 45.3 us
  matrix products: 19.5 us -> 0 us
  Pallas kernels: 0 us -> 15.2 us
  local copies, waits for them, and re-layouts: 0.02 us -> 14.5 us
  between operations: 14.5 us -> 0.99 us
    reduce_scatter x2 -> x0, waiting for transfers between devices: 397 us -> none  [the longest x1 287 us: body(): lax.psum_scatter(local_grad, 'dp', scatter_dimension=0, tiled=True)]
    all_gather x2 -> x0, waiting for transfers between devices: 317 us -> none  [the longest x1 258 us: body(): lax.all_gather(zero_weight.astype(jnp.bfloat16), 'dp', axis=0, tiled=True)]
    psum x1 -> x0, blocking collectives: 120 us -> none  [body(): norm_sq = lax.psum(jnp.sum(owner_grad * owner_grad), ('dp', 'tensor'))]
    all_to_all x0 -> x2, blocking collectives: none -> 50.2 us  [the longest x1 27.4 us: gather(): return lax.all_to_all(copies, axes, 0, 0, tiled=True)]
    ppermute x0 -> x18, waiting for transfers between devices: none -> 48.8 us  [send(): return lax.ppermute(value, AXES, perm)]
    ppermute x0 -> x18, starting transfers between devices: none -> 32.7 us  [send(): return lax.ppermute(value, AXES, perm)]
    dot_general x2 -> x0, matrix products: 19.5 us -> none  [the longest x1 10.2 us: body(): lax.dot_general(lax.all_gather(block_out, 'tensor', axis=0, tiled=True),...]
    pallas_call x0 -> x2, Pallas kernels: none -> 15.2 us  [the longest x1 8.16 us: stream_parts(): pl.pallas_call(stream_kernel, grid_spec=pltpu.PrefetchScalarGridSpec(num_...]
  transfers between devices with their start and end apart: 4 -> 20, of which waited for: 4 -> 11; matrix products, arithmetic and copies ran while one was open for 0% -> 6% of each run, Pallas kernels for 0% -> 8%
where the time goes in v2:
time: 192 us; the launch traced here: 191 us
  waiting for transfers between devices  51.5 us (27%)
  blocking collectives  50.2 us (26%)
  starting transfers between devices  45.3 us (24%)
  Pallas kernels  15.2 us (8%)
  local copies, waits for them, and re-layouts  14.5 us (8%)
  other arithmetic  13.3 us (7%)
    ppermute x18, waiting for transfers between devices, send(): return lax.ppermute(value, AXES, perm)  48.8 us
    ppermute x18, starting transfers between devices, send(): return lax.ppermute(value, AXES, perm)  32.7 us
    all_to_all x1, blocking collectives, gather(): return lax.all_to_all(copies, axes, 0, 0, tiled=True)  27.4 us
    all_to_all x1, blocking collectives, body(): owner_grad = add(*lax.all_to_all(total, ('z',), 0, 0, tiled=True))  22.8 us
    unnamed x42, local copies, waits for them, and re-layouts  13.1 us
    pallas_call x1, Pallas kernels, stream_parts(): pl.pallas_call(stream_kernel, grid_spec=pltpu.PrefetchScalarGridSpec(num_...  8.16 us
    all_to_all x1, starting transfers between devices, gather(): return lax.all_to_all(copies, axes, 0, 0, tiled=True)  7.58 us
    pallas_call x1, Pallas kernels, weight_grad(): pl.pallas_call(grad_kernel, grid=(D // tile,), in_specs=[pl.BlockSpec((TO...  7.02 us
  transfers between devices with their start and end apart: 20, of which 11 were waited for; matrix products, arithmetic and copies ran while one was open for 6% of the time, Pallas kernels for 8%

profile of v2, /device:TPU:1, one launch (start us, length us, event | category | flops | bytes accessed | tf_op | source)
XLA Modules:
  0.0 191.0 jit_solution(4241124979122483552)
XLA Ops:
  0.6 3.3 %collective-permute-start.1 = (bf16[256,3072]{1,0:T(8,128)(2,1)}, bf16[256,3072]{1,0:T(8,128)(2,1)S(1)}, u32[]{:S(2)}, u32[]{:S(2)}) collective-permute-start(bf16[256,3072]{1,0:T(8,128)(2,1)} %b0), channel_id=1, source_target_pairs={{0,1},{1,0},{2,3},{3,2},{4,5},{5,4},{6,7},{7,6},{8,9},{9,8},{10,11... | collective-permute-start | bytes 4718600 | tf_op jit(solution)/shard_map/start/ppermute | solution.py:53
  5.0 3.7 %collective-permute-done = bf16[48,768]{1,0:T(8,128)(2,1)S(1)} collective-permute-done((bf16[48,768]{1,0:T(8,128)(2,1)S(1)}, bf16[48,768]{1,0:T(8,128)(2,1)S(1)}, u32[]{:S(2)}, u32[]{:S(2)}) %collective-permute-start) | collective-permute-done | bytes 73760 | tf_op jit(solution)/shard_map/start/ppermute | solution.py:53
  9.9 1.2 collective-permute-start.7
  12.0 1.3 collective-permute-start.4
  13.3 2.5 %collective-permute-start.3 = (bf16[2,48,768]{2,1,0:T(8,128)(2,1)S(1)}, bf16[2,48,768]{2,1,0:T(8,128)(2,1)S(1)}, u32[]{:S(2)}, u32[]{:S(2)}) collective-permute-start(bf16[2,48,768]{2,1,0:T(8,128)(2,1)S(1)} %get-tuple-element.50), channel_id=1, source_target_pairs={{0,64},{1,65},{2,66},{3,67},{4,68},{5,69},{6,70},{7,71},{8,72},{9,... | collective-permute-start | bytes 442376 | tf_op jit(solution)/shard_map/start/ppermute | solution.py:53
  15.7 1.2 collective-permute-start.2
  17.7 4.0 %collective-permute-done.3 = bf16[2,48,768]{2,1,0:T(8,128)(2,1)S(1)} collective-permute-done((bf16[2,48,768]{2,1,0:T(8,128)(2,1)S(1)}, bf16[2,48,768]{2,1,0:T(8,128)(2,1)S(1)}, u32[]{:S(2)}, u32[]{:S(2)}) %collective-permute-start.3) | collective-permute-done | bytes 147488 | tf_op jit(solution)/shard_map/start/ppermute | solution.py:53
  21.7 1.7 collective-permute-start.5
  23.5 4.0 %collective-permute-start.6 = (bf16[4,2,48,768]{3,2,1,0:T(8,128)(2,1)S(1)}, bf16[4,2,48,768]{3,2,1,0:T(8,128)(2,1)S(1)}, u32[]{:S(2)}, u32[]{:S(2)}) collective-permute-start(bf16[4,2,48,768]{3,2,1,0:T(8,128)(2,1)S(1)} %pad_maximum_fusion.1.refs_0_), channel_id=1, source_target_pairs={{0,28},{1,29},{2,30},{3,31},{4,0},{5,1},{6,2},{7,3},{8,4},{9,5},{1... | collective-permute-start | bytes 1769480 | tf_op jit(solution)/shard_map/weight_gather/ppermute | solution.py:53
  27.7 11.4 %collective-permute-done.5.refs_6_ = bf16[4,2,48,768]{3,2,1,0:T(8,128)(2,1)S(1)} collective-permute-done((bf16[4,2,48,768]{3,2,1,0:T(8,128)(2,1)S(1)}, bf16[4,2,48,768]{3,2,1,0:T(8,128)(2,1)S(1)}, u32[]{:S(2)}, u32[]{:S(2)}) %collective-permute-start.5) | collective-permute-done | bytes 589856 | tf_op jit(solution)/shard_map/weight_gather/ppermute | solution.py:53
  39.1 7.5 %collective-permute-done.7.b2 = bf16[256,3072]{1,0:T(8,128)(2,1)} collective-permute-done((bf16[256,3072]{1,0:T(8,128)(2,1)}, bf16[256,3072]{1,0:T(8,128)(2,1)}, u32[]{:S(2)}, u32[]{:S(2)}) %collective-permute-start.7) | collective-permute-done | bytes 1572896 | tf_op jit(solution)/shard_map/start/ppermute | solution.py:53
  46.6 1.9 collective-permute-start.8
  48.5 3.8 %collective-permute-start.10 = (bf16[4,2,48,768]{3,2,1,0:T(8,128)(2,1)S(1)}, bf16[4,2,48,768]{3,2,1,0:T(8,128)(2,1)}, u32[]{:S(2)}, u32[]{:S(2)}) collective-permute-start(bf16[4,2,48,768]{3,2,1,0:T(8,128)(2,1)S(1)} %collective-permute-done.6.refs_1_), channel_id=1, source_target_pairs={{0,28},{1,29},{2,30},{3,31},{4,0},{5,1},{6,2},{7,3},{8,4},{9,5},{1... | collective-permute-start | bytes 1769480 | tf_op jit(solution)/shard_map/weight_gather/ppermute | solution.py:53
  52.3 7.0 %weight_grad.1 = bf16[3072,768]{1,0:T(8,128)(2,1)S(1)} custom-call(bf16[256,3072]{1,0:T(8,128)(2,1)S(1)} %copy-done.7, bf16[256,3072]{1,0:T(8,128)(2,1)S(1)} %copy-done.9, bf16[256,3072]{1,0:T(8,128)(2,1)} %collective-permute-done.7.b2, bf16[256,3072]{1,0:T(8,128)(2,1)S(1)} %collective-permute-done.8.b3, bf16[1024,768]{1,0:T(8,128)(2,1)S(1)} %pad_maximum_fusion.og), custom_call_target="tpu_custom_call" | custom-call | flops 4831838208 | bytes 16777216 | tf_op jit(solution)/shard_map/weight_grad/weight_grad/pallas_call | solution.py:84
  59.4 2.2 %copy-done = bf16[3072,768]{1,0:T(8,128)(2,1)} copy-done((bf16[3072,768]{1,0:T(8,128)(2,1)}, bf16[3072,768]{1,0:T(8,128)(2,1)S(1)}, u32[]{:S(2)}) %copy-start) | copy-done | bytes 4718616
  61.6 5.0 %all-to-all-start = ((bf16[8,8,48,768]{3,2,1,0:T(8,128)(2,1)}), bf16[8,8,48,768]{3,2,1,0:T(8,128)(2,1)}, u32[]{:S(2)}, u32[]{:S(2)}) async-start(bf16[8,8,48,768]{3,2,1,0:T(8,128)(2,1)} %bitcast.31), calls=%async_computation | async-start | bytes 9437184 | tf_op jit(solution)/shard_map/grad_scatter/all_to_all | solution.py:161
  67.5 3.2 %collective-permute-start.12 = (bf16[4,2,48,768]{3,2,1,0:T(8,128)(2,1)}, bf16[4,2,48,768]{3,2,1,0:T(8,128)(2,1)S(1)}, u32[]{:S(2)}, u32[]{:S(2)}) collective-permute-start(bf16[4,2,48,768]{3,2,1,0:T(8,128)(2,1)} %collective-permute-done.10.refs_2_), channel_id=1, source_target_pairs={{0,28},{1,29},{2,30},{3,31},{4,0},{5,1},{6,2},{7,3},{8,4},{9,5},{1... | collective-permute-start | bytes 1769480 | tf_op jit(solution)/shard_map/weight_gather/ppermute | solution.py:53
  70.8 12.4 %collective-permute-done.11.refs_4_ = bf16[4,2,48,768]{3,2,1,0:T(8,128)(2,1)S(1)} collective-permute-done((bf16[4,2,48,768]{3,2,1,0:T(8,128)(2,1)S(1)}, bf16[4,2,48,768]{3,2,1,0:T(8,128)(2,1)S(1)}, u32[]{:S(2)}, u32[]{:S(2)}) %collective-permute-start.11) | collective-permute-done | bytes 589856 | tf_op jit(solution)/shard_map/weight_gather/ppermute | solution.py:53
  84.8 3.0 %collective-permute-start.14 = (bf16[2,2,48,768]{3,2,1,0:T(8,128)(2,1)S(1)}, bf16[2,2,48,768]{3,2,1,0:T(8,128)(2,1)S(1)}, u32[]{:S(2)}, u32[]{:S(2)}) collective-permute-start(bf16[2,2,48,768]{3,2,1,0:T(8,128)(2,1)S(1)} %slice.10), channel_id=1, source_target_pairs={{0,28},{1,29},{2,30},{3,31},{4,0},{5,1},{6,2},{7,3},{8,4},{9,5},{1... | collective-permute-start | bytes 884744 | tf_op jit(solution)/shard_map/weight_gather/ppermute | solution.py:53
  87.9 5.6 %collective-permute-done.13.refs_7_ = bf16[2,2,48,768]{3,2,1,0:T(8,128)(2,1)S(1)} collective-permute-done((bf16[2,2,48,768]{3,2,1,0:T(8,128)(2,1)S(1)}, bf16[2,2,48,768]{3,2,1,0:T(8,128)(2,1)S(1)}, u32[]{:S(2)}, u32[]{:S(2)}) %collective-permute-start.13) | collective-permute-done | bytes 294944 | tf_op jit(solution)/shard_map/weight_gather/ppermute | solution.py:53
  101.5 8.2 %stream_parts.1 = (bf16[256,3072]{1,0:T(8,128)(2,1)S(1)}, bf16[256,3072]{1,0:T(8,128)(2,1)S(1)}, bf16[256,3072]{1,0:T(8,128)(2,1)S(1)}, bf16[256,3072]{1,0:T(8,128)(2,1)S(1)}) custom-call(s32[3]{0:T(128)S(1)} %pad_add_fusion.here, bf16[1024,768]{1,0:T(8,128)(2,1)S(1)} %pad_maximum_fusion.og, bf16[4,2,48,768]{3,2,1,0:T(8,128)(2,1)S(1)} %copy-done.2, ...), custom_call_target="tpu_custom_call" | custom-call | flops 4831838208 | bytes 16777216 | tf_op jit(solution)/shard_map/stream/stream_parts/pallas_call | solution.py:117
  109.7 2.0 %collective-permute-start.15 = (bf16[256,3072]{1,0:T(8,128)(2,1)S(1)}, bf16[256,3072]{1,0:T(8,128)(2,1)S(1)}, u32[]{:S(2)}, u32[]{:S(2)}) collective-permute-start(bf16[256,3072]{1,0:T(8,128)(2,1)S(1)} %get-tuple-element.35), channel_id=1, source_target_pairs={{0,1},{1,0},{2,3},{3,2},{4,5},{5,4},{6,7},{7,6},{8,9},{9,8},{10,11... | collective-permute-start | bytes 4718600 | tf_op jit(solution)/shard_map/stream/ppermute | solution.py:53
  111.8 2.9 %collective-permute-done.15 = bf16[256,3072]{1,0:T(8,128)(2,1)S(1)} collective-permute-done((bf16[256,3072]{1,0:T(8,128)(2,1)S(1)}, bf16[256,3072]{1,0:T(8,128)(2,1)S(1)}, u32[]{:S(2)}, u32[]{:S(2)}) %collective-permute-start.15) | collective-permute-done | bytes 1572896 | tf_op jit(solution)/shard_map/stream/ppermute | solution.py:53
  114.8 1.7 add_convert_fusion
  117.0 2.6 %collective-permute-start.17 = (bf16[256,3072]{1,0:T(8,128)(2,1)}, bf16[256,3072]{1,0:T(8,128)(2,1)}, u32[]{:S(2)}, u32[]{:S(2)}) collective-permute-start(bf16[256,3072]{1,0:T(8,128)(2,1)} %add_convert_fusion), channel_id=1, source_target_pairs={{0,2},{1,3},{2,0},{3,1},{4,6},{5,7},{6,4},{7,5},{8,10},{9,11},{10,... | collective-permute-start | bytes 4718600 | tf_op jit(solution)/shard_map/stream/ppermute | solution.py:53
  119.6 2.3 %all-to-all-done = bf16[8,8,48,768]{3,2,1,0:T(8,128)(2,1)} async-done(((bf16[8,8,48,768]{3,2,1,0:T(8,128)(2,1)}), bf16[8,8,48,768]{3,2,1,0:T(8,128)(2,1)}, u32[]{:S(2)}, u32[]{:S(2)}) %all-to-all-start) | async-done | bytes 4718624 | tf_op jit(solution)/shard_map/grad_scatter/all_to_all | solution.py:161
  121.9 2.9 %fusion.1 = bf16[8,48,768]{2,1,0:T(8,128)(2,1)S(1)} fusion(bf16[8,8,48,768]{3,2,1,0:T(8,128)(2,1)} %all-to-all-done), kind=kLoop, calls=%fused_computation.6 | loop fusion | flops 4718592 | bytes 5308416 | tf_op jit(solution)/shard_map/grad_scatter/convert_element_type | solution.py:177
  124.8 22.8 %all_to_all.20 = bf16[8,48,768]{2,1,0:T(8,128)(2,1)S(1)} all-to-all(bf16[8,48,768]{2,1,0:T(8,128)(2,1)S(1)} %fusion.1), channel_id=1, replica_groups=mesh['yl'=2,'x'=4,'z'=8,'yh'=2,'c'=2] {'z'}, dimensions={0} | all-to-all | bytes 1179648 | tf_op jit(solution)/shard_map/grad_scatter/all_to_all | solution.py:178
  148.9 27.4 %all_to_all.21 = f32[32,1,128]{2,1,0:T(1,128)S(1)} all-to-all(f32[32,1,128]{2,1,0:T(1,128)S(1)} %broadcast_in_dim.14), channel_id=1, replica_groups=mesh['yl'=2,'x'=4,'z'=8,'yh'=2,'c'=2] {'x','z'}, dimensions={0} | all-to-all | bytes 32768 | tf_op jit(solution)/shard_map/norm/all_to_all | solution.py:58
  177.0 7.6 %all-to-all-start.3 = ((f32[8,1,128]{2,1,0:T(1,128)}), f32[8,1,128]{2,1,0:T(1,128)S(1)}, u32[]{:S(2)}, u32[]{:S(2)}) async-start(f32[8,1,128]{2,1,0:T(1,128)} %broadcast_in_dim.17), calls=%async_computation.3 | async-start | bytes 8192 | tf_op jit(solution)/shard_map/norm/all_to_all | solution.py:58
  184.6 4.1 %multiply_convert_fusion = (bf16[256,3072]{1,0:T(8,128)(2,1)}, bf16[256,3072]{1,0:T(8,128)(2,1)}) fusion(bf16[256,3072]{1,0:T(8,128)(2,1)} %collective-permute-done.17, bf16[256,3072]{1,0:T(8,128)(2,1)S(1)} %collective-permute-done.16, bf16[256,3072]{1,0:T(8,128)(2,1)S(1)} %get-tuple-element.33, f32[3072]{0:T(1024)S(1)} %bitcast.38), kind=kLoop, calls=%fused_computation | loop fusion | flops 6291456 | bytes 7876608 | tf_op jit(solution)/shard_map/stream/convert_element_type | solution.py:189
  189.2 1.8 fusion.7
  (72 shorter events, 18.0 us)
Async XLA Ops:
  0.6 26.9 %copy-start.18 = (bf16[1024,768]{1,0:T(8,128)(2,1)S(1)}, bf16[1024,768]{1,0:T(8,128)(2,1)}, u32[]{:S(2)}) copy-start(bf16[1024,768]{1,0:T(8,128)(2,1)} %param.8) | copy-start | bytes 4718596
  0.6 8.1 %collective-permute-start.1 = (bf16[256,3072]{1,0:T(8,128)(2,1)}, bf16[256,3072]{1,0:T(8,128)(2,1)S(1)}, u32[]{:S(2)}, u32[]{:S(2)}) collective-permute-start(bf16[256,3072]{1,0:T(8,128)(2,1)} %b0), channel_id=1, source_target_pairs={{0,1},{1,0},{2,3},{3,2},{4,5},{5,4},{6,7},{7,6},{8,9},{9,8},{10,11... | collective-permute-start | bytes 4718600 | tf_op jit(solution)/shard_map/start/ppermute | solution.py:53
  4.9 3.8 %collective-permute-start = (bf16[48,768]{1,0:T(8,128)(2,1)S(1)}, bf16[48,768]{1,0:T(8,128)(2,1)S(1)}, u32[]{:S(2)}, u32[]{:S(2)}) collective-permute-start(bf16[48,768]{1,0:T(8,128)(2,1)S(1)} %convert_element_type.110), channel_id=1, source_target_pairs={{0,128},{1,129},{2,130},{3,131},{4,132},{5,133},{6,134},{7,135},{8... | collective-permute-start | bytes 221192 | tf_op jit(solution)/shard_map/start/ppermute | solution.py:53
  8.7 1.1 copy-start.8
  9.9 36.8 %collective-permute-start.7 = (bf16[256,3072]{1,0:T(8,128)(2,1)}, bf16[256,3072]{1,0:T(8,128)(2,1)}, u32[]{:S(2)}, u32[]{:S(2)}) collective-permute-start(bf16[256,3072]{1,0:T(8,128)(2,1)} %b0), channel_id=1, source_target_pairs={{0,2},{1,3},{2,0},{3,1},{4,6},{5,7},{6,4},{7,5},{8,10},{9,11},{10,... | collective-permute-start | bytes 4718600 | tf_op jit(solution)/shard_map/start/ppermute | solution.py:53
  12.0 5.7 %collective-permute-start.4 = (bf16[2,48,768]{2,1,0:T(8,128)(2,1)S(1)}, bf16[2,48,768]{2,1,0:T(8,128)(2,1)S(1)}, u32[]{:S(2)}, u32[]{:S(2)}) collective-permute-start(bf16[2,48,768]{2,1,0:T(8,128)(2,1)S(1)} %get-tuple-element.50), channel_id=1, source_target_pairs={{0,32},{1,33},{2,34},{3,35},{4,36},{5,37},{6,38},{7,39},{8,40},{9,... | collective-permute-start | bytes 442376 | tf_op jit(solution)/shard_map/start/ppermute | solution.py:53
  13.3 8.4 %collective-permute-start.3 = (bf16[2,48,768]{2,1,0:T(8,128)(2,1)S(1)}, bf16[2,48,768]{2,1,0:T(8,128)(2,1)S(1)}, u32[]{:S(2)}, u32[]{:S(2)}) collective-permute-start(bf16[2,48,768]{2,1,0:T(8,128)(2,1)S(1)} %get-tuple-element.50), channel_id=1, source_target_pairs={{0,64},{1,65},{2,66},{3,67},{4,68},{5,69},{6,70},{7,71},{8,72},{9,... | collective-permute-start | bytes 442376 | tf_op jit(solution)/shard_map/start/ppermute | solution.py:53
  15.7 5.9 %collective-permute-start.2 = (bf16[2,48,768]{2,1,0:T(8,128)(2,1)S(1)}, bf16[2,48,768]{2,1,0:T(8,128)(2,1)S(1)}, u32[]{:S(2)}, u32[]{:S(2)}) collective-permute-start(bf16[2,48,768]{2,1,0:T(8,128)(2,1)S(1)} %get-tuple-element.50), channel_id=1, source_target_pairs={{0,96},{1,97},{2,98},{3,99},{4,100},{5,101},{6,102},{7,103},{8,104... | collective-permute-start | bytes 442376 | tf_op jit(solution)/shard_map/start/ppermute | solution.py:53
  21.7 5.9 %copy-start.1 = (bf16[4,2,48,768]{3,2,1,0:T(8,128)(2,1)}, bf16[4,2,48,768]{3,2,1,0:T(8,128)(2,1)S(1)}, u32[]{:S(2)}) copy-start(bf16[4,2,48,768]{3,2,1,0:T(8,128)(2,1)S(1)} %pad_maximum_fusion.1.refs_0_) | copy-start | bytes 1769476
  21.7 17.4 %collective-permute-start.5 = (bf16[4,2,48,768]{3,2,1,0:T(8,128)(2,1)S(1)}, bf16[4,2,48,768]{3,2,1,0:T(8,128)(2,1)S(1)}, u32[]{:S(2)}, u32[]{:S(2)}) collective-permute-start(bf16[4,2,48,768]{3,2,1,0:T(8,128)(2,1)S(1)} %pad_maximum_fusion.1.refs_0_), channel_id=1, source_target_pairs={{0,4},{1,5},{2,6},{3,7},{4,8},{5,9},{6,10},{7,11},{8,12},{9,13},{1... | collective-permute-start | bytes 1769480 | tf_op jit(solution)/shard_map/weight_gather/ppermute | solution.py:53
  23.5 15.6 %collective-permute-start.6 = (bf16[4,2,48,768]{3,2,1,0:T(8,128)(2,1)S(1)}, bf16[4,2,48,768]{3,2,1,0:T(8,128)(2,1)S(1)}, u32[]{:S(2)}, u32[]{:S(2)}) collective-permute-start(bf16[4,2,48,768]{3,2,1,0:T(8,128)(2,1)S(1)} %pad_maximum_fusion.1.refs_0_), channel_id=1, source_target_pairs={{0,28},{1,29},{2,30},{3,31},{4,0},{5,1},{6,2},{7,3},{8,4},{9,5},{1... | collective-permute-start | bytes 1769480 | tf_op jit(solution)/shard_map/weight_gather/ppermute | solution.py:53
  27.6 24.7 %copy-start.7 = (bf16[256,3072]{1,0:T(8,128)(2,1)S(1)}, bf16[256,3072]{1,0:T(8,128)(2,1)}, u32[]{:S(2)}) copy-start(bf16[256,3072]{1,0:T(8,128)(2,1)} %b0) | copy-start | bytes 4718596
  27.6 24.7 %copy-start.9 = (bf16[256,3072]{1,0:T(8,128)(2,1)S(1)}, bf16[256,3072]{1,0:T(8,128)(2,1)}, u32[]{:S(2)}) copy-start(bf16[256,3072]{1,0:T(8,128)(2,1)} %copy-done.8) | copy-start | bytes 4718596
  39.1 20.3 %copy-start.10 = (bf16[4,2,48,768]{3,2,1,0:T(8,128)(2,1)}, bf16[4,2,48,768]{3,2,1,0:T(8,128)(2,1)S(1)}, u32[]{:S(2)}) copy-start(bf16[4,2,48,768]{3,2,1,0:T(8,128)(2,1)S(1)} %collective-permute-done.5.refs_6_) | copy-start | bytes 1769476
  39.1 20.3 %copy-start.12 = (bf16[4,2,48,768]{3,2,1,0:T(8,128)(2,1)}, bf16[4,2,48,768]{3,2,1,0:T(8,128)(2,1)S(1)}, u32[]{:S(2)}) copy-start(bf16[4,2,48,768]{3,2,1,0:T(8,128)(2,1)S(1)} %collective-permute-done.6.refs_1_) | copy-start | bytes 1769476
  46.6 5.7 %collective-permute-start.8 = (bf16[256,3072]{1,0:T(8,128)(2,1)}, bf16[256,3072]{1,0:T(8,128)(2,1)S(1)}, u32[]{:S(2)}, u32[]{:S(2)}) collective-permute-start(bf16[256,3072]{1,0:T(8,128)(2,1)} %collective-permute-done.7.b2), channel_id=1, source_target_pairs={{0,1},{1,0},{2,3},{3,2},{4,5},{5,4},{6,7},{7,6},{8,9},{9,8},{10,11... | collective-permute-start | bytes 4718600 | tf_op jit(solution)/shard_map/weight_grad/ppermute | solution.py:53
  48.5 18.1 %collective-permute-start.9 = (bf16[4,2,48,768]{3,2,1,0:T(8,128)(2,1)S(1)}, bf16[4,2,48,768]{3,2,1,0:T(8,128)(2,1)S(1)}, u32[]{:S(2)}, u32[]{:S(2)}) collective-permute-start(bf16[4,2,48,768]{3,2,1,0:T(8,128)(2,1)S(1)} %collective-permute-done.5.refs_6_), channel_id=1, source_target_pairs={{0,4},{1,5},{2,6},{3,7},{4,8},{5,9},{6,10},{7,11},{8,12},{9,13},{1... | collective-permute-start | bytes 1769480 | tf_op jit(solution)/shard_map/weight_gather/ppermute | solution.py:53
  48.5 18.1 %collective-permute-start.10 = (bf16[4,2,48,768]{3,2,1,0:T(8,128)(2,1)S(1)}, bf16[4,2,48,768]{3,2,1,0:T(8,128)(2,1)}, u32[]{:S(2)}, u32[]{:S(2)}) collective-permute-start(bf16[4,2,48,768]{3,2,1,0:T(8,128)(2,1)S(1)} %collective-permute-done.6.refs_1_), channel_id=1, source_target_pairs={{0,28},{1,29},{2,30},{3,31},{4,0},{5,1},{6,2},{7,3},{8,4},{9,5},{1... | collective-permute-start | bytes 1769480 | tf_op jit(solution)/shard_map/weight_gather/ppermute | solution.py:53
  59.4 2.2 %copy-start = (bf16[3072,768]{1,0:T(8,128)(2,1)}, bf16[3072,768]{1,0:T(8,128)(2,1)S(1)}, u32[]{:S(2)}) copy-start(bf16[3072,768]{1,0:T(8,128)(2,1)S(1)} %weight_grad.1) | copy-start | bytes 14155780
  61.6 60.3 %all-to-all-start = ((bf16[8,8,48,768]{3,2,1,0:T(8,128)(2,1)}), bf16[8,8,48,768]{3,2,1,0:T(8,128)(2,1)}, u32[]{:S(2)}, u32[]{:S(2)}) async-start(bf16[8,8,48,768]{3,2,1,0:T(8,128)(2,1)} %bitcast.31), calls=%async_computation | async-start | bytes 9437184 | tf_op jit(solution)/shard_map/grad_scatter/all_to_all | solution.py:161
  66.6 16.5 %collective-permute-start.11 = (bf16[4,2,48,768]{3,2,1,0:T(8,128)(2,1)S(1)}, bf16[4,2,48,768]{3,2,1,0:T(8,128)(2,1)S(1)}, u32[]{:S(2)}, u32[]{:S(2)}) collective-permute-start(bf16[4,2,48,768]{3,2,1,0:T(8,128)(2,1)S(1)} %collective-permute-done.9.refs_5_), channel_id=1, source_target_pairs={{0,4},{1,5},{2,6},{3,7},{4,8},{5,9},{6,10},{7,11},{8,12},{9,13},{1... | collective-permute-start | bytes 1769480 | tf_op jit(solution)/shard_map/weight_gather/ppermute | solution.py:53
  67.5 15.6 %collective-permute-start.12 = (bf16[4,2,48,768]{3,2,1,0:T(8,128)(2,1)}, bf16[4,2,48,768]{3,2,1,0:T(8,128)(2,1)S(1)}, u32[]{:S(2)}, u32[]{:S(2)}) collective-permute-start(bf16[4,2,48,768]{3,2,1,0:T(8,128)(2,1)} %collective-permute-done.10.refs_2_), channel_id=1, source_target_pairs={{0,28},{1,29},{2,30},{3,31},{4,0},{5,1},{6,2},{7,3},{8,4},{9,5},{1... | collective-permute-start | bytes 1769480 | tf_op jit(solution)/shard_map/weight_gather/ppermute | solution.py:53
  83.1 1.7 copy-start.5
  84.0 9.4 %collective-permute-start.13 = (bf16[2,2,48,768]{3,2,1,0:T(8,128)(2,1)S(1)}, bf16[2,2,48,768]{3,2,1,0:T(8,128)(2,1)S(1)}, u32[]{:S(2)}, u32[]{:S(2)}) collective-permute-start(bf16[2,2,48,768]{3,2,1,0:T(8,128)(2,1)S(1)} %slice.9), channel_id=1, source_target_pairs={{0,4},{1,5},{2,6},{3,7},{4,8},{5,9},{6,10},{7,11},{8,12},{9,13},{1... | collective-permute-start | bytes 884744 | tf_op jit(solution)/shard_map/weight_gather/ppermute | solution.py:53
  84.8 8.6 %collective-permute-start.14 = (bf16[2,2,48,768]{3,2,1,0:T(8,128)(2,1)S(1)}, bf16[2,2,48,768]{3,2,1,0:T(8,128)(2,1)S(1)}, u32[]{:S(2)}, u32[]{:S(2)}) collective-permute-start(bf16[2,2,48,768]{3,2,1,0:T(8,128)(2,1)S(1)} %slice.10), channel_id=1, source_target_pairs={{0,28},{1,29},{2,30},{3,31},{4,0},{5,1},{6,2},{7,3},{8,4},{9,5},{1... | collective-permute-start | bytes 884744 | tf_op jit(solution)/shard_map/weight_gather/ppermute | solution.py:53
  96.3 1.1 copy-start.6
  109.7 5.1 %collective-permute-start.15 = (bf16[256,3072]{1,0:T(8,128)(2,1)S(1)}, bf16[256,3072]{1,0:T(8,128)(2,1)S(1)}, u32[]{:S(2)}, u32[]{:S(2)}) collective-permute-start(bf16[256,3072]{1,0:T(8,128)(2,1)S(1)} %get-tuple-element.35), channel_id=1, source_target_pairs={{0,1},{1,0},{2,3},{3,2},{4,5},{5,4},{6,7},{7,6},{8,9},{9,8},{10,11... | collective-permute-start | bytes 4718600 | tf_op jit(solution)/shard_map/stream/ppermute | solution.py:53
  111.7 5.3 %collective-permute-start.16 = (bf16[256,3072]{1,0:T(8,128)(2,1)S(1)}, bf16[256,3072]{1,0:T(8,128)(2,1)S(1)}, u32[]{:S(2)}, u32[]{:S(2)}) collective-permute-start(bf16[256,3072]{1,0:T(8,128)(2,1)S(1)} %get-tuple-element.36), channel_id=1, source_target_pairs={{0,1},{1,0},{2,3},{3,2},{4,5},{5,4},{6,7},{7,6},{8,9},{9,8},{10,11... | collective-permute-start | bytes 4718600 | tf_op jit(solution)/shard_map/stream/ppermute | solution.py:53
  117.0 59.4 %collective-permute-start.17 = (bf16[256,3072]{1,0:T(8,128)(2,1)}, bf16[256,3072]{1,0:T(8,128)(2,1)}, u32[]{:S(2)}, u32[]{:S(2)}) collective-permute-start(bf16[256,3072]{1,0:T(8,128)(2,1)} %add_convert_fusion), channel_id=1, source_target_pairs={{0,2},{1,3},{2,0},{3,1},{4,6},{5,7},{6,4},{7,5},{8,10},{9,11},{10,... | collective-permute-start | bytes 4718600 | tf_op jit(solution)/shard_map/stream/ppermute | solution.py:53
  124.8 59.7 %copy-start.20 = (f32[1,3072]{1,0:T(1,128)S(1)}, f32[1,3072]{1,0:T(1,128)}, u32[]{:S(2)}) copy-start(f32[1,3072]{1,0:T(1,128)} %param.7) | copy-start | bytes 36868
  177.0 12.1 %all-to-all-start.3 = ((f32[8,1,128]{2,1,0:T(1,128)}), f32[8,1,128]{2,1,0:T(1,128)S(1)}, u32[]{:S(2)}, u32[]{:S(2)}) async-start(f32[8,1,128]{2,1,0:T(1,128)} %broadcast_in_dim.17), calls=%async_computation.3 | async-start | bytes 8192 | tf_op jit(solution)/shard_map/norm/all_to_all | solution.py:58
  184.5 4.6 %copy-start.19 = (f32[48,768]{1,0:T(8,128)S(1)}, f32[48,768]{1,0:T(8,128)}, u32[]{:S(2)}) copy-start(f32[48,768]{1,0:T(8,128)} %param.9) | copy-start | bytes 442372
  (9 other events, 8.7 us)

commit v3 on v2

--- a/solution.py
+++ b/solution.py
@@ -70,6 +70,7 @@
 
 
 VMEM_LIMIT = 28 * 1024 * 1024
+ALL_VMEM = 60 * 1024 * 1024
 
 
 def grad_kernel(b0, b1, b2, b3, og, out, blocks):
@@ -95,15 +96,20 @@
 
 
 def stream_kernel(here, og, *refs):
-    blocks, far_low, far_high, (p0, p1, p2, p3, rows) = refs[:7], refs[7], refs[8], refs[9:]
+    lanes, (p0, p1, p2, p3, rows) = (refs[:9], refs[9:18]), refs[18:]
     step = pl.program_id(0)
     yl = lax.rem(step // 2 - here[0] + 2, 2)
-    for k in range(2):
-        x = lax.rem(lax.rem(step, 2) * 2 + k - here[1] + 4, 4)
-        for z, block in zip((0, 1, 2, 3, 5, 6, 7), blocks):
-            rows[k, lax.rem(here[2] + z, NZ)] = block[x, yl]
-        far = jnp.where(x < 2, far_low[jnp.minimum(x, 1), yl], far_high[jnp.maximum(x - 2, 0), yl])
-        rows[k, lax.rem(here[2] + 4, NZ)] = far
+    for lane, blocks in enumerate(lanes):
+
+        @pl.when(yl == lane)
+        def _():
+            for k in range(2):
+                x = lax.rem(lax.rem(step, 2) * 2 + k - here[1] + 4, 4)
+                for z, block in zip((0, 1, 2, 3, 5, 6, 7), blocks):
+                    rows[k, lax.rem(here[2] + z, NZ)] = block[x]
+                far = jnp.where(x < 2, blocks[7][jnp.minimum(x, 1)], blocks[8][jnp.maximum(x - 2, 0)])
+                rows[k, lax.rem(here[2] + 4, NZ)] = far
+
     full = rows[...].reshape(2 * NZ * OWN, WIDTH)
     for k, out in enumerate((p0, p1, p2, p3)):
         out[...] = lax.dot_general(
@@ -111,9 +117,9 @@
         ).astype(BF16)
 
 
-def stream_parts(here, og, blocks, far):
+def stream_parts(here, og, blocks):
     tile = 2 * NZ * OWN
-    whole = [pl.BlockSpec((n, 2, OWN, WIDTH), lambda i, here: (0, 0, 0, 0)) for n in (4, 4, 4, 4, 4, 4, 4, 2, 2)]
+    whole = [pl.BlockSpec((n, OWN, WIDTH), lambda i, here: (0, 0, 0)) for n in (4, 4, 4, 4, 4, 4, 4, 2, 2) * 2]
     return pl.pallas_call(
         stream_kernel,
         grid_spec=pltpu.PrefetchScalarGridSpec(
@@ -124,10 +130,10 @@
             scratch_shapes=[pltpu.VMEM((2, NZ, OWN, WIDTH), BF16)],
         ),
         out_shape=[jax.ShapeDtypeStruct((TOK, D), BF16)] * 4,
-        compiler_params=pltpu.CompilerParams(vmem_limit_bytes=VMEM_LIMIT),
+        compiler_params=pltpu.CompilerParams(vmem_limit_bytes=ALL_VMEM),
         cost_estimate=pl.CostEstimate(flops=8 * TOK * WIDTH * D, bytes_accessed=16 * 1024 * 1024, transcendentals=0),
         name="stream_parts",
-    )(here, og, *blocks, *far)
+    )(here, og, *blocks)
 
 
 def body(block_out, gate, out_grad, zero_weight, first_moment, second_moment):
@@ -138,36 +144,45 @@
     out_grad = jnp.concatenate(order)
 
     with jax.named_scope("start"):
+        far = send(block_out, SWAP_YH)
+        weight = zero_weight.astype(BF16)
+        lane_0 = jnp.stack([weight, send(weight, X_DOWN), send(weight, X_FAR), send(weight, X_UP)])
         near = send(block_out, SWAP_CORE)
-        weight = zero_weight.astype(BF16)
-        other = send(weight, SWAP_YL)
-        block_out, other, near = lax.optimization_barrier((block_out, other, near))
-        far = send(block_out, SWAP_YH)
-        rows = jnp.stack([weight, other])
-        x_up, x_down, x_far = send(rows, X_UP), send(rows, X_DOWN), send(rows, X_FAR)
-        rows = jnp.stack([rows, x_down, x_far, x_up])
+        lane_0, near = lax.optimization_barrier((lane_0, near))
+        lane_1 = send(lane_0, SWAP_YL)
+
+    def ring(up, down):
+        return send(up, Z_UP), send(down, Z_DOWN)
 
     with jax.named_scope("weight_gather"):
-        up, down = send(rows, Z_UP), send(rows, Z_DOWN)
-        up, down, far, out_grad = lax.optimization_barrier((up, down, far, out_grad))
-        up2, down2 = send(up, Z_UP), send(down, Z_DOWN)
+        first_0 = ring(lane_0, lane_0)
+        second_0 = ring(*first_0)
+        third_0 = ring(*second_0)
+        far, out_grad, third_0 = lax.optimization_barrier((far, out_grad, third_0))
+        fourth_0 = ring(third_0[0][:2], third_0[1][2:])
+        first_1 = ring(lane_1, lane_1)
 
     with jax.named_scope("weight_grad"):
         far_near = send(far, SWAP_CORE)
         grad = weight_grad((block_out, near, far, far_near), out_grad)
-        up2, down2 = lax.optimization_barrier((grad, up2, down2))[1:]
 
     with jax.named_scope("grad_scatter"):
         got = lax.all_to_all(grad.reshape(8, NZ, OWN, WIDTH), ("yl", "x"), 0, 0, tiled=True)
 
     with jax.named_scope("weight_gather"):
-        up3, down3 = send(up2, Z_UP), send(down2, Z_DOWN)
-        up3, down3 = lax.optimization_barrier((up3, down3))
-        up4, down4 = send(up3[:2], Z_UP), send(down3[2:], Z_DOWN)
+        first_1, fourth_0 = lax.optimization_barrier((first_1, fourth_0, grad))[:2]
+        second_1 = ring(*first_1)
+        third_1 = ring(*second_1)
+        fourth_1 = ring(third_1[0][:2], third_1[1][2:])
 
     with jax.named_scope("stream"):
-        blocks = (rows, down, down2, down3, up3, up2, up)
-        p0, p1, p2, p3 = stream_parts(here, out_grad, blocks, (up4, down4))
+        blocks = []
+        for lane, (up, down), (up2, down2), (up3, down3), fourth in (
+            (lane_0, first_0, second_0, third_0, fourth_0),
+            (lane_1, first_1, second_1, third_1, fourth_1),
+        ):
+            blocks += [lane, down, down2, down3, up3, up2, up, *fourth]
+        p0, p1, p2, p3 = stream_parts(here, out_grad, blocks)
         r3, r1 = send(p3, SWAP_CORE), send(p1, SWAP_CORE)
         s2 = add(p2, r3).astype(BF16)
         s2, r1 = lax.optimization_barrier((s2, r1))
@@ -179,14 +194,13 @@
 
     with jax.named_scope("norm"):
         local = jnp.sum(owner_grad * owner_grad)
-        local = jnp.sum(gather(jnp.full((1, 128), local, F32), ("x", "z"), 32).reshape(32, 128), axis=0, keepdims=True)
-        local, q2 = lax.optimization_barrier((local, q2))
-        norm_sq = jnp.sum(gather(local, ("yl", "yh", "c"), 8), axis=0)[:1, :1]
-
-    with jax.named_scope("stream"):
+        local = gather(jnp.full((1, 128), local, F32), ("x", "z"), 32)
         stream = add(p0, r1, q2)
         stream_out = stream.astype(BF16)
         branch_out = (gate * stream).astype(BF16)
+        local, stream_out, branch_out = lax.optimization_barrier((local, stream_out, branch_out))
+        local = jnp.sum(local.reshape(32, 128), axis=0, keepdims=True)
+        norm_sq = jnp.sum(gather(local, ("yl", "yh", "c"), 8), axis=0)[:1, :1]
 
     factor = jnp.minimum(1.0, max_norm / (jnp.sqrt(norm_sq) + 1e-06))
     clipped = factor * owner_grad

time: 192 us -> 186 us (0.969)
  starting transfers between devices: 45.3 us -> 63.6 us
  blocking collectives: 50.2 us -> 33.1 us
  local copies, waits for them, and re-layouts: 14.5 us -> 6.13 us
  waiting for transfers between devices: 51.5 us -> 48.2 us
  Pallas kernels: 15.2 us -> 17.9 us
    all_to_all x1, blocking collectives: 27.4 us -> 10.9 us  [gather(): return lax.all_to_all(copies, axes, 0, 0, tiled=True)]
    ppermute x18 -> x26, starting transfers between devices: 32.7 us -> 43.5 us  [send(): return lax.ppermute(value, AXES, perm)]
    unnamed x42 -> x46, local copies, waits for them, and re-layouts: 13.1 us -> 3.46 us
    all_to_all x1, starting transfers between devices: 7.58 us -> 15.5 us  [gather(): return lax.all_to_all(copies, axes, 0, 0, tiled=True)]
    ppermute x18 -> x26, waiting for transfers between devices: 48.8 us -> 43.8 us  [send(): return lax.ppermute(value, AXES, perm)]
    all_to_all x1, waiting for transfers between devices: 0.42 us -> 4.46 us  [gather(): return lax.all_to_all(copies, axes, 0, 0, tiled=True)]
    pallas_call x1, Pallas kernels: 8.16 us -> 10.9 us  [stream_parts(): pl.pallas_call(stream_kernel, grid_spec=pltpu.PrefetchScalarGridSpec(num_...]
    all_to_all x1, waiting for transfers between devices: 2.27 us -> 0.01 us  [body(): lax.all_to_all(grad.reshape(8, NZ, OWN, WIDTH), ('yl', 'x'), 0, 0, tiled=...]
  transfers between devices with their start and end apart: 20 -> 28, of which waited for: 11 -> 12; matrix products, arithmetic and copies ran while one was open for 6% -> 9% of each run, Pallas kernels for 8% -> 10%
where the time goes in v3:
time: 186 us; the launch traced here: 185 us
  starting transfers between devices  63.6 us (34%)
  waiting for transfers between devices  48.2 us (26%)
  blocking collectives  33.1 us (18%)
  Pallas kernels  17.9 us (10%)
  other arithmetic  15.1 us (8%)
  local copies, waits for them, and re-layouts  6.13 us (3%)
    ppermute x26, waiting for transfers between devices, send(): return lax.ppermute(value, AXES, perm)  43.8 us
    ppermute x26, starting transfers between devices, send(): return lax.ppermute(value, AXES, perm)  43.5 us
    all_to_all x1, blocking collectives, body(): owner_grad = add(*lax.all_to_all(total, ('z',), 0, 0, tiled=True))  22.2 us
    all_to_all x1, starting transfers between devices, gather(): return lax.all_to_all(copies, axes, 0, 0, tiled=True)  15.5 us
    all_to_all x1, blocking collectives, gather(): return lax.all_to_all(copies, axes, 0, 0, tiled=True)  10.9 us
    pallas_call x1, Pallas kernels, stream_parts(): pl.pallas_call(stream_kernel, grid_spec=pltpu.PrefetchScalarGridSpec(num_...  10.9 us
    pallas_call x1, Pallas kernels, weight_grad(): pl.pallas_call(grad_kernel, grid=(D // tile,), in_specs=[pl.BlockSpec((TO...  7.01 us
    all_to_all x1, starting transfers between devices, body(): lax.all_to_all(grad.reshape(8, NZ, OWN, WIDTH), ('yl', 'x'), 0, 0, tiled=...  4.6 us
  transfers between devices with their start and end apart: 28, of which 12 were waited for; matrix products, arithmetic and copies ran while one was open for 9% of the time, Pallas kernels for 10%

profile of v3, /device:TPU:1, one launch (start us, length us, event | category | flops | bytes accessed | tf_op | source)
XLA Modules:
  0.0 185.1 jit_solution(5617096615824619090)
XLA Ops:
  0.6 3.3 %collective-permute-start.3 = (bf16[256,3072]{1,0:T(8,128)(2,1)}, bf16[256,3072]{1,0:T(8,128)(2,1)S(1)}, u32[]{:S(2)}, u32[]{:S(2)}) collective-permute-start(bf16[256,3072]{1,0:T(8,128)(2,1)} %b0.1), channel_id=1, source_target_pairs={{0,1},{1,0},{2,3},{3,2},{4,5},{5,4},{6,7},{7,6},{8,9},{9,8},{10,11... | collective-permute-start | bytes 4718600 | tf_op jit(solution)/shard_map/start/ppermute | solution.py:53
  7.4 2.5 %collective-permute-start.1 = (bf16[48,768]{1,0:T(8,128)(2,1)S(1)}, bf16[48,768]{1,0:T(8,128)(2,1)S(1)}, u32[]{:S(2)}, u32[]{:S(2)}) collective-permute-start(bf16[48,768]{1,0:T(8,128)(2,1)S(1)} %convert_element_type.110), channel_id=1, source_target_pairs={{0,64},{1,65},{2,66},{3,67},{4,68},{5,69},{6,70},{7,71},{8,72},{9,... | collective-permute-start | bytes 221192 | tf_op jit(solution)/shard_map/start/ppermute | solution.py:53
  15.3 4.0 %collective-permute-start.8 = (bf16[4,48,768]{2,1,0:T(8,128)(2,1)S(1)}, bf16[4,48,768]{2,1,0:T(8,128)(2,1)S(1)}, u32[]{:S(2)}, u32[]{:S(2)}) collective-permute-start(bf16[4,48,768]{2,1,0:T(8,128)(2,1)S(1)} %pad_maximum_fusion.1.refs_0_), channel_id=1, source_target_pairs={{0,28},{1,29},{2,30},{3,31},{4,0},{5,1},{6,2},{7,3},{8,4},{9,5},{1... | collective-permute-start | bytes 884744 | tf_op jit(solution)/shard_map/weight_gather/ppermute | solution.py:53
  19.3 5.8 %collective-permute-done.5.refs_6_ = bf16[4,48,768]{2,1,0:T(8,128)(2,1)S(1)} collective-permute-done((bf16[4,48,768]{2,1,0:T(8,128)(2,1)S(1)}, bf16[4,48,768]{2,1,0:T(8,128)(2,1)S(1)}, u32[]{:S(2)}, u32[]{:S(2)}) %collective-permute-start.5) | collective-permute-done | bytes 294944 | tf_op jit(solution)/shard_map/weight_gather/ppermute | solution.py:53
  25.1 2.7 %collective-permute-start.9 = (bf16[4,48,768]{2,1,0:T(8,128)(2,1)S(1)}, bf16[4,48,768]{2,1,0:T(8,128)(2,1)}, u32[]{:S(2)}, u32[]{:S(2)}) collective-permute-start(bf16[4,48,768]{2,1,0:T(8,128)(2,1)S(1)} %collective-permute-done.8.refs_1_), channel_id=1, source_target_pairs={{0,28},{1,29},{2,30},{3,31},{4,0},{5,1},{6,2},{7,3},{8,4},{9,5},{1... | collective-permute-start | bytes 884744 | tf_op jit(solution)/shard_map/weight_gather/ppermute | solution.py:53
  27.8 5.0 %collective-permute-done.6.refs_5_ = bf16[4,48,768]{2,1,0:T(8,128)(2,1)S(1)} collective-permute-done((bf16[4,48,768]{2,1,0:T(8,128)(2,1)S(1)}, bf16[4,48,768]{2,1,0:T(8,128)(2,1)S(1)}, u32[]{:S(2)}, u32[]{:S(2)}) %collective-permute-start.6) | collective-permute-done | bytes 294944 | tf_op jit(solution)/shard_map/weight_gather/ppermute | solution.py:53
  32.9 2.7 %collective-permute-start.10 = (bf16[4,48,768]{2,1,0:T(8,128)(2,1)}, bf16[4,48,768]{2,1,0:T(8,128)(2,1)S(1)}, u32[]{:S(2)}, u32[]{:S(2)}) collective-permute-start(bf16[4,48,768]{2,1,0:T(8,128)(2,1)} %collective-permute-done.9.refs_2_), channel_id=1, source_target_pairs={{0,28},{1,29},{2,30},{3,31},{4,0},{5,1},{6,2},{7,3},{8,4},{9,5},{1... | collective-permute-start | bytes 884744 | tf_op jit(solution)/shard_map/weight_gather/ppermute | solution.py:53
  37.1 4.6 %collective-permute-done.4.b2 = bf16[256,3072]{1,0:T(8,128)(2,1)} collective-permute-done((bf16[256,3072]{1,0:T(8,128)(2,1)}, bf16[256,3072]{1,0:T(8,128)(2,1)}, u32[]{:S(2)}, u32[]{:S(2)}) %collective-permute-start.4) | collective-permute-done | bytes 1572896 | tf_op jit(solution)/shard_map/start/ppermute | solution.py:53
  43.9 3.1 %collective-permute-done.11.b3 = bf16[256,3072]{1,0:T(8,128)(2,1)S(1)} collective-permute-done((bf16[256,3072]{1,0:T(8,128)(2,1)}, bf16[256,3072]{1,0:T(8,128)(2,1)S(1)}, u32[]{:S(2)}, u32[]{:S(2)}) %collective-permute-start.11) | collective-permute-done | bytes 1572896 | tf_op jit(solution)/shard_map/weight_grad/ppermute | solution.py:53
  47.0 7.0 %weight_grad.1 = bf16[3072,768]{1,0:T(8,128)(2,1)S(1)} custom-call(bf16[256,3072]{1,0:T(8,128)(2,1)S(1)} %copy-done.2, bf16[256,3072]{1,0:T(8,128)(2,1)S(1)} %collective-permute-done.3.b1, bf16[256,3072]{1,0:T(8,128)(2,1)} %collective-permute-done.4.b2, bf16[256,3072]{1,0:T(8,128)(2,1)S(1)} %collective-permute-done.11.b3, ...), custom_call_target="tpu_custom_call" | custom-call | flops 4831838208 | bytes 16777216 | tf_op jit(solution)/shard_map/weight_grad/weight_grad/pallas_call | solution.py:85
  54.1 2.2 %copy-done = bf16[3072,768]{1,0:T(8,128)(2,1)} copy-done((bf16[3072,768]{1,0:T(8,128)(2,1)}, bf16[3072,768]{1,0:T(8,128)(2,1)S(1)}, u32[]{:S(2)}) %copy-start) | copy-done | bytes 4718616
  56.2 4.6 %all-to-all-start = ((bf16[8,8,48,768]{3,2,1,0:T(8,128)(2,1)}), bf16[8,8,48,768]{3,2,1,0:T(8,128)(2,1)}, u32[]{:S(2)}, u32[]{:S(2)}) async-start(bf16[8,8,48,768]{3,2,1,0:T(8,128)(2,1)} %bitcast.25), calls=%async_computation | async-start | bytes 9437184 | tf_op jit(solution)/shard_map/grad_scatter/all_to_all | solution.py:170
  60.9 3.5 %collective-permute-start.14 = (bf16[4,48,768]{2,1,0:T(8,128)(2,1)S(1)}, bf16[4,48,768]{2,1,0:T(8,128)(2,1)S(1)}, u32[]{:S(2)}, u32[]{:S(2)}) collective-permute-start(bf16[4,48,768]{2,1,0:T(8,128)(2,1)S(1)} %collective-permute-done.12.refs_9_), channel_id=1, source_target_pairs={{0,28},{1,29},{2,30},{3,31},{4,0},{5,1},{6,2},{7,3},{8,4},{9,5},{1... | collective-permute-start | bytes 884744 | tf_op jit(solution)/shard_map/weight_gather/ppermute | solution.py:53
  64.5 2.7 %collective-permute-start.16 = (bf16[2,48,768]{2,1,0:T(8,128)(2,1)S(1)}, bf16[2,48,768]{2,1,0:T(8,128)(2,1)S(1)}, u32[]{:S(2)}, u32[]{:S(2)}) collective-permute-start(bf16[2,48,768]{2,1,0:T(8,128)(2,1)S(1)} %slice.16), channel_id=1, source_target_pairs={{0,28},{1,29},{2,30},{3,31},{4,0},{5,1},{6,2},{7,3},{8,4},{9,5},{1... | collective-permute-start | bytes 442376 | tf_op jit(solution)/shard_map/weight_gather/ppermute | solution.py:53
  67.3 3.7 %collective-permute-done.13.refs_15_ = bf16[4,48,768]{2,1,0:T(8,128)(2,1)S(1)} collective-permute-done((bf16[4,48,768]{2,1,0:T(8,128)(2,1)S(1)}, bf16[4,48,768]{2,1,0:T(8,128)(2,1)S(1)}, u32[]{:S(2)}, u32[]{:S(2)}) %collective-permute-start.13) | collective-permute-done | bytes 294944 | tf_op jit(solution)/shard_map/weight_gather/ppermute | solution.py:53
  71.0 3.2 %collective-permute-done.15.refs_7_ = bf16[2,48,768]{2,1,0:T(8,128)(2,1)S(1)} collective-permute-done((bf16[2,48,768]{2,1,0:T(8,128)(2,1)S(1)}, bf16[2,48,768]{2,1,0:T(8,128)(2,1)S(1)}, u32[]{:S(2)}, u32[]{:S(2)}) %collective-permute-start.15) | collective-permute-done | bytes 147488 | tf_op jit(solution)/shard_map/weight_gather/ppermute | solution.py:53
  76.9 6.0 %collective-permute-done.19.refs_14_ = bf16[4,48,768]{2,1,0:T(8,128)(2,1)S(1)} collective-permute-done((bf16[4,48,768]{2,1,0:T(8,128)(2,1)S(1)}, bf16[4,48,768]{2,1,0:T(8,128)(2,1)S(1)}, u32[]{:S(2)}, u32[]{:S(2)}) %collective-permute-start.19) | collective-permute-done | bytes 294944 | tf_op jit(solution)/shard_map/weight_gather/ppermute | solution.py:53
  83.5 2.2 %collective-permute-start.18 = (bf16[4,48,768]{2,1,0:T(8,128)(2,1)S(1)}, bf16[4,48,768]{2,1,0:T(8,128)(2,1)S(1)}, u32[]{:S(2)}, u32[]{:S(2)}) collective-permute-start(bf16[4,48,768]{2,1,0:T(8,128)(2,1)S(1)} %collective-permute-done.17.refs_11_), channel_id=1, source_target_pairs={{0,28},{1,29},{2,30},{3,31},{4,0},{5,1},{6,2},{7,3},{8,4},{9,5},{1... | collective-permute-start | bytes 884744 | tf_op jit(solution)/shard_map/weight_gather/ppermute | solution.py:53
  85.6 5.2 %collective-permute-done.20.refs_13_ = bf16[4,48,768]{2,1,0:T(8,128)(2,1)S(1)} collective-permute-done((bf16[4,48,768]{2,1,0:T(8,128)(2,1)S(1)}, bf16[4,48,768]{2,1,0:T(8,128)(2,1)S(1)}, u32[]{:S(2)}, u32[]{:S(2)}) %collective-permute-start.20) | collective-permute-done | bytes 294944 | tf_op jit(solution)/shard_map/weight_gather/ppermute | solution.py:53
  91.0 2.7 %collective-permute-start.22 = (bf16[2,48,768]{2,1,0:T(8,128)(2,1)S(1)}, bf16[2,48,768]{2,1,0:T(8,128)(2,1)S(1)}, u32[]{:S(2)}, u32[]{:S(2)}) collective-permute-start(bf16[2,48,768]{2,1,0:T(8,128)(2,1)S(1)} %slice.21), channel_id=1, source_target_pairs={{0,28},{1,29},{2,30},{3,31},{4,0},{5,1},{6,2},{7,3},{8,4},{9,5},{1... | collective-permute-start | bytes 442376 | tf_op jit(solution)/shard_map/weight_gather/ppermute | solution.py:53
  94.3 2.3 %collective-permute-done.21.refs_16_ = bf16[2,48,768]{2,1,0:T(8,128)(2,1)S(1)} collective-permute-done((bf16[2,48,768]{2,1,0:T(8,128)(2,1)S(1)}, bf16[2,48,768]{2,1,0:T(8,128)(2,1)S(1)}, u32[]{:S(2)}, u32[]{:S(2)}) %collective-permute-start.21) | collective-permute-done | bytes 147488 | tf_op jit(solution)/shard_map/weight_gather/ppermute | solution.py:53
  97.9 10.9 %stream_parts.1 = (bf16[256,3072]{1,0:T(8,128)(2,1)}, bf16[256,3072]{1,0:T(8,128)(2,1)}, bf16[256,3072]{1,0:T(8,128)(2,1)}, bf16[256,3072]{1,0:T(8,128)(2,1)}) custom-call(s32[3]{0:T(128)} %pad_add_fusion.here, bf16[1024,768]{1,0:T(8,128)(2,1)} %copy-done.1, bf16[4,48,768]{2,1,0:T(8,128)(2,1)} %copy-done.5, bf16[4,48,768]{2,1,0:T(8,128)(2,1)} %copy-done.12, ...), custom_call_target="tpu_custom_call" | custom-call | flops 4831838208 | bytes 16777216 | tf_op jit(solution)/shard_map/stream/stream_parts/pallas_call | solution.py:123
  108.7 3.6 %collective-permute-start.23 = (bf16[256,3072]{1,0:T(8,128)(2,1)}, bf16[256,3072]{1,0:T(8,128)(2,1)S(1)}, u32[]{:S(2)}, u32[]{:S(2)}) collective-permute-start(bf16[256,3072]{1,0:T(8,128)(2,1)} %get-tuple-element.34), channel_id=1, source_target_pairs={{0,1},{1,0},{2,3},{3,2},{4,5},{5,4},{6,7},{7,6},{8,9},{9,8},{10,11... | collective-permute-start | bytes 4718600 | tf_op jit(solution)/shard_map/stream/ppermute | solution.py:53
  112.4 3.1 %collective-permute-done.23 = bf16[256,3072]{1,0:T(8,128)(2,1)S(1)} collective-permute-done((bf16[256,3072]{1,0:T(8,128)(2,1)}, bf16[256,3072]{1,0:T(8,128)(2,1)S(1)}, u32[]{:S(2)}, u32[]{:S(2)}) %collective-permute-start.23) | collective-permute-done | bytes 1572896 | tf_op jit(solution)/shard_map/stream/ppermute | solution.py:53
  115.5 3.1 %add_convert_fusion = bf16[256,3072]{1,0:T(8,128)(2,1)} fusion(bf16[256,3072]{1,0:T(8,128)(2,1)S(1)} %collective-permute-done.23, bf16[256,3072]{1,0:T(8,128)(2,1)} %get-tuple-element.33), kind=kLoop, calls=%fused_computation.2 | loop fusion | flops 3145728 | bytes 4718592 | tf_op jit(solution)/shard_map/stream/convert_element_type | solution.py:187
  118.7 2.6 %collective-permute-start.25 = (bf16[256,3072]{1,0:T(8,128)(2,1)}, bf16[256,3072]{1,0:T(8,128)(2,1)}, u32[]{:S(2)}, u32[]{:S(2)}) collective-permute-start(bf16[256,3072]{1,0:T(8,128)(2,1)} %add_convert_fusion), channel_id=1, source_target_pairs={{0,2},{1,3},{2,0},{3,1},{4,6},{5,7},{6,4},{7,5},{8,10},{9,11},{10,... | collective-permute-start | bytes 4718600 | tf_op jit(solution)/shard_map/stream/ppermute | solution.py:53
  121.3 2.9 %fusion.1 = bf16[8,48,768]{2,1,0:T(8,128)(2,1)S(1)} fusion(bf16[8,8,48,768]{3,2,1,0:T(8,128)(2,1)} %all-to-all-done), kind=kLoop, calls=%fused_computation.6 | loop fusion | flops 4718592 | bytes 5308416 | tf_op jit(solution)/shard_map/grad_scatter/convert_element_type | solution.py:192
  124.2 22.2 %all_to_all.20 = bf16[8,48,768]{2,1,0:T(8,128)(2,1)S(1)} all-to-all(bf16[8,48,768]{2,1,0:T(8,128)(2,1)S(1)} %fusion.1), channel_id=1, replica_groups=mesh['yl'=2,'x'=4,'z'=8,'yh'=2,'c'=2] {'z'}, dimensions={0} | all-to-all | bytes 1179648 | tf_op jit(solution)/shard_map/grad_scatter/all_to_all | solution.py:193
  148.2 15.5 %all-to-all-start.2 = ((f32[32,1,128]{2,1,0:T(1,128)}), f32[32,1,128]{2,1,0:T(1,128)S(1)}, u32[]{:S(2)}, u32[]{:S(2)}) async-start(f32[32,1,128]{2,1,0:T(1,128)} %broadcast_in_dim.4), calls=%async_computation.2 | async-start | bytes 32768 | tf_op jit(solution)/shard_map/norm/all_to_all | solution.py:58
  163.8 4.1 %multiply_convert_fusion = (bf16[256,3072]{1,0:T(8,128)(2,1)}, bf16[256,3072]{1,0:T(8,128)(2,1)}) fusion(bf16[256,3072]{1,0:T(8,128)(2,1)} %collective-permute-done.25, bf16[256,3072]{1,0:T(8,128)(2,1)S(1)} %collective-permute-done.24, bf16[256,3072]{1,0:T(8,128)(2,1)S(1)} %copy-done.3, f32[3072]{0:T(1024)S(1)} %bitcast.30), kind=kLoop, calls=%fused_computation | loop fusion | flops 6291456 | bytes 7876608 | tf_op jit(solution)/shard_map/norm/convert_element_type | solution.py:200
  167.8 4.5 %all-to-all-done.2 = f32[32,1,128]{2,1,0:T(1,128)S(1)} async-done(((f32[32,1,128]{2,1,0:T(1,128)}), f32[32,1,128]{2,1,0:T(1,128)S(1)}, u32[]{:S(2)}, u32[]{:S(2)}) %all-to-all-start.2) | async-done | bytes 16416 | tf_op jit(solution)/shard_map/norm/all_to_all | solution.py:58
  172.3 10.9 %all_to_all.21 = f32[8,1,128]{2,1,0:T(1,128)S(1)} all-to-all(f32[8,1,128]{2,1,0:T(1,128)S(1)} %broadcast_in_dim.10), channel_id=1, replica_groups=mesh['yl'=2,'x'=4,'z'=8,'yh'=2,'c'=2] {'yl','yh','c'}, dimensions={0} | all-to-all | bytes 8192 | tf_op jit(solution)/shard_map/norm/all_to_all | solution.py:58
  (93 shorter events, 21.8 us)
Async XLA Ops:
  0.6 13.0 %collective-permute-start.3 = (bf16[256,3072]{1,0:T(8,128)(2,1)}, bf16[256,3072]{1,0:T(8,128)(2,1)S(1)}, u32[]{:S(2)}, u32[]{:S(2)}) collective-permute-start(bf16[256,3072]{1,0:T(8,128)(2,1)} %b0.1), channel_id=1, source_target_pairs={{0,1},{1,0},{2,3},{3,2},{4,5},{5,4},{6,7},{7,6},{8,9},{9,8},{10,11... | collective-permute-start | bytes 4718600 | tf_op jit(solution)/shard_map/start/ppermute | solution.py:53
  4.0 37.8 %collective-permute-start.4 = (bf16[256,3072]{1,0:T(8,128)(2,1)}, bf16[256,3072]{1,0:T(8,128)(2,1)}, u32[]{:S(2)}, u32[]{:S(2)}) collective-permute-start(bf16[256,3072]{1,0:T(8,128)(2,1)} %b0.1), channel_id=1, source_target_pairs={{0,2},{1,3},{2,0},{3,1},{4,6},{5,7},{6,4},{7,5},{8,10},{9,11},{10,... | collective-permute-start | bytes 4718600 | tf_op jit(solution)/shard_map/start/ppermute | solution.py:53
  6.1 5.8 %collective-permute-start.2 = (bf16[48,768]{1,0:T(8,128)(2,1)S(1)}, bf16[48,768]{1,0:T(8,128)(2,1)S(1)}, u32[]{:S(2)}, u32[]{:S(2)}) collective-permute-start(bf16[48,768]{1,0:T(8,128)(2,1)S(1)} %convert_element_type.110), channel_id=1, source_target_pairs={{0,32},{1,33},{2,34},{3,35},{4,36},{5,37},{6,38},{7,39},{8,40},{9,... | collective-permute-start | bytes 221192 | tf_op jit(solution)/shard_map/start/ppermute | solution.py:53
  7.4 6.2 %collective-permute-start.1 = (bf16[48,768]{1,0:T(8,128)(2,1)S(1)}, bf16[48,768]{1,0:T(8,128)(2,1)S(1)}, u32[]{:S(2)}, u32[]{:S(2)}) collective-permute-start(bf16[48,768]{1,0:T(8,128)(2,1)S(1)} %convert_element_type.110), channel_id=1, source_target_pairs={{0,64},{1,65},{2,66},{3,67},{4,68},{5,69},{6,70},{7,71},{8,72},{9,... | collective-permute-start | bytes 221192 | tf_op jit(solution)/shard_map/start/ppermute | solution.py:53
  9.8 3.7 %collective-permute-start = (bf16[48,768]{1,0:T(8,128)(2,1)S(1)}, bf16[48,768]{1,0:T(8,128)(2,1)S(1)}, u32[]{:S(2)}, u32[]{:S(2)}) collective-permute-start(bf16[48,768]{1,0:T(8,128)(2,1)S(1)} %convert_element_type.110), channel_id=1, source_target_pairs={{0,96},{1,97},{2,98},{3,99},{4,100},{5,101},{6,102},{7,103},{8,104... | collective-permute-start | bytes 221192 | tf_op jit(solution)/shard_map/start/ppermute | solution.py:53
  13.6 30.2 %copy-start.5 = (bf16[4,48,768]{2,1,0:T(8,128)(2,1)}, bf16[4,48,768]{2,1,0:T(8,128)(2,1)S(1)}, u32[]{:S(2)}) copy-start(bf16[4,48,768]{2,1,0:T(8,128)(2,1)S(1)} %pad_maximum_fusion.1.refs_0_) | copy-start | bytes 884740
  13.6 11.5 %collective-permute-start.5 = (bf16[4,48,768]{2,1,0:T(8,128)(2,1)S(1)}, bf16[4,48,768]{2,1,0:T(8,128)(2,1)S(1)}, u32[]{:S(2)}, u32[]{:S(2)}) collective-permute-start(bf16[4,48,768]{2,1,0:T(8,128)(2,1)S(1)} %pad_maximum_fusion.1.refs_0_), channel_id=1, source_target_pairs={{0,4},{1,5},{2,6},{3,7},{4,8},{5,9},{6,10},{7,11},{8,12},{9,13},{1... | collective-permute-start | bytes 884744 | tf_op jit(solution)/shard_map/weight_gather/ppermute | solution.py:53
  15.3 9.8 %collective-permute-start.8 = (bf16[4,48,768]{2,1,0:T(8,128)(2,1)S(1)}, bf16[4,48,768]{2,1,0:T(8,128)(2,1)S(1)}, u32[]{:S(2)}, u32[]{:S(2)}) collective-permute-start(bf16[4,48,768]{2,1,0:T(8,128)(2,1)S(1)} %pad_maximum_fusion.1.refs_0_), channel_id=1, source_target_pairs={{0,28},{1,29},{2,30},{3,31},{4,0},{5,1},{6,2},{7,3},{8,4},{9,5},{1... | collective-permute-start | bytes 884744 | tf_op jit(solution)/shard_map/weight_gather/ppermute | solution.py:53
  25.1 7.7 %collective-permute-start.6 = (bf16[4,48,768]{2,1,0:T(8,128)(2,1)S(1)}, bf16[4,48,768]{2,1,0:T(8,128)(2,1)S(1)}, u32[]{:S(2)}, u32[]{:S(2)}) collective-permute-start(bf16[4,48,768]{2,1,0:T(8,128)(2,1)S(1)} %collective-permute-done.5.refs_6_), channel_id=1, source_target_pairs={{0,4},{1,5},{2,6},{3,7},{4,8},{5,9},{6,10},{7,11},{8,12},{9,13},{1... | collective-permute-start | bytes 884744 | tf_op jit(solution)/shard_map/weight_gather/ppermute | solution.py:53
  25.1 7.7 %collective-permute-start.9 = (bf16[4,48,768]{2,1,0:T(8,128)(2,1)S(1)}, bf16[4,48,768]{2,1,0:T(8,128)(2,1)}, u32[]{:S(2)}, u32[]{:S(2)}) collective-permute-start(bf16[4,48,768]{2,1,0:T(8,128)(2,1)S(1)} %collective-permute-done.8.refs_1_), channel_id=1, source_target_pairs={{0,28},{1,29},{2,30},{3,31},{4,0},{5,1},{6,2},{7,3},{8,4},{9,5},{1... | collective-permute-start | bytes 884744 | tf_op jit(solution)/shard_map/weight_gather/ppermute | solution.py:53
  32.8 8.9 %collective-permute-start.7 = (bf16[4,48,768]{2,1,0:T(8,128)(2,1)S(1)}, bf16[4,48,768]{2,1,0:T(8,128)(2,1)S(1)}, u32[]{:S(2)}, u32[]{:S(2)}) collective-permute-start(bf16[4,48,768]{2,1,0:T(8,128)(2,1)S(1)} %collective-permute-done.6.refs_5_), channel_id=1, source_target_pairs={{0,4},{1,5},{2,6},{3,7},{4,8},{5,9},{6,10},{7,11},{8,12},{9,13},{1... | collective-permute-start | bytes 884744 | tf_op jit(solution)/shard_map/weight_gather/ppermute | solution.py:53
  32.9 8.9 %collective-permute-start.10 = (bf16[4,48,768]{2,1,0:T(8,128)(2,1)}, bf16[4,48,768]{2,1,0:T(8,128)(2,1)S(1)}, u32[]{:S(2)}, u32[]{:S(2)}) collective-permute-start(bf16[4,48,768]{2,1,0:T(8,128)(2,1)} %collective-permute-done.9.refs_2_), channel_id=1, source_target_pairs={{0,28},{1,29},{2,30},{3,31},{4,0},{5,1},{6,2},{7,3},{8,4},{9,5},{1... | collective-permute-start | bytes 884744 | tf_op jit(solution)/shard_map/weight_gather/ppermute | solution.py:53
  41.8 5.3 %collective-permute-start.11 = (bf16[256,3072]{1,0:T(8,128)(2,1)}, bf16[256,3072]{1,0:T(8,128)(2,1)S(1)}, u32[]{:S(2)}, u32[]{:S(2)}) collective-permute-start(bf16[256,3072]{1,0:T(8,128)(2,1)} %collective-permute-done.4.b2), channel_id=1, source_target_pairs={{0,1},{1,0},{2,3},{3,2},{4,5},{5,4},{6,7},{7,6},{8,9},{9,8},{10,11... | collective-permute-start | bytes 4718600 | tf_op jit(solution)/shard_map/weight_grad/ppermute | solution.py:53
  43.8 17.0 %collective-permute-start.12 = (bf16[4,48,768]{2,1,0:T(8,128)(2,1)S(1)}, bf16[4,48,768]{2,1,0:T(8,128)(2,1)S(1)}, u32[]{:S(2)}, u32[]{:S(2)}) collective-permute-start(bf16[4,48,768]{2,1,0:T(8,128)(2,1)S(1)} %pad_maximum_fusion.1.refs_0_), channel_id=1, source_target_pairs={{0,128},{1,129},{2,130},{3,131},{4,132},{5,133},{6,134},{7,135},{8... | collective-permute-start | bytes 884744 | tf_op jit(solution)/shard_map/start/ppermute | solution.py:53
  56.2 65.1 %all-to-all-start = ((bf16[8,8,48,768]{3,2,1,0:T(8,128)(2,1)}), bf16[8,8,48,768]{3,2,1,0:T(8,128)(2,1)}, u32[]{:S(2)}, u32[]{:S(2)}) async-start(bf16[8,8,48,768]{3,2,1,0:T(8,128)(2,1)} %bitcast.25), calls=%async_computation | async-start | bytes 9437184 | tf_op jit(solution)/shard_map/grad_scatter/all_to_all | solution.py:170
  60.8 35.7 %copy-start.14 = (bf16[4,48,768]{2,1,0:T(8,128)(2,1)}, bf16[4,48,768]{2,1,0:T(8,128)(2,1)S(1)}, u32[]{:S(2)}) copy-start(bf16[4,48,768]{2,1,0:T(8,128)(2,1)S(1)} %collective-permute-done.12.refs_9_) | copy-start | bytes 884740
  60.9 10.1 %collective-permute-start.13 = (bf16[4,48,768]{2,1,0:T(8,128)(2,1)S(1)}, bf16[4,48,768]{2,1,0:T(8,128)(2,1)S(1)}, u32[]{:S(2)}, u32[]{:S(2)}) collective-permute-start(bf16[4,48,768]{2,1,0:T(8,128)(2,1)S(1)} %collective-permute-done.12.refs_9_), channel_id=1, source_target_pairs={{0,4},{1,5},{2,6},{3,7},{4,8},{5,9},{6,10},{7,11},{8,12},{9,13},{1... | collective-permute-start | bytes 884744 | tf_op jit(solution)/shard_map/weight_gather/ppermute | solution.py:53
  60.9 10.1 %collective-permute-start.14 = (bf16[4,48,768]{2,1,0:T(8,128)(2,1)S(1)}, bf16[4,48,768]{2,1,0:T(8,128)(2,1)S(1)}, u32[]{:S(2)}, u32[]{:S(2)}) collective-permute-start(bf16[4,48,768]{2,1,0:T(8,128)(2,1)S(1)} %collective-permute-done.12.refs_9_), channel_id=1, source_target_pairs={{0,28},{1,29},{2,30},{3,31},{4,0},{5,1},{6,2},{7,3},{8,4},{9,5},{1... | collective-permute-start | bytes 884744 | tf_op jit(solution)/shard_map/weight_gather/ppermute | solution.py:53
  64.4 9.7 %collective-permute-start.15 = (bf16[2,48,768]{2,1,0:T(8,128)(2,1)S(1)}, bf16[2,48,768]{2,1,0:T(8,128)(2,1)S(1)}, u32[]{:S(2)}, u32[]{:S(2)}) collective-permute-start(bf16[2,48,768]{2,1,0:T(8,128)(2,1)S(1)} %slice.15), channel_id=1, source_target_pairs={{0,4},{1,5},{2,6},{3,7},{4,8},{5,9},{6,10},{7,11},{8,12},{9,13},{1... | collective-permute-start | bytes 442376 | tf_op jit(solution)/shard_map/weight_gather/ppermute | solution.py:53
  64.5 9.6 %collective-permute-start.16 = (bf16[2,48,768]{2,1,0:T(8,128)(2,1)S(1)}, bf16[2,48,768]{2,1,0:T(8,128)(2,1)S(1)}, u32[]{:S(2)}, u32[]{:S(2)}) collective-permute-start(bf16[2,48,768]{2,1,0:T(8,128)(2,1)S(1)} %slice.16), channel_id=1, source_target_pairs={{0,28},{1,29},{2,30},{3,31},{4,0},{5,1},{6,2},{7,3},{8,4},{9,5},{1... | collective-permute-start | bytes 442376 | tf_op jit(solution)/shard_map/weight_gather/ppermute | solution.py:53
  74.2 8.8 %collective-permute-start.19 = (bf16[4,48,768]{2,1,0:T(8,128)(2,1)S(1)}, bf16[4,48,768]{2,1,0:T(8,128)(2,1)S(1)}, u32[]{:S(2)}, u32[]{:S(2)}) collective-permute-start(bf16[4,48,768]{2,1,0:T(8,128)(2,1)S(1)} %collective-permute-done.13.refs_15_), channel_id=1, source_target_pairs={{0,4},{1,5},{2,6},{3,7},{4,8},{5,9},{6,10},{7,11},{8,12},{9,13},{1... | collective-permute-start | bytes 884744 | tf_op jit(solution)/shard_map/weight_gather/ppermute | solution.py:53
  75.9 7.5 %collective-permute-start.17 = (bf16[4,48,768]{2,1,0:T(8,128)(2,1)S(1)}, bf16[4,48,768]{2,1,0:T(8,128)(2,1)S(1)}, u32[]{:S(2)}, u32[]{:S(2)}) collective-permute-start(bf16[4,48,768]{2,1,0:T(8,128)(2,1)S(1)} %collective-permute-done.14.refs_10_), channel_id=1, source_target_pairs={{0,28},{1,29},{2,30},{3,31},{4,0},{5,1},{6,2},{7,3},{8,4},{9,5},{1... | collective-permute-start | bytes 884744 | tf_op jit(solution)/shard_map/weight_gather/ppermute | solution.py:53
  83.0 7.9 %collective-permute-start.20 = (bf16[4,48,768]{2,1,0:T(8,128)(2,1)S(1)}, bf16[4,48,768]{2,1,0:T(8,128)(2,1)S(1)}, u32[]{:S(2)}, u32[]{:S(2)}) collective-permute-start(bf16[4,48,768]{2,1,0:T(8,128)(2,1)S(1)} %collective-permute-done.19.refs_14_), channel_id=1, source_target_pairs={{0,4},{1,5},{2,6},{3,7},{4,8},{5,9},{6,10},{7,11},{8,12},{9,13},{1... | collective-permute-start | bytes 884744 | tf_op jit(solution)/shard_map/weight_gather/ppermute | solution.py:53
  83.5 7.5 %collective-permute-start.18 = (bf16[4,48,768]{2,1,0:T(8,128)(2,1)S(1)}, bf16[4,48,768]{2,1,0:T(8,128)(2,1)S(1)}, u32[]{:S(2)}, u32[]{:S(2)}) collective-permute-start(bf16[4,48,768]{2,1,0:T(8,128)(2,1)S(1)} %collective-permute-done.17.refs_11_), channel_id=1, source_target_pairs={{0,28},{1,29},{2,30},{3,31},{4,0},{5,1},{6,2},{7,3},{8,4},{9,5},{1... | collective-permute-start | bytes 884744 | tf_op jit(solution)/shard_map/weight_gather/ppermute | solution.py:53
  90.9 5.7 %collective-permute-start.21 = (bf16[2,48,768]{2,1,0:T(8,128)(2,1)S(1)}, bf16[2,48,768]{2,1,0:T(8,128)(2,1)S(1)}, u32[]{:S(2)}, u32[]{:S(2)}) collective-permute-start(bf16[2,48,768]{2,1,0:T(8,128)(2,1)S(1)} %slice.20), channel_id=1, source_target_pairs={{0,4},{1,5},{2,6},{3,7},{4,8},{5,9},{6,10},{7,11},{8,12},{9,13},{1... | collective-permute-start | bytes 442376 | tf_op jit(solution)/shard_map/weight_gather/ppermute | solution.py:53
  91.0 5.6 %collective-permute-start.22 = (bf16[2,48,768]{2,1,0:T(8,128)(2,1)S(1)}, bf16[2,48,768]{2,1,0:T(8,128)(2,1)S(1)}, u32[]{:S(2)}, u32[]{:S(2)}) collective-permute-start(bf16[2,48,768]{2,1,0:T(8,128)(2,1)S(1)} %slice.21), channel_id=1, source_target_pairs={{0,28},{1,29},{2,30},{3,31},{4,0},{5,1},{6,2},{7,3},{8,4},{9,5},{1... | collective-permute-start | bytes 442376 | tf_op jit(solution)/shard_map/weight_gather/ppermute | solution.py:53
  108.7 6.8 %collective-permute-start.23 = (bf16[256,3072]{1,0:T(8,128)(2,1)}, bf16[256,3072]{1,0:T(8,128)(2,1)S(1)}, u32[]{:S(2)}, u32[]{:S(2)}) collective-permute-start(bf16[256,3072]{1,0:T(8,128)(2,1)} %get-tuple-element.34), channel_id=1, source_target_pairs={{0,1},{1,0},{2,3},{3,2},{4,5},{5,4},{6,7},{7,6},{8,9},{9,8},{10,11... | collective-permute-start | bytes 4718600 | tf_op jit(solution)/shard_map/stream/ppermute | solution.py:53
  112.3 6.4 %collective-permute-start.24 = (bf16[256,3072]{1,0:T(8,128)(2,1)}, bf16[256,3072]{1,0:T(8,128)(2,1)S(1)}, u32[]{:S(2)}, u32[]{:S(2)}) collective-permute-start(bf16[256,3072]{1,0:T(8,128)(2,1)} %get-tuple-element.35), channel_id=1, source_target_pairs={{0,1},{1,0},{2,3},{3,2},{4,5},{5,4},{6,7},{7,6},{8,9},{9,8},{10,11... | collective-permute-start | bytes 4718600 | tf_op jit(solution)/shard_map/stream/ppermute | solution.py:53
  118.7 45.0 %collective-permute-start.25 = (bf16[256,3072]{1,0:T(8,128)(2,1)}, bf16[256,3072]{1,0:T(8,128)(2,1)}, u32[]{:S(2)}, u32[]{:S(2)}) collective-permute-start(bf16[256,3072]{1,0:T(8,128)(2,1)} %add_convert_fusion), channel_id=1, source_target_pairs={{0,2},{1,3},{2,0},{3,1},{4,6},{5,7},{6,4},{7,5},{8,10},{9,11},{10,... | collective-permute-start | bytes 4718600 | tf_op jit(solution)/shard_map/stream/ppermute | solution.py:53
  124.2 39.5 %copy-start.3 = (bf16[256,3072]{1,0:T(8,128)(2,1)S(1)}, bf16[256,3072]{1,0:T(8,128)(2,1)}, u32[]{:S(2)}) copy-start(bf16[256,3072]{1,0:T(8,128)(2,1)} %get-tuple-element.32) | copy-start | bytes 4718596
  124.2 39.5 %copy-start.10 = (f32[1,3072]{1,0:T(1,128)S(1)}, f32[1,3072]{1,0:T(1,128)}, u32[]{:S(2)}) copy-start(f32[1,3072]{1,0:T(1,128)} %param.7) | copy-start | bytes 36868
  148.2 24.0 %all-to-all-start.2 = ((f32[32,1,128]{2,1,0:T(1,128)}), f32[32,1,128]{2,1,0:T(1,128)S(1)}, u32[]{:S(2)}, u32[]{:S(2)}) async-start(f32[32,1,128]{2,1,0:T(1,128)} %broadcast_in_dim.4), calls=%async_computation.2 | async-start | bytes 32768 | tf_op jit(solution)/shard_map/norm/all_to_all | solution.py:58
  (19 other events, 257.6 us)

commit v4 on v3

--- a/solution.py
+++ b/solution.py
@@ -13,8 +13,8 @@
 decay_rate = 0.1
 max_norm = 1.0
 
-AXES = ("yl", "x", "z", "yh", "c")
-SIZES = (2, 4, 8, 2, 2)
+AXES = ("yl", "xa", "xb", "z", "yh", "c")
+SIZES = (2, 2, 2, 8, 2, 2)
 NZ = 8
 OWN = 48
 WIDTH = 768
@@ -77,7 +77,7 @@
     for k, block in enumerate((b0, b1, b2, b3)):
         blocks[k * TOK : (k + 1) * TOK, :] = block[...]
     total = lax.dot_general(blocks[...], og[...], (((0,), (0,)), ((), ())), preferred_element_type=F32)
-    out[...] = total.astype(BF16)
+    out[...] = total.astype(BF16).reshape(2, 1, 1, NZ, OWN, WIDTH)
 
 
 def weight_grad(blocks, og):
@@ -86,9 +86,9 @@
         grad_kernel,
         grid=(D // tile,),
         in_specs=[pl.BlockSpec((TOK, tile), lambda i: (0, i))] * 4 + [pl.BlockSpec((4 * TOK, WIDTH), lambda i: (0, 0))],
-        out_specs=pl.BlockSpec((tile, WIDTH), lambda i: (i, 0)),
+        out_specs=pl.BlockSpec((2, 1, 1, NZ, OWN, WIDTH), lambda i: (0, lax.rem(i, 2), i // 2, 0, 0, 0)),
         scratch_shapes=[pltpu.VMEM((4 * TOK, tile), BF16)],
-        out_shape=jax.ShapeDtypeStruct((D, WIDTH), BF16),
+        out_shape=jax.ShapeDtypeStruct((2, 2, 2, NZ, OWN, WIDTH), BF16),
         compiler_params=pltpu.CompilerParams(vmem_limit_bytes=VMEM_LIMIT),
         cost_estimate=pl.CostEstimate(flops=8 * TOK * WIDTH * D, bytes_accessed=16 * 1024 * 1024, transcendentals=0),
         name="weight_grad",
@@ -137,7 +137,7 @@
 
 
 def body(block_out, gate, out_grad, zero_weight, first_moment, second_moment):
-    here = jnp.stack([lax.axis_index("yl"), lax.axis_index("x"), lax.axis_index("z")]).astype(jnp.int32)
+    here = jnp.stack([lax.axis_index("yl"), lax.axis_index(("xa", "xb")), lax.axis_index("z")]).astype(jnp.int32)
     ti = lax.axis_index("yh") * 2 + lax.axis_index("c")
 
     order = [lax.dynamic_slice_in_dim(out_grad, lax.bitwise_xor(ti, k) * TOK, TOK, 0) for k in range(4)]
@@ -167,7 +167,7 @@
         grad = weight_grad((block_out, near, far, far_near), out_grad)
 
     with jax.named_scope("grad_scatter"):
-        got = lax.all_to_all(grad.reshape(8, NZ, OWN, WIDTH), ("yl", "x"), 0, 0, tiled=True)
+        got = lax.all_to_all(grad.reshape(8, NZ, OWN, WIDTH), ("xb", "xa", "yl"), 0, 0, tiled=True)
 
     with jax.named_scope("weight_gather"):
         first_1, fourth_0 = lax.optimization_barrier((first_1, fourth_0, grad))[:2]
@@ -194,7 +194,7 @@
 
     with jax.named_scope("norm"):
         local = jnp.sum(owner_grad * owner_grad)
-        local = gather(jnp.full((1, 128), local, F32), ("x", "z"), 32)
+        local = gather(jnp.full((1, 128), local, F32), ("xa", "xb", "z"), 32)
         stream = add(p0, r1, q2)
         stream_out = stream.astype(BF16)
         branch_out = (gate * stream).astype(BF16)
@@ -212,7 +212,7 @@
 
 def solution(mesh):
     fine = Mesh(mesh.devices.reshape(SIZES), AXES)
-    dp, tensor = ("yl", "x", "z"), ("yh", "c")
+    dp, tensor = ("yl", "xa", "xb", "z"), ("yh", "c")
     placed = (P(AXES, None), P(dp, None), P(dp, tensor), P(dp, tensor), P(dp, tensor), P(dp, tensor))
     return jax.shard_map(
         body,

time: 186 us -> 181 us (0.973)
  starting transfers between devices: 63.6 us -> 52.8 us
  waiting for transfers between devices: 48.2 us -> 52.6 us
    all_to_all x1, starting transfers between devices: 15.5 us -> 4.58 us  [gather(): return lax.all_to_all(copies, axes, 0, 0, tiled=True)]
    all_to_all x1, waiting for transfers between devices: 0.01 us -> 4.73 us  [body(): lax.all_to_all(grad.reshape(8, NZ, OWN, WIDTH), ('xb', 'xa', 'yl'), 0, 0,...]
  transfers between devices with their start and end apart: 28 -> 28, of which waited for: 12 -> 13; matrix products, arithmetic and copies ran while one was open for 9% -> 9% of each run, Pallas kernels for 10% -> 10%
where the time goes in v4:
time: 181 us; the launch traced here: 180 us
  starting transfers between devices  52.8 us (29%)
  waiting for transfers between devices  52.6 us (29%)
  blocking collectives  34 us (19%)
  Pallas kernels  18.2 us (10%)
  other arithmetic  15.1 us (8%)
  local copies, waits for them, and re-layouts  6.13 us (3%)
    ppermute x26, starting transfers between devices, send(): return lax.ppermute(value, AXES, perm)  43.6 us
    ppermute x26, waiting for transfers between devices, send(): return lax.ppermute(value, AXES, perm)  43.4 us
    all_to_all x1, blocking collectives, body(): owner_grad = add(*lax.all_to_all(total, ('z',), 0, 0, tiled=True))  22.6 us
    all_to_all x1, blocking collectives, gather(): return lax.all_to_all(copies, axes, 0, 0, tiled=True)  11.5 us
    pallas_call x1, Pallas kernels, stream_parts(): pl.pallas_call(stream_kernel, grid_spec=pltpu.PrefetchScalarGridSpec(num_...  10.9 us
    pallas_call x1, Pallas kernels, weight_grad(): pl.pallas_call(grad_kernel, grid=(D // tile,), in_specs=[pl.BlockSpec((TO...  7.39 us
    all_to_all x1, waiting for transfers between devices, body(): lax.all_to_all(grad.reshape(8, NZ, OWN, WIDTH), ('xb', 'xa', 'yl'), 0, 0,...  4.73 us
    all_to_all x1, starting transfers between devices, body(): lax.all_to_all(grad.reshape(8, NZ, OWN, WIDTH), ('xb', 'xa', 'yl'), 0, 0,...  4.6 us
  transfers between devices with their start and end apart: 28, of which 13 were waited for; matrix products, arithmetic and copies ran while one was open for 9% of the time, Pallas kernels for 10%

profile of v4, /device:TPU:1, one launch (start us, length us, event | category | flops | bytes accessed | tf_op | source)
XLA Modules:
  0.0 180.1 jit_solution(17694539191851829998)
XLA Ops:
  0.6 3.3 %collective-permute-start.3 = (bf16[256,3072]{1,0:T(8,128)(2,1)}, bf16[256,3072]{1,0:T(8,128)(2,1)S(1)}, u32[]{:S(2)}, u32[]{:S(2)}) collective-permute-start(bf16[256,3072]{1,0:T(8,128)(2,1)} %b0.1), channel_id=1, source_target_pairs={{0,1},{1,0},{2,3},{3,2},{4,5},{5,4},{6,7},{7,6},{8,9},{9,8},{10,11... | collective-permute-start | bytes 4718600 | tf_op jit(solution)/shard_map/start/ppermute | solution.py:53
  7.4 2.5 %collective-permute-start.1 = (bf16[48,768]{1,0:T(8,128)(2,1)S(1)}, bf16[48,768]{1,0:T(8,128)(2,1)S(1)}, u32[]{:S(2)}, u32[]{:S(2)}) collective-permute-start(bf16[48,768]{1,0:T(8,128)(2,1)S(1)} %convert_element_type.110), channel_id=1, source_target_pairs={{0,64},{1,65},{2,66},{3,67},{4,68},{5,69},{6,70},{7,71},{8,72},{9,... | collective-permute-start | bytes 221192 | tf_op jit(solution)/shard_map/start/ppermute | solution.py:53
  15.3 4.0 %collective-permute-start.8 = (bf16[4,48,768]{2,1,0:T(8,128)(2,1)S(1)}, bf16[4,48,768]{2,1,0:T(8,128)(2,1)S(1)}, u32[]{:S(2)}, u32[]{:S(2)}) collective-permute-start(bf16[4,48,768]{2,1,0:T(8,128)(2,1)S(1)} %pad_maximum_fusion.1.refs_0_), channel_id=1, source_target_pairs={{0,28},{1,29},{2,30},{3,31},{4,0},{5,1},{6,2},{7,3},{8,4},{9,5},{1... | collective-permute-start | bytes 884744 | tf_op jit(solution)/shard_map/weight_gather/ppermute | solution.py:53
  19.3 5.8 %collective-permute-done.5.refs_6_ = bf16[4,48,768]{2,1,0:T(8,128)(2,1)S(1)} collective-permute-done((bf16[4,48,768]{2,1,0:T(8,128)(2,1)S(1)}, bf16[4,48,768]{2,1,0:T(8,128)(2,1)S(1)}, u32[]{:S(2)}, u32[]{:S(2)}) %collective-permute-start.5) | collective-permute-done | bytes 294944 | tf_op jit(solution)/shard_map/weight_gather/ppermute | solution.py:53
  25.1 2.7 %collective-permute-start.9 = (bf16[4,48,768]{2,1,0:T(8,128)(2,1)S(1)}, bf16[4,48,768]{2,1,0:T(8,128)(2,1)}, u32[]{:S(2)}, u32[]{:S(2)}) collective-permute-start(bf16[4,48,768]{2,1,0:T(8,128)(2,1)S(1)} %collective-permute-done.8.refs_1_), channel_id=1, source_target_pairs={{0,28},{1,29},{2,30},{3,31},{4,0},{5,1},{6,2},{7,3},{8,4},{9,5},{1... | collective-permute-start | bytes 884744 | tf_op jit(solution)/shard_map/weight_gather/ppermute | solution.py:53
  27.8 5.0 %collective-permute-done.6.refs_5_ = bf16[4,48,768]{2,1,0:T(8,128)(2,1)S(1)} collective-permute-done((bf16[4,48,768]{2,1,0:T(8,128)(2,1)S(1)}, bf16[4,48,768]{2,1,0:T(8,128)(2,1)S(1)}, u32[]{:S(2)}, u32[]{:S(2)}) %collective-permute-start.6) | collective-permute-done | bytes 294944 | tf_op jit(solution)/shard_map/weight_gather/ppermute | solution.py:53
  32.9 2.7 %collective-permute-start.10 = (bf16[4,48,768]{2,1,0:T(8,128)(2,1)}, bf16[4,48,768]{2,1,0:T(8,128)(2,1)S(1)}, u32[]{:S(2)}, u32[]{:S(2)}) collective-permute-start(bf16[4,48,768]{2,1,0:T(8,128)(2,1)} %collective-permute-done.9.refs_2_), channel_id=1, source_target_pairs={{0,28},{1,29},{2,30},{3,31},{4,0},{5,1},{6,2},{7,3},{8,4},{9,5},{1... | collective-permute-start | bytes 884744 | tf_op jit(solution)/shard_map/weight_gather/ppermute | solution.py:53
  37.1 4.6 %collective-permute-done.4.b2 = bf16[256,3072]{1,0:T(8,128)(2,1)} collective-permute-done((bf16[256,3072]{1,0:T(8,128)(2,1)}, bf16[256,3072]{1,0:T(8,128)(2,1)}, u32[]{:S(2)}, u32[]{:S(2)}) %collective-permute-start.4) | collective-permute-done | bytes 1572896 | tf_op jit(solution)/shard_map/start/ppermute | solution.py:53
  43.9 3.1 %collective-permute-done.11.b3 = bf16[256,3072]{1,0:T(8,128)(2,1)S(1)} collective-permute-done((bf16[256,3072]{1,0:T(8,128)(2,1)}, bf16[256,3072]{1,0:T(8,128)(2,1)S(1)}, u32[]{:S(2)}, u32[]{:S(2)}) %collective-permute-start.11) | collective-permute-done | bytes 1572896 | tf_op jit(solution)/shard_map/weight_grad/ppermute | solution.py:53
  47.0 7.4 %weight_grad.1 = bf16[2,2,2,8,48,768]{5,4,3,2,1,0:T(8,128)(2,1)S(1)} custom-call(bf16[256,3072]{1,0:T(8,128)(2,1)S(1)} %copy-done.2, bf16[256,3072]{1,0:T(8,128)(2,1)S(1)} %collective-permute-done.3.b1, bf16[256,3072]{1,0:T(8,128)(2,1)} %collective-permute-done.4.b2, bf16[256,3072]{1,0:T(8,128)(2,1)S(1)} %collective-permute-done.11.b3, ...), custom_call_target="tpu_custom_call" | custom-call | flops 4831838208 | bytes 16777216 | tf_op jit(solution)/shard_map/weight_grad/weight_grad/pallas_call | solution.py:85
  54.5 2.2 %copy-done = bf16[2,2,2,8,48,768]{5,4,3,2,1,0:T(8,128)(2,1)} copy-done((bf16[2,2,2,8,48,768]{5,4,3,2,1,0:T(8,128)(2,1)}, bf16[2,2,2,8,48,768]{5,4,3,2,1,0:T(8,128)(2,1)S(1)}, u32[]{:S(2)}) %copy-start) | copy-done | bytes 4718616
  56.6 4.6 %all-to-all-start = ((bf16[8,8,48,768]{3,2,1,0:T(8,128)(2,1)}), bf16[8,8,48,768]{3,2,1,0:T(8,128)(2,1)}, u32[]{:S(2)}, u32[]{:S(2)}) async-start(bf16[8,8,48,768]{3,2,1,0:T(8,128)(2,1)} %bitcast.25), calls=%async_computation | async-start | bytes 9437184 | tf_op jit(solution)/shard_map/grad_scatter/all_to_all | solution.py:170
  61.3 3.4 %collective-permute-start.14 = (bf16[4,48,768]{2,1,0:T(8,128)(2,1)S(1)}, bf16[4,48,768]{2,1,0:T(8,128)(2,1)S(1)}, u32[]{:S(2)}, u32[]{:S(2)}) collective-permute-start(bf16[4,48,768]{2,1,0:T(8,128)(2,1)S(1)} %collective-permute-done.12.refs_9_), channel_id=1, source_target_pairs={{0,28},{1,29},{2,30},{3,31},{4,0},{5,1},{6,2},{7,3},{8,4},{9,5},{1... | collective-permute-start | bytes 884744 | tf_op jit(solution)/shard_map/weight_gather/ppermute | solution.py:53
  64.9 2.7 %collective-permute-start.16 = (bf16[2,48,768]{2,1,0:T(8,128)(2,1)S(1)}, bf16[2,48,768]{2,1,0:T(8,128)(2,1)S(1)}, u32[]{:S(2)}, u32[]{:S(2)}) collective-permute-start(bf16[2,48,768]{2,1,0:T(8,128)(2,1)S(1)} %slice.16), channel_id=1, source_target_pairs={{0,28},{1,29},{2,30},{3,31},{4,0},{5,1},{6,2},{7,3},{8,4},{9,5},{1... | collective-permute-start | bytes 442376 | tf_op jit(solution)/shard_map/weight_gather/ppermute | solution.py:53
  67.6 3.6 %collective-permute-done.13.refs_15_ = bf16[4,48,768]{2,1,0:T(8,128)(2,1)S(1)} collective-permute-done((bf16[4,48,768]{2,1,0:T(8,128)(2,1)S(1)}, bf16[4,48,768]{2,1,0:T(8,128)(2,1)S(1)}, u32[]{:S(2)}, u32[]{:S(2)}) %collective-permute-start.13) | collective-permute-done | bytes 294944 | tf_op jit(solution)/shard_map/weight_gather/ppermute | solution.py:53
  71.3 3.2 %collective-permute-done.15.refs_7_ = bf16[2,48,768]{2,1,0:T(8,128)(2,1)S(1)} collective-permute-done((bf16[2,48,768]{2,1,0:T(8,128)(2,1)S(1)}, bf16[2,48,768]{2,1,0:T(8,128)(2,1)S(1)}, u32[]{:S(2)}, u32[]{:S(2)}) %collective-permute-start.15) | collective-permute-done | bytes 147488 | tf_op jit(solution)/shard_map/weight_gather/ppermute | solution.py:53
  77.2 5.9 %collective-permute-done.19.refs_14_ = bf16[4,48,768]{2,1,0:T(8,128)(2,1)S(1)} collective-permute-done((bf16[4,48,768]{2,1,0:T(8,128)(2,1)S(1)}, bf16[4,48,768]{2,1,0:T(8,128)(2,1)S(1)}, u32[]{:S(2)}, u32[]{:S(2)}) %collective-permute-start.19) | collective-permute-done | bytes 294944 | tf_op jit(solution)/shard_map/weight_gather/ppermute | solution.py:53
  85.8 5.1 %collective-permute-done.20.refs_13_ = bf16[4,48,768]{2,1,0:T(8,128)(2,1)S(1)} collective-permute-done((bf16[4,48,768]{2,1,0:T(8,128)(2,1)S(1)}, bf16[4,48,768]{2,1,0:T(8,128)(2,1)S(1)}, u32[]{:S(2)}, u32[]{:S(2)}) %collective-permute-start.20) | collective-permute-done | bytes 294944 | tf_op jit(solution)/shard_map/weight_gather/ppermute | solution.py:53
  91.1 2.7 %collective-permute-start.22 = (bf16[2,48,768]{2,1,0:T(8,128)(2,1)S(1)}, bf16[2,48,768]{2,1,0:T(8,128)(2,1)S(1)}, u32[]{:S(2)}, u32[]{:S(2)}) collective-permute-start(bf16[2,48,768]{2,1,0:T(8,128)(2,1)S(1)} %slice.21), channel_id=1, source_target_pairs={{0,28},{1,29},{2,30},{3,31},{4,0},{5,1},{6,2},{7,3},{8,4},{9,5},{1... | collective-permute-start | bytes 442376 | tf_op jit(solution)/shard_map/weight_gather/ppermute | solution.py:53
  94.3 2.3 %collective-permute-done.21.refs_16_ = bf16[2,48,768]{2,1,0:T(8,128)(2,1)S(1)} collective-permute-done((bf16[2,48,768]{2,1,0:T(8,128)(2,1)S(1)}, bf16[2,48,768]{2,1,0:T(8,128)(2,1)S(1)}, u32[]{:S(2)}, u32[]{:S(2)}) %collective-permute-start.21) | collective-permute-done | bytes 147488 | tf_op jit(solution)/shard_map/weight_gather/ppermute | solution.py:53
  97.9 10.9 %stream_parts.1 = (bf16[256,3072]{1,0:T(8,128)(2,1)}, bf16[256,3072]{1,0:T(8,128)(2,1)}, bf16[256,3072]{1,0:T(8,128)(2,1)}, bf16[256,3072]{1,0:T(8,128)(2,1)}) custom-call(s32[3]{0:T(128)} %pad_add_fusion.here, bf16[1024,768]{1,0:T(8,128)(2,1)} %copy-done.1, bf16[4,48,768]{2,1,0:T(8,128)(2,1)} %copy-done.5, bf16[4,48,768]{2,1,0:T(8,128)(2,1)} %copy-done.12, ...), custom_call_target="tpu_custom_call" | custom-call | flops 4831838208 | bytes 16777216 | tf_op jit(solution)/shard_map/stream/stream_parts/pallas_call | solution.py:123
  108.8 3.7 %collective-permute-start.23 = (bf16[256,3072]{1,0:T(8,128)(2,1)}, bf16[256,3072]{1,0:T(8,128)(2,1)S(1)}, u32[]{:S(2)}, u32[]{:S(2)}) collective-permute-start(bf16[256,3072]{1,0:T(8,128)(2,1)} %get-tuple-element.34), channel_id=1, source_target_pairs={{0,1},{1,0},{2,3},{3,2},{4,5},{5,4},{6,7},{7,6},{8,9},{9,8},{10,11... | collective-permute-start | bytes 4718600 | tf_op jit(solution)/shard_map/stream/ppermute | solution.py:53
  112.5 3.1 %collective-permute-done.23 = bf16[256,3072]{1,0:T(8,128)(2,1)S(1)} collective-permute-done((bf16[256,3072]{1,0:T(8,128)(2,1)}, bf16[256,3072]{1,0:T(8,128)(2,1)S(1)}, u32[]{:S(2)}, u32[]{:S(2)}) %collective-permute-start.23) | collective-permute-done | bytes 1572896 | tf_op jit(solution)/shard_map/stream/ppermute | solution.py:53
  115.7 3.1 %add_convert_fusion = bf16[256,3072]{1,0:T(8,128)(2,1)} fusion(bf16[256,3072]{1,0:T(8,128)(2,1)S(1)} %collective-permute-done.23, bf16[256,3072]{1,0:T(8,128)(2,1)} %get-tuple-element.33), kind=kLoop, calls=%fused_computation.2 | loop fusion | flops 3145728 | bytes 4718592 | tf_op jit(solution)/shard_map/stream/convert_element_type | solution.py:187
  118.8 2.6 %collective-permute-start.25 = (bf16[256,3072]{1,0:T(8,128)(2,1)}, bf16[256,3072]{1,0:T(8,128)(2,1)}, u32[]{:S(2)}, u32[]{:S(2)}) collective-permute-start(bf16[256,3072]{1,0:T(8,128)(2,1)} %add_convert_fusion), channel_id=1, source_target_pairs={{0,2},{1,3},{2,0},{3,1},{4,6},{5,7},{6,4},{7,5},{8,10},{9,11},{10,... | collective-permute-start | bytes 4718600 | tf_op jit(solution)/shard_map/stream/ppermute | solution.py:53
  121.4 4.7 %all-to-all-done = bf16[8,8,48,768]{3,2,1,0:T(8,128)(2,1)} async-done(((bf16[8,8,48,768]{3,2,1,0:T(8,128)(2,1)}), bf16[8,8,48,768]{3,2,1,0:T(8,128)(2,1)}, u32[]{:S(2)}, u32[]{:S(2)}) %all-to-all-start) | async-done | bytes 4718624 | tf_op jit(solution)/shard_map/grad_scatter/all_to_all | solution.py:170
  126.2 2.9 %fusion.1 = bf16[8,48,768]{2,1,0:T(8,128)(2,1)S(1)} fusion(bf16[8,8,48,768]{3,2,1,0:T(8,128)(2,1)} %all-to-all-done), kind=kLoop, calls=%fused_computation.6 | loop fusion | flops 4718592 | bytes 5308416 | tf_op jit(solution)/shard_map/grad_scatter/convert_element_type | solution.py:192
  129.1 22.6 %all_to_all.20 = bf16[8,48,768]{2,1,0:T(8,128)(2,1)S(1)} all-to-all(bf16[8,48,768]{2,1,0:T(8,128)(2,1)S(1)} %fusion.1), channel_id=1, replica_groups=mesh['yl'=2,'xa'=2,'xb'=2,'z'=8,'yh'=2,'c'=2] {'z'}, dimensions={0} | all-to-all | bytes 1179648 | tf_op jit(solution)/shard_map/grad_scatter/all_to_all | solution.py:193
  153.5 4.6 %all-to-all-start.2 = ((f32[32,1,128]{2,1,0:T(1,128)}), f32[32,1,128]{2,1,0:T(1,128)S(1)}, u32[]{:S(2)}, u32[]{:S(2)}) async-start(f32[32,1,128]{2,1,0:T(1,128)} %broadcast_in_dim.4), calls=%async_computation.2 | async-start | bytes 32768 | tf_op jit(solution)/shard_map/norm/all_to_all | solution.py:58
  158.1 4.1 %multiply_convert_fusion = (bf16[256,3072]{1,0:T(8,128)(2,1)}, bf16[256,3072]{1,0:T(8,128)(2,1)}) fusion(bf16[256,3072]{1,0:T(8,128)(2,1)} %collective-permute-done.25, bf16[256,3072]{1,0:T(8,128)(2,1)S(1)} %collective-permute-done.24, bf16[256,3072]{1,0:T(8,128)(2,1)S(1)} %copy-done.3, f32[3072]{0:T(1024)S(1)} %bitcast.30), kind=kLoop, calls=%fused_computation | loop fusion | flops 6291456 | bytes 7876608 | tf_op jit(solution)/shard_map/norm/convert_element_type | solution.py:200
  162.2 4.5 %all-to-all-done.2 = f32[32,1,128]{2,1,0:T(1,128)S(1)} async-done(((f32[32,1,128]{2,1,0:T(1,128)}), f32[32,1,128]{2,1,0:T(1,128)S(1)}, u32[]{:S(2)}, u32[]{:S(2)}) %all-to-all-start.2) | async-done | bytes 16416 | tf_op jit(solution)/shard_map/norm/all_to_all | solution.py:58
  166.7 11.5 %all_to_all.21 = f32[8,1,128]{2,1,0:T(1,128)S(1)} all-to-all(f32[8,1,128]{2,1,0:T(1,128)S(1)} %broadcast_in_dim.10), channel_id=1, replica_groups=mesh['yl'=2,'xa'=2,'xb'=2,'z'=8,'yh'=2,'c'=2] {'yl','yh','c'}, dimensions={0} | all-to-all | bytes 8192 | tf_op jit(solution)/shard_map/norm/all_to_all | solution.py:58
  (93 shorter events, 23.9 us)
Async XLA Ops:
  0.6 13.0 %collective-permute-start.3 = (bf16[256,3072]{1,0:T(8,128)(2,1)}, bf16[256,3072]{1,0:T(8,128)(2,1)S(1)}, u32[]{:S(2)}, u32[]{:S(2)}) collective-permute-start(bf16[256,3072]{1,0:T(8,128)(2,1)} %b0.1), channel_id=1, source_target_pairs={{0,1},{1,0},{2,3},{3,2},{4,5},{5,4},{6,7},{7,6},{8,9},{9,8},{10,11... | collective-permute-start | bytes 4718600 | tf_op jit(solution)/shard_map/start/ppermute | solution.py:53
  4.0 37.8 %collective-permute-start.4 = (bf16[256,3072]{1,0:T(8,128)(2,1)}, bf16[256,3072]{1,0:T(8,128)(2,1)}, u32[]{:S(2)}, u32[]{:S(2)}) collective-permute-start(bf16[256,3072]{1,0:T(8,128)(2,1)} %b0.1), channel_id=1, source_target_pairs={{0,2},{1,3},{2,0},{3,1},{4,6},{5,7},{6,4},{7,5},{8,10},{9,11},{10,... | collective-permute-start | bytes 4718600 | tf_op jit(solution)/shard_map/start/ppermute | solution.py:53
  6.1 5.8 %collective-permute-start.2 = (bf16[48,768]{1,0:T(8,128)(2,1)S(1)}, bf16[48,768]{1,0:T(8,128)(2,1)S(1)}, u32[]{:S(2)}, u32[]{:S(2)}) collective-permute-start(bf16[48,768]{1,0:T(8,128)(2,1)S(1)} %convert_element_type.110), channel_id=1, source_target_pairs={{0,32},{1,33},{2,34},{3,35},{4,36},{5,37},{6,38},{7,39},{8,40},{9,... | collective-permute-start | bytes 221192 | tf_op jit(solution)/shard_map/start/ppermute | solution.py:53
  7.4 6.2 %collective-permute-start.1 = (bf16[48,768]{1,0:T(8,128)(2,1)S(1)}, bf16[48,768]{1,0:T(8,128)(2,1)S(1)}, u32[]{:S(2)}, u32[]{:S(2)}) collective-permute-start(bf16[48,768]{1,0:T(8,128)(2,1)S(1)} %convert_element_type.110), channel_id=1, source_target_pairs={{0,64},{1,65},{2,66},{3,67},{4,68},{5,69},{6,70},{7,71},{8,72},{9,... | collective-permute-start | bytes 221192 | tf_op jit(solution)/shard_map/start/ppermute | solution.py:53
  9.8 3.7 %collective-permute-start = (bf16[48,768]{1,0:T(8,128)(2,1)S(1)}, bf16[48,768]{1,0:T(8,128)(2,1)S(1)}, u32[]{:S(2)}, u32[]{:S(2)}) collective-permute-start(bf16[48,768]{1,0:T(8,128)(2,1)S(1)} %convert_element_type.110), channel_id=1, source_target_pairs={{0,96},{1,97},{2,98},{3,99},{4,100},{5,101},{6,102},{7,103},{8,104... | collective-permute-start | bytes 221192 | tf_op jit(solution)/shard_map/start/ppermute | solution.py:53
  13.6 30.2 %copy-start.5 = (bf16[4,48,768]{2,1,0:T(8,128)(2,1)}, bf16[4,48,768]{2,1,0:T(8,128)(2,1)S(1)}, u32[]{:S(2)}) copy-start(bf16[4,48,768]{2,1,0:T(8,128)(2,1)S(1)} %pad_maximum_fusion.1.refs_0_) | copy-start | bytes 884740
  13.6 11.5 %collective-permute-start.5 = (bf16[4,48,768]{2,1,0:T(8,128)(2,1)S(1)}, bf16[4,48,768]{2,1,0:T(8,128)(2,1)S(1)}, u32[]{:S(2)}, u32[]{:S(2)}) collective-permute-start(bf16[4,48,768]{2,1,0:T(8,128)(2,1)S(1)} %pad_maximum_fusion.1.refs_0_), channel_id=1, source_target_pairs={{0,4},{1,5},{2,6},{3,7},{4,8},{5,9},{6,10},{7,11},{8,12},{9,13},{1... | collective-permute-start | bytes 884744 | tf_op jit(solution)/shard_map/weight_gather/ppermute | solution.py:53
  15.3 9.8 %collective-permute-start.8 = (bf16[4,48,768]{2,1,0:T(8,128)(2,1)S(1)}, bf16[4,48,768]{2,1,0:T(8,128)(2,1)S(1)}, u32[]{:S(2)}, u32[]{:S(2)}) collective-permute-start(bf16[4,48,768]{2,1,0:T(8,128)(2,1)S(1)} %pad_maximum_fusion.1.refs_0_), channel_id=1, source_target_pairs={{0,28},{1,29},{2,30},{3,31},{4,0},{5,1},{6,2},{7,3},{8,4},{9,5},{1... | collective-permute-start | bytes 884744 | tf_op jit(solution)/shard_map/weight_gather/ppermute | solution.py:53
  25.1 7.7 %collective-permute-start.6 = (bf16[4,48,768]{2,1,0:T(8,128)(2,1)S(1)}, bf16[4,48,768]{2,1,0:T(8,128)(2,1)S(1)}, u32[]{:S(2)}, u32[]{:S(2)}) collective-permute-start(bf16[4,48,768]{2,1,0:T(8,128)(2,1)S(1)} %collective-permute-done.5.refs_6_), channel_id=1, source_target_pairs={{0,4},{1,5},{2,6},{3,7},{4,8},{5,9},{6,10},{7,11},{8,12},{9,13},{1... | collective-permute-start | bytes 884744 | tf_op jit(solution)/shard_map/weight_gather/ppermute | solution.py:53
  25.1 7.7 %collective-permute-start.9 = (bf16[4,48,768]{2,1,0:T(8,128)(2,1)S(1)}, bf16[4,48,768]{2,1,0:T(8,128)(2,1)}, u32[]{:S(2)}, u32[]{:S(2)}) collective-permute-start(bf16[4,48,768]{2,1,0:T(8,128)(2,1)S(1)} %collective-permute-done.8.refs_1_), channel_id=1, source_target_pairs={{0,28},{1,29},{2,30},{3,31},{4,0},{5,1},{6,2},{7,3},{8,4},{9,5},{1... | collective-permute-start | bytes 884744 | tf_op jit(solution)/shard_map/weight_gather/ppermute | solution.py:53
  32.8 8.9 %collective-permute-start.7 = (bf16[4,48,768]{2,1,0:T(8,128)(2,1)S(1)}, bf16[4,48,768]{2,1,0:T(8,128)(2,1)S(1)}, u32[]{:S(2)}, u32[]{:S(2)}) collective-permute-start(bf16[4,48,768]{2,1,0:T(8,128)(2,1)S(1)} %collective-permute-done.6.refs_5_), channel_id=1, source_target_pairs={{0,4},{1,5},{2,6},{3,7},{4,8},{5,9},{6,10},{7,11},{8,12},{9,13},{1... | collective-permute-start | bytes 884744 | tf_op jit(solution)/shard_map/weight_gather/ppermute | solution.py:53
  32.9 8.9 %collective-permute-start.10 = (bf16[4,48,768]{2,1,0:T(8,128)(2,1)}, bf16[4,48,768]{2,1,0:T(8,128)(2,1)S(1)}, u32[]{:S(2)}, u32[]{:S(2)}) collective-permute-start(bf16[4,48,768]{2,1,0:T(8,128)(2,1)} %collective-permute-done.9.refs_2_), channel_id=1, source_target_pairs={{0,28},{1,29},{2,30},{3,31},{4,0},{5,1},{6,2},{7,3},{8,4},{9,5},{1... | collective-permute-start | bytes 884744 | tf_op jit(solution)/shard_map/weight_gather/ppermute | solution.py:53
  41.8 5.3 %collective-permute-start.11 = (bf16[256,3072]{1,0:T(8,128)(2,1)}, bf16[256,3072]{1,0:T(8,128)(2,1)S(1)}, u32[]{:S(2)}, u32[]{:S(2)}) collective-permute-start(bf16[256,3072]{1,0:T(8,128)(2,1)} %collective-permute-done.4.b2), channel_id=1, source_target_pairs={{0,1},{1,0},{2,3},{3,2},{4,5},{5,4},{6,7},{7,6},{8,9},{9,8},{10,11... | collective-permute-start | bytes 4718600 | tf_op jit(solution)/shard_map/weight_grad/ppermute | solution.py:53
  43.8 17.4 %collective-permute-start.12 = (bf16[4,48,768]{2,1,0:T(8,128)(2,1)S(1)}, bf16[4,48,768]{2,1,0:T(8,128)(2,1)S(1)}, u32[]{:S(2)}, u32[]{:S(2)}) collective-permute-start(bf16[4,48,768]{2,1,0:T(8,128)(2,1)S(1)} %pad_maximum_fusion.1.refs_0_), channel_id=1, source_target_pairs={{0,128},{1,129},{2,130},{3,131},{4,132},{5,133},{6,134},{7,135},{8... | collective-permute-start | bytes 884744 | tf_op jit(solution)/shard_map/start/ppermute | solution.py:53
  56.6 69.6 %all-to-all-start = ((bf16[8,8,48,768]{3,2,1,0:T(8,128)(2,1)}), bf16[8,8,48,768]{3,2,1,0:T(8,128)(2,1)}, u32[]{:S(2)}, u32[]{:S(2)}) async-start(bf16[8,8,48,768]{3,2,1,0:T(8,128)(2,1)} %bitcast.25), calls=%async_computation | async-start | bytes 9437184 | tf_op jit(solution)/shard_map/grad_scatter/all_to_all | solution.py:170
  61.2 35.4 %copy-start.14 = (bf16[4,48,768]{2,1,0:T(8,128)(2,1)}, bf16[4,48,768]{2,1,0:T(8,128)(2,1)S(1)}, u32[]{:S(2)}) copy-start(bf16[4,48,768]{2,1,0:T(8,128)(2,1)S(1)} %collective-permute-done.12.refs_9_) | copy-start | bytes 884740
  61.2 10.0 %collective-permute-start.13 = (bf16[4,48,768]{2,1,0:T(8,128)(2,1)S(1)}, bf16[4,48,768]{2,1,0:T(8,128)(2,1)S(1)}, u32[]{:S(2)}, u32[]{:S(2)}) collective-permute-start(bf16[4,48,768]{2,1,0:T(8,128)(2,1)S(1)} %collective-permute-done.12.refs_9_), channel_id=1, source_target_pairs={{0,4},{1,5},{2,6},{3,7},{4,8},{5,9},{6,10},{7,11},{8,12},{9,13},{1... | collective-permute-start | bytes 884744 | tf_op jit(solution)/shard_map/weight_gather/ppermute | solution.py:53
  61.3 9.9 %collective-permute-start.14 = (bf16[4,48,768]{2,1,0:T(8,128)(2,1)S(1)}, bf16[4,48,768]{2,1,0:T(8,128)(2,1)S(1)}, u32[]{:S(2)}, u32[]{:S(2)}) collective-permute-start(bf16[4,48,768]{2,1,0:T(8,128)(2,1)S(1)} %collective-permute-done.12.refs_9_), channel_id=1, source_target_pairs={{0,28},{1,29},{2,30},{3,31},{4,0},{5,1},{6,2},{7,3},{8,4},{9,5},{1... | collective-permute-start | bytes 884744 | tf_op jit(solution)/shard_map/weight_gather/ppermute | solution.py:53
  64.8 9.6 %collective-permute-start.15 = (bf16[2,48,768]{2,1,0:T(8,128)(2,1)S(1)}, bf16[2,48,768]{2,1,0:T(8,128)(2,1)S(1)}, u32[]{:S(2)}, u32[]{:S(2)}) collective-permute-start(bf16[2,48,768]{2,1,0:T(8,128)(2,1)S(1)} %slice.15), channel_id=1, source_target_pairs={{0,4},{1,5},{2,6},{3,7},{4,8},{5,9},{6,10},{7,11},{8,12},{9,13},{1... | collective-permute-start | bytes 442376 | tf_op jit(solution)/shard_map/weight_gather/ppermute | solution.py:53
  64.9 9.5 %collective-permute-start.16 = (bf16[2,48,768]{2,1,0:T(8,128)(2,1)S(1)}, bf16[2,48,768]{2,1,0:T(8,128)(2,1)S(1)}, u32[]{:S(2)}, u32[]{:S(2)}) collective-permute-start(bf16[2,48,768]{2,1,0:T(8,128)(2,1)S(1)} %slice.16), channel_id=1, source_target_pairs={{0,28},{1,29},{2,30},{3,31},{4,0},{5,1},{6,2},{7,3},{8,4},{9,5},{1... | collective-permute-start | bytes 442376 | tf_op jit(solution)/shard_map/weight_gather/ppermute | solution.py:53
  74.4 8.7 %collective-permute-start.19 = (bf16[4,48,768]{2,1,0:T(8,128)(2,1)S(1)}, bf16[4,48,768]{2,1,0:T(8,128)(2,1)S(1)}, u32[]{:S(2)}, u32[]{:S(2)}) collective-permute-start(bf16[4,48,768]{2,1,0:T(8,128)(2,1)S(1)} %collective-permute-done.13.refs_15_), channel_id=1, source_target_pairs={{0,4},{1,5},{2,6},{3,7},{4,8},{5,9},{6,10},{7,11},{8,12},{9,13},{1... | collective-permute-start | bytes 884744 | tf_op jit(solution)/shard_map/weight_gather/ppermute | solution.py:53
  76.3 7.5 %collective-permute-start.17 = (bf16[4,48,768]{2,1,0:T(8,128)(2,1)S(1)}, bf16[4,48,768]{2,1,0:T(8,128)(2,1)S(1)}, u32[]{:S(2)}, u32[]{:S(2)}) collective-permute-start(bf16[4,48,768]{2,1,0:T(8,128)(2,1)S(1)} %collective-permute-done.14.refs_10_), channel_id=1, source_target_pairs={{0,28},{1,29},{2,30},{3,31},{4,0},{5,1},{6,2},{7,3},{8,4},{9,5},{1... | collective-permute-start | bytes 884744 | tf_op jit(solution)/shard_map/weight_gather/ppermute | solution.py:53
  83.1 7.8 %collective-permute-start.20 = (bf16[4,48,768]{2,1,0:T(8,128)(2,1)S(1)}, bf16[4,48,768]{2,1,0:T(8,128)(2,1)S(1)}, u32[]{:S(2)}, u32[]{:S(2)}) collective-permute-start(bf16[4,48,768]{2,1,0:T(8,128)(2,1)S(1)} %collective-permute-done.19.refs_14_), channel_id=1, source_target_pairs={{0,4},{1,5},{2,6},{3,7},{4,8},{5,9},{6,10},{7,11},{8,12},{9,13},{1... | collective-permute-start | bytes 884744 | tf_op jit(solution)/shard_map/weight_gather/ppermute | solution.py:53
  83.8 7.2 %collective-permute-start.18 = (bf16[4,48,768]{2,1,0:T(8,128)(2,1)S(1)}, bf16[4,48,768]{2,1,0:T(8,128)(2,1)S(1)}, u32[]{:S(2)}, u32[]{:S(2)}) collective-permute-start(bf16[4,48,768]{2,1,0:T(8,128)(2,1)S(1)} %collective-permute-done.17.refs_11_), channel_id=1, source_target_pairs={{0,28},{1,29},{2,30},{3,31},{4,0},{5,1},{6,2},{7,3},{8,4},{9,5},{1... | collective-permute-start | bytes 884744 | tf_op jit(solution)/shard_map/weight_gather/ppermute | solution.py:53
  90.9 5.7 %collective-permute-start.21 = (bf16[2,48,768]{2,1,0:T(8,128)(2,1)S(1)}, bf16[2,48,768]{2,1,0:T(8,128)(2,1)S(1)}, u32[]{:S(2)}, u32[]{:S(2)}) collective-permute-start(bf16[2,48,768]{2,1,0:T(8,128)(2,1)S(1)} %slice.20), channel_id=1, source_target_pairs={{0,4},{1,5},{2,6},{3,7},{4,8},{5,9},{6,10},{7,11},{8,12},{9,13},{1... | collective-permute-start | bytes 442376 | tf_op jit(solution)/shard_map/weight_gather/ppermute | solution.py:53
  91.1 5.6 %collective-permute-start.22 = (bf16[2,48,768]{2,1,0:T(8,128)(2,1)S(1)}, bf16[2,48,768]{2,1,0:T(8,128)(2,1)S(1)}, u32[]{:S(2)}, u32[]{:S(2)}) collective-permute-start(bf16[2,48,768]{2,1,0:T(8,128)(2,1)S(1)} %slice.21), channel_id=1, source_target_pairs={{0,28},{1,29},{2,30},{3,31},{4,0},{5,1},{6,2},{7,3},{8,4},{9,5},{1... | collective-permute-start | bytes 442376 | tf_op jit(solution)/shard_map/weight_gather/ppermute | solution.py:53
  108.8 6.9 %collective-permute-start.23 = (bf16[256,3072]{1,0:T(8,128)(2,1)}, bf16[256,3072]{1,0:T(8,128)(2,1)S(1)}, u32[]{:S(2)}, u32[]{:S(2)}) collective-permute-start(bf16[256,3072]{1,0:T(8,128)(2,1)} %get-tuple-element.34), channel_id=1, source_target_pairs={{0,1},{1,0},{2,3},{3,2},{4,5},{5,4},{6,7},{7,6},{8,9},{9,8},{10,11... | collective-permute-start | bytes 4718600 | tf_op jit(solution)/shard_map/stream/ppermute | solution.py:53
  112.4 6.4 %collective-permute-start.24 = (bf16[256,3072]{1,0:T(8,128)(2,1)}, bf16[256,3072]{1,0:T(8,128)(2,1)S(1)}, u32[]{:S(2)}, u32[]{:S(2)}) collective-permute-start(bf16[256,3072]{1,0:T(8,128)(2,1)} %get-tuple-element.35), channel_id=1, source_target_pairs={{0,1},{1,0},{2,3},{3,2},{4,5},{5,4},{6,7},{7,6},{8,9},{9,8},{10,11... | collective-permute-start | bytes 4718600 | tf_op jit(solution)/shard_map/stream/ppermute | solution.py:53
  118.8 39.2 %collective-permute-start.25 = (bf16[256,3072]{1,0:T(8,128)(2,1)}, bf16[256,3072]{1,0:T(8,128)(2,1)}, u32[]{:S(2)}, u32[]{:S(2)}) collective-permute-start(bf16[256,3072]{1,0:T(8,128)(2,1)} %add_convert_fusion), channel_id=1, source_target_pairs={{0,2},{1,3},{2,0},{3,1},{4,6},{5,7},{6,4},{7,5},{8,10},{9,11},{10,... | collective-permute-start | bytes 4718600 | tf_op jit(solution)/shard_map/stream/ppermute | solution.py:53
  129.1 29.0 %copy-start.3 = (bf16[256,3072]{1,0:T(8,128)(2,1)S(1)}, bf16[256,3072]{1,0:T(8,128)(2,1)}, u32[]{:S(2)}) copy-start(bf16[256,3072]{1,0:T(8,128)(2,1)} %get-tuple-element.32) | copy-start | bytes 4718596
  129.1 29.0 %copy-start.10 = (f32[1,3072]{1,0:T(1,128)S(1)}, f32[1,3072]{1,0:T(1,128)}, u32[]{:S(2)}) copy-start(f32[1,3072]{1,0:T(1,128)} %param.7) | copy-start | bytes 36868
  153.5 13.2 %all-to-all-start.2 = ((f32[32,1,128]{2,1,0:T(1,128)}), f32[32,1,128]{2,1,0:T(1,128)S(1)}, u32[]{:S(2)}, u32[]{:S(2)}) async-start(f32[32,1,128]{2,1,0:T(1,128)} %broadcast_in_dim.4), calls=%async_computation.2 | async-start | bytes 32768 | tf_op jit(solution)/shard_map/norm/all_to_all | solution.py:58
  (19 other events, 258.0 us)

commit v5 on v4

--- a/solution.py
+++ b/solution.py
@@ -86,7 +86,7 @@
         grad_kernel,
         grid=(D // tile,),
         in_specs=[pl.BlockSpec((TOK, tile), lambda i: (0, i))] * 4 + [pl.BlockSpec((4 * TOK, WIDTH), lambda i: (0, 0))],
-        out_specs=pl.BlockSpec((2, 1, 1, NZ, OWN, WIDTH), lambda i: (0, lax.rem(i, 2), i // 2, 0, 0, 0)),
+        out_specs=pl.BlockSpec((2, 1, 1, NZ, OWN, WIDTH), lambda i: (0, i // 2, lax.rem(i, 2), 0, 0, 0)),
         scratch_shapes=[pltpu.VMEM((4 * TOK, tile), BF16)],
         out_shape=jax.ShapeDtypeStruct((2, 2, 2, NZ, OWN, WIDTH), BF16),
         compiler_params=pltpu.CompilerParams(vmem_limit_bytes=VMEM_LIMIT),
@@ -167,7 +167,7 @@
         grad = weight_grad((block_out, near, far, far_near), out_grad)
 
     with jax.named_scope("grad_scatter"):
-        got = lax.all_to_all(grad.reshape(8, NZ, OWN, WIDTH), ("xb", "xa", "yl"), 0, 0, tiled=True)
+        got = lax.all_to_all(grad.reshape(8, NZ, OWN, WIDTH), ("xb", "yl", "xa"), 0, 0, tiled=True)
 
     with jax.named_scope("weight_gather"):
         first_1, fourth_0 = lax.optimization_barrier((first_1, fourth_0, grad))[:2]

time: 181 us -> 178 us (0.983)
  waiting for transfers between devices: 52.6 us -> 48.1 us
    all_to_all x1, waiting for transfers between devices: 4.73 us -> 0.01 us  [body(): lax.all_to_all(grad.reshape(8, NZ, OWN, WIDTH), ('xb', 'yl', 'xa'), 0, 0,...]
    ppermute x26, waiting for transfers between devices: 43.4 us -> 45.3 us  [send(): return lax.ppermute(value, AXES, perm)]
where the time goes in v5:
time: 178 us; the launch traced here: 177 us
  starting transfers between devices  54.4 us (31%)
  waiting for transfers between devices  48.1 us (27%)
  blocking collectives  34 us (19%)
  Pallas kernels  18.2 us (10%)
  other arithmetic  15.1 us (8%)
  local copies, waits for them, and re-layouts  6.13 us (3%)
    ppermute x26, waiting for transfers between devices, send(): return lax.ppermute(value, AXES, perm)  45.3 us
    ppermute x26, starting transfers between devices, send(): return lax.ppermute(value, AXES, perm)  43.6 us
    all_to_all x1, blocking collectives, body(): owner_grad = add(*lax.all_to_all(total, ('z',), 0, 0, tiled=True))  22.2 us
    all_to_all x1, blocking collectives, gather(): return lax.all_to_all(copies, axes, 0, 0, tiled=True)  11.8 us
    pallas_call x1, Pallas kernels, stream_parts(): pl.pallas_call(stream_kernel, grid_spec=pltpu.PrefetchScalarGridSpec(num_...  10.9 us
    pallas_call x1, Pallas kernels, weight_grad(): pl.pallas_call(grad_kernel, grid=(D // tile,), in_specs=[pl.BlockSpec((TO...  7.39 us
    all_to_all x1, starting transfers between devices, gather(): return lax.all_to_all(copies, axes, 0, 0, tiled=True)  6.22 us
    all_to_all x1, starting transfers between devices, body(): lax.all_to_all(grad.reshape(8, NZ, OWN, WIDTH), ('xb', 'yl', 'xa'), 0, 0,...  4.6 us
  transfers between devices with their start and end apart: 28, of which 13 were waited for; matrix products, arithmetic and copies ran while one was open for 9% of the time, Pallas kernels for 10%

profile of v5, /device:TPU:1, one launch (start us, length us, event | category | flops | bytes accessed | tf_op | source)
XLA Modules:
  0.0 177.2 jit_solution(11262620422065996236)
XLA Ops:
  0.6 3.3 %collective-permute-start.3 = (bf16[256,3072]{1,0:T(8,128)(2,1)}, bf16[256,3072]{1,0:T(8,128)(2,1)S(1)}, u32[]{:S(2)}, u32[]{:S(2)}) collective-permute-start(bf16[256,3072]{1,0:T(8,128)(2,1)} %b0.1), channel_id=1, source_target_pairs={{0,1},{1,0},{2,3},{3,2},{4,5},{5,4},{6,7},{7,6},{8,9},{9,8},{10,11... | collective-permute-start | bytes 4718600 | tf_op jit(solution)/shard_map/start/ppermute | solution.py:53
  7.4 2.5 %collective-permute-start.1 = (bf16[48,768]{1,0:T(8,128)(2,1)S(1)}, bf16[48,768]{1,0:T(8,128)(2,1)S(1)}, u32[]{:S(2)}, u32[]{:S(2)}) collective-permute-start(bf16[48,768]{1,0:T(8,128)(2,1)S(1)} %convert_element_type.110), channel_id=1, source_target_pairs={{0,64},{1,65},{2,66},{3,67},{4,68},{5,69},{6,70},{7,71},{8,72},{9,... | collective-permute-start | bytes 221192 | tf_op jit(solution)/shard_map/start/ppermute | solution.py:53
  15.3 4.0 %collective-permute-start.8 = (bf16[4,48,768]{2,1,0:T(8,128)(2,1)S(1)}, bf16[4,48,768]{2,1,0:T(8,128)(2,1)S(1)}, u32[]{:S(2)}, u32[]{:S(2)}) collective-permute-start(bf16[4,48,768]{2,1,0:T(8,128)(2,1)S(1)} %pad_maximum_fusion.1.refs_0_), channel_id=1, source_target_pairs={{0,28},{1,29},{2,30},{3,31},{4,0},{5,1},{6,2},{7,3},{8,4},{9,5},{1... | collective-permute-start | bytes 884744 | tf_op jit(solution)/shard_map/weight_gather/ppermute | solution.py:53
  19.3 5.8 %collective-permute-done.5.refs_6_ = bf16[4,48,768]{2,1,0:T(8,128)(2,1)S(1)} collective-permute-done((bf16[4,48,768]{2,1,0:T(8,128)(2,1)S(1)}, bf16[4,48,768]{2,1,0:T(8,128)(2,1)S(1)}, u32[]{:S(2)}, u32[]{:S(2)}) %collective-permute-start.5) | collective-permute-done | bytes 294944 | tf_op jit(solution)/shard_map/weight_gather/ppermute | solution.py:53
  25.1 2.7 %collective-permute-start.9 = (bf16[4,48,768]{2,1,0:T(8,128)(2,1)S(1)}, bf16[4,48,768]{2,1,0:T(8,128)(2,1)}, u32[]{:S(2)}, u32[]{:S(2)}) collective-permute-start(bf16[4,48,768]{2,1,0:T(8,128)(2,1)S(1)} %collective-permute-done.8.refs_1_), channel_id=1, source_target_pairs={{0,28},{1,29},{2,30},{3,31},{4,0},{5,1},{6,2},{7,3},{8,4},{9,5},{1... | collective-permute-start | bytes 884744 | tf_op jit(solution)/shard_map/weight_gather/ppermute | solution.py:53
  27.8 5.0 %collective-permute-done.6.refs_5_ = bf16[4,48,768]{2,1,0:T(8,128)(2,1)S(1)} collective-permute-done((bf16[4,48,768]{2,1,0:T(8,128)(2,1)S(1)}, bf16[4,48,768]{2,1,0:T(8,128)(2,1)S(1)}, u32[]{:S(2)}, u32[]{:S(2)}) %collective-permute-start.6) | collective-permute-done | bytes 294944 | tf_op jit(solution)/shard_map/weight_gather/ppermute | solution.py:53
  32.9 2.7 %collective-permute-start.10 = (bf16[4,48,768]{2,1,0:T(8,128)(2,1)}, bf16[4,48,768]{2,1,0:T(8,128)(2,1)S(1)}, u32[]{:S(2)}, u32[]{:S(2)}) collective-permute-start(bf16[4,48,768]{2,1,0:T(8,128)(2,1)} %collective-permute-done.9.refs_2_), channel_id=1, source_target_pairs={{0,28},{1,29},{2,30},{3,31},{4,0},{5,1},{6,2},{7,3},{8,4},{9,5},{1... | collective-permute-start | bytes 884744 | tf_op jit(solution)/shard_map/weight_gather/ppermute | solution.py:53
  37.1 4.6 %collective-permute-done.4.b2 = bf16[256,3072]{1,0:T(8,128)(2,1)} collective-permute-done((bf16[256,3072]{1,0:T(8,128)(2,1)}, bf16[256,3072]{1,0:T(8,128)(2,1)}, u32[]{:S(2)}, u32[]{:S(2)}) %collective-permute-start.4) | collective-permute-done | bytes 1572896 | tf_op jit(solution)/shard_map/start/ppermute | solution.py:53
  43.9 3.1 %collective-permute-done.11.b3 = bf16[256,3072]{1,0:T(8,128)(2,1)S(1)} collective-permute-done((bf16[256,3072]{1,0:T(8,128)(2,1)}, bf16[256,3072]{1,0:T(8,128)(2,1)S(1)}, u32[]{:S(2)}, u32[]{:S(2)}) %collective-permute-start.11) | collective-permute-done | bytes 1572896 | tf_op jit(solution)/shard_map/weight_grad/ppermute | solution.py:53
  47.0 7.4 %weight_grad.1 = bf16[2,2,2,8,48,768]{5,4,3,2,1,0:T(8,128)(2,1)S(1)} custom-call(bf16[256,3072]{1,0:T(8,128)(2,1)S(1)} %copy-done.2, bf16[256,3072]{1,0:T(8,128)(2,1)S(1)} %collective-permute-done.3.b1, bf16[256,3072]{1,0:T(8,128)(2,1)} %collective-permute-done.4.b2, bf16[256,3072]{1,0:T(8,128)(2,1)S(1)} %collective-permute-done.11.b3, ...), custom_call_target="tpu_custom_call" | custom-call | flops 4831838208 | bytes 16777216 | tf_op jit(solution)/shard_map/weight_grad/weight_grad/pallas_call | solution.py:85
  54.4 2.2 %copy-done = bf16[2,2,2,8,48,768]{5,4,3,2,1,0:T(8,128)(2,1)} copy-done((bf16[2,2,2,8,48,768]{5,4,3,2,1,0:T(8,128)(2,1)}, bf16[2,2,2,8,48,768]{5,4,3,2,1,0:T(8,128)(2,1)S(1)}, u32[]{:S(2)}) %copy-start) | copy-done | bytes 4718616
  56.6 4.6 %all-to-all-start = ((bf16[8,8,48,768]{3,2,1,0:T(8,128)(2,1)}), bf16[8,8,48,768]{3,2,1,0:T(8,128)(2,1)}, u32[]{:S(2)}, u32[]{:S(2)}) async-start(bf16[8,8,48,768]{3,2,1,0:T(8,128)(2,1)} %bitcast.25), calls=%async_computation | async-start | bytes 9437184 | tf_op jit(solution)/shard_map/grad_scatter/all_to_all | solution.py:170
  61.3 3.5 %collective-permute-start.14 = (bf16[4,48,768]{2,1,0:T(8,128)(2,1)S(1)}, bf16[4,48,768]{2,1,0:T(8,128)(2,1)S(1)}, u32[]{:S(2)}, u32[]{:S(2)}) collective-permute-start(bf16[4,48,768]{2,1,0:T(8,128)(2,1)S(1)} %collective-permute-done.12.refs_9_), channel_id=1, source_target_pairs={{0,28},{1,29},{2,30},{3,31},{4,0},{5,1},{6,2},{7,3},{8,4},{9,5},{1... | collective-permute-start | bytes 884744 | tf_op jit(solution)/shard_map/weight_gather/ppermute | solution.py:53
  64.9 2.7 %collective-permute-start.16 = (bf16[2,48,768]{2,1,0:T(8,128)(2,1)S(1)}, bf16[2,48,768]{2,1,0:T(8,128)(2,1)S(1)}, u32[]{:S(2)}, u32[]{:S(2)}) collective-permute-start(bf16[2,48,768]{2,1,0:T(8,128)(2,1)S(1)} %slice.16), channel_id=1, source_target_pairs={{0,28},{1,29},{2,30},{3,31},{4,0},{5,1},{6,2},{7,3},{8,4},{9,5},{1... | collective-permute-start | bytes 442376 | tf_op jit(solution)/shard_map/weight_gather/ppermute | solution.py:53
  67.6 3.7 %collective-permute-done.13.refs_15_ = bf16[4,48,768]{2,1,0:T(8,128)(2,1)S(1)} collective-permute-done((bf16[4,48,768]{2,1,0:T(8,128)(2,1)S(1)}, bf16[4,48,768]{2,1,0:T(8,128)(2,1)S(1)}, u32[]{:S(2)}, u32[]{:S(2)}) %collective-permute-start.13) | collective-permute-done | bytes 294944 | tf_op jit(solution)/shard_map/weight_gather/ppermute | solution.py:53
  71.4 3.2 %collective-permute-done.15.refs_7_ = bf16[2,48,768]{2,1,0:T(8,128)(2,1)S(1)} collective-permute-done((bf16[2,48,768]{2,1,0:T(8,128)(2,1)S(1)}, bf16[2,48,768]{2,1,0:T(8,128)(2,1)S(1)}, u32[]{:S(2)}, u32[]{:S(2)}) %collective-permute-start.15) | collective-permute-done | bytes 147488 | tf_op jit(solution)/shard_map/weight_gather/ppermute | solution.py:53
  77.3 6.0 %collective-permute-done.19.refs_14_ = bf16[4,48,768]{2,1,0:T(8,128)(2,1)S(1)} collective-permute-done((bf16[4,48,768]{2,1,0:T(8,128)(2,1)S(1)}, bf16[4,48,768]{2,1,0:T(8,128)(2,1)S(1)}, u32[]{:S(2)}, u32[]{:S(2)}) %collective-permute-start.19) | collective-permute-done | bytes 294944 | tf_op jit(solution)/shard_map/weight_gather/ppermute | solution.py:53
  83.8 2.2 %collective-permute-start.18 = (bf16[4,48,768]{2,1,0:T(8,128)(2,1)S(1)}, bf16[4,48,768]{2,1,0:T(8,128)(2,1)S(1)}, u32[]{:S(2)}, u32[]{:S(2)}) collective-permute-start(bf16[4,48,768]{2,1,0:T(8,128)(2,1)S(1)} %collective-permute-done.17.refs_11_), channel_id=1, source_target_pairs={{0,28},{1,29},{2,30},{3,31},{4,0},{5,1},{6,2},{7,3},{8,4},{9,5},{1... | collective-permute-start | bytes 884744 | tf_op jit(solution)/shard_map/weight_gather/ppermute | solution.py:53
  86.0 5.1 %collective-permute-done.20.refs_13_ = bf16[4,48,768]{2,1,0:T(8,128)(2,1)S(1)} collective-permute-done((bf16[4,48,768]{2,1,0:T(8,128)(2,1)S(1)}, bf16[4,48,768]{2,1,0:T(8,128)(2,1)S(1)}, u32[]{:S(2)}, u32[]{:S(2)}) %collective-permute-start.20) | collective-permute-done | bytes 294944 | tf_op jit(solution)/shard_map/weight_gather/ppermute | solution.py:53
  91.3 2.7 %collective-permute-start.22 = (bf16[2,48,768]{2,1,0:T(8,128)(2,1)S(1)}, bf16[2,48,768]{2,1,0:T(8,128)(2,1)S(1)}, u32[]{:S(2)}, u32[]{:S(2)}) collective-permute-start(bf16[2,48,768]{2,1,0:T(8,128)(2,1)S(1)} %slice.21), channel_id=1, source_target_pairs={{0,28},{1,29},{2,30},{3,31},{4,0},{5,1},{6,2},{7,3},{8,4},{9,5},{1... | collective-permute-start | bytes 442376 | tf_op jit(solution)/shard_map/weight_gather/ppermute | solution.py:53
  94.6 2.3 %collective-permute-done.21.refs_16_ = bf16[2,48,768]{2,1,0:T(8,128)(2,1)S(1)} collective-permute-done((bf16[2,48,768]{2,1,0:T(8,128)(2,1)S(1)}, bf16[2,48,768]{2,1,0:T(8,128)(2,1)S(1)}, u32[]{:S(2)}, u32[]{:S(2)}) %collective-permute-start.21) | collective-permute-done | bytes 147488 | tf_op jit(solution)/shard_map/weight_gather/ppermute | solution.py:53
  98.1 10.9 %stream_parts.1 = (bf16[256,3072]{1,0:T(8,128)(2,1)}, bf16[256,3072]{1,0:T(8,128)(2,1)}, bf16[256,3072]{1,0:T(8,128)(2,1)}, bf16[256,3072]{1,0:T(8,128)(2,1)}) custom-call(s32[3]{0:T(128)} %pad_add_fusion.here, bf16[1024,768]{1,0:T(8,128)(2,1)} %copy-done.1, bf16[4,48,768]{2,1,0:T(8,128)(2,1)} %copy-done.5, bf16[4,48,768]{2,1,0:T(8,128)(2,1)} %copy-done.12, ...), custom_call_target="tpu_custom_call" | custom-call | flops 4831838208 | bytes 16777216 | tf_op jit(solution)/shard_map/stream/stream_parts/pallas_call | solution.py:123
  109.0 3.7 %collective-permute-start.23 = (bf16[256,3072]{1,0:T(8,128)(2,1)}, bf16[256,3072]{1,0:T(8,128)(2,1)S(1)}, u32[]{:S(2)}, u32[]{:S(2)}) collective-permute-start(bf16[256,3072]{1,0:T(8,128)(2,1)} %get-tuple-element.34), channel_id=1, source_target_pairs={{0,1},{1,0},{2,3},{3,2},{4,5},{5,4},{6,7},{7,6},{8,9},{9,8},{10,11... | collective-permute-start | bytes 4718600 | tf_op jit(solution)/shard_map/stream/ppermute | solution.py:53
  112.8 3.1 %collective-permute-done.23 = bf16[256,3072]{1,0:T(8,128)(2,1)S(1)} collective-permute-done((bf16[256,3072]{1,0:T(8,128)(2,1)}, bf16[256,3072]{1,0:T(8,128)(2,1)S(1)}, u32[]{:S(2)}, u32[]{:S(2)}) %collective-permute-start.23) | collective-permute-done | bytes 1572896 | tf_op jit(solution)/shard_map/stream/ppermute | solution.py:53
  115.9 3.1 %add_convert_fusion = bf16[256,3072]{1,0:T(8,128)(2,1)} fusion(bf16[256,3072]{1,0:T(8,128)(2,1)S(1)} %collective-permute-done.23, bf16[256,3072]{1,0:T(8,128)(2,1)} %get-tuple-element.33), kind=kLoop, calls=%fused_computation.2 | loop fusion | flops 3145728 | bytes 4718592 | tf_op jit(solution)/shard_map/stream/convert_element_type | solution.py:187
  119.1 2.6 %collective-permute-start.25 = (bf16[256,3072]{1,0:T(8,128)(2,1)}, bf16[256,3072]{1,0:T(8,128)(2,1)}, u32[]{:S(2)}, u32[]{:S(2)}) collective-permute-start(bf16[256,3072]{1,0:T(8,128)(2,1)} %add_convert_fusion), channel_id=1, source_target_pairs={{0,2},{1,3},{2,0},{3,1},{4,6},{5,7},{6,4},{7,5},{8,10},{9,11},{10,... | collective-permute-start | bytes 4718600 | tf_op jit(solution)/shard_map/stream/ppermute | solution.py:53
  121.7 2.9 %fusion.1 = bf16[8,48,768]{2,1,0:T(8,128)(2,1)S(1)} fusion(bf16[8,8,48,768]{3,2,1,0:T(8,128)(2,1)} %all-to-all-done), kind=kLoop, calls=%fused_computation.6 | loop fusion | flops 4718592 | bytes 5308416 | tf_op jit(solution)/shard_map/grad_scatter/convert_element_type | solution.py:192
  124.6 22.2 %all_to_all.20 = bf16[8,48,768]{2,1,0:T(8,128)(2,1)S(1)} all-to-all(bf16[8,48,768]{2,1,0:T(8,128)(2,1)S(1)} %fusion.1), channel_id=1, replica_groups=mesh['yl'=2,'xa'=2,'xb'=2,'z'=8,'yh'=2,'c'=2] {'z'}, dimensions={0} | all-to-all | bytes 1179648 | tf_op jit(solution)/shard_map/grad_scatter/all_to_all | solution.py:193
  148.6 6.2 %all-to-all-start.2 = ((f32[32,1,128]{2,1,0:T(1,128)}), f32[32,1,128]{2,1,0:T(1,128)S(1)}, u32[]{:S(2)}, u32[]{:S(2)}) async-start(f32[32,1,128]{2,1,0:T(1,128)} %broadcast_in_dim.4), calls=%async_computation.2 | async-start | bytes 32768 | tf_op jit(solution)/shard_map/norm/all_to_all | solution.py:58
  156.5 4.1 %multiply_convert_fusion = (bf16[256,3072]{1,0:T(8,128)(2,1)}, bf16[256,3072]{1,0:T(8,128)(2,1)}) fusion(bf16[256,3072]{1,0:T(8,128)(2,1)} %collective-permute-done.25, bf16[256,3072]{1,0:T(8,128)(2,1)S(1)} %collective-permute-done.24, bf16[256,3072]{1,0:T(8,128)(2,1)S(1)} %copy-done.3, f32[3072]{0:T(1024)S(1)} %bitcast.30), kind=kLoop, calls=%fused_computation | loop fusion | flops 6291456 | bytes 7876608 | tf_op jit(solution)/shard_map/norm/convert_element_type | solution.py:200
  160.5 2.9 %all-to-all-done.2 = f32[32,1,128]{2,1,0:T(1,128)S(1)} async-done(((f32[32,1,128]{2,1,0:T(1,128)}), f32[32,1,128]{2,1,0:T(1,128)S(1)}, u32[]{:S(2)}, u32[]{:S(2)}) %all-to-all-start.2) | async-done | bytes 16416 | tf_op jit(solution)/shard_map/norm/all_to_all | solution.py:58
  163.5 11.8 %all_to_all.21 = f32[8,1,128]{2,1,0:T(1,128)S(1)} all-to-all(f32[8,1,128]{2,1,0:T(1,128)S(1)} %broadcast_in_dim.10), channel_id=1, replica_groups=mesh['yl'=2,'xa'=2,'xb'=2,'z'=8,'yh'=2,'c'=2] {'yl','yh','c'}, dimensions={0} | all-to-all | bytes 8192 | tf_op jit(solution)/shard_map/norm/all_to_all | solution.py:58
  (93 shorter events, 23.4 us)
Async XLA Ops:
  0.6 13.0 %collective-permute-start.3 = (bf16[256,3072]{1,0:T(8,128)(2,1)}, bf16[256,3072]{1,0:T(8,128)(2,1)S(1)}, u32[]{:S(2)}, u32[]{:S(2)}) collective-permute-start(bf16[256,3072]{1,0:T(8,128)(2,1)} %b0.1), channel_id=1, source_target_pairs={{0,1},{1,0},{2,3},{3,2},{4,5},{5,4},{6,7},{7,6},{8,9},{9,8},{10,11... | collective-permute-start | bytes 4718600 | tf_op jit(solution)/shard_map/start/ppermute | solution.py:53
  4.0 37.8 %collective-permute-start.4 = (bf16[256,3072]{1,0:T(8,128)(2,1)}, bf16[256,3072]{1,0:T(8,128)(2,1)}, u32[]{:S(2)}, u32[]{:S(2)}) collective-permute-start(bf16[256,3072]{1,0:T(8,128)(2,1)} %b0.1), channel_id=1, source_target_pairs={{0,2},{1,3},{2,0},{3,1},{4,6},{5,7},{6,4},{7,5},{8,10},{9,11},{10,... | collective-permute-start | bytes 4718600 | tf_op jit(solution)/shard_map/start/ppermute | solution.py:53
  6.1 5.8 %collective-permute-start.2 = (bf16[48,768]{1,0:T(8,128)(2,1)S(1)}, bf16[48,768]{1,0:T(8,128)(2,1)S(1)}, u32[]{:S(2)}, u32[]{:S(2)}) collective-permute-start(bf16[48,768]{1,0:T(8,128)(2,1)S(1)} %convert_element_type.110), channel_id=1, source_target_pairs={{0,32},{1,33},{2,34},{3,35},{4,36},{5,37},{6,38},{7,39},{8,40},{9,... | collective-permute-start | bytes 221192 | tf_op jit(solution)/shard_map/start/ppermute | solution.py:53
  7.4 6.2 %collective-permute-start.1 = (bf16[48,768]{1,0:T(8,128)(2,1)S(1)}, bf16[48,768]{1,0:T(8,128)(2,1)S(1)}, u32[]{:S(2)}, u32[]{:S(2)}) collective-permute-start(bf16[48,768]{1,0:T(8,128)(2,1)S(1)} %convert_element_type.110), channel_id=1, source_target_pairs={{0,64},{1,65},{2,66},{3,67},{4,68},{5,69},{6,70},{7,71},{8,72},{9,... | collective-permute-start | bytes 221192 | tf_op jit(solution)/shard_map/start/ppermute | solution.py:53
  9.8 3.7 %collective-permute-start = (bf16[48,768]{1,0:T(8,128)(2,1)S(1)}, bf16[48,768]{1,0:T(8,128)(2,1)S(1)}, u32[]{:S(2)}, u32[]{:S(2)}) collective-permute-start(bf16[48,768]{1,0:T(8,128)(2,1)S(1)} %convert_element_type.110), channel_id=1, source_target_pairs={{0,96},{1,97},{2,98},{3,99},{4,100},{5,101},{6,102},{7,103},{8,104... | collective-permute-start | bytes 221192 | tf_op jit(solution)/shard_map/start/ppermute | solution.py:53
  13.6 30.2 %copy-start.5 = (bf16[4,48,768]{2,1,0:T(8,128)(2,1)}, bf16[4,48,768]{2,1,0:T(8,128)(2,1)S(1)}, u32[]{:S(2)}) copy-start(bf16[4,48,768]{2,1,0:T(8,128)(2,1)S(1)} %pad_maximum_fusion.1.refs_0_) | copy-start | bytes 884740
  13.6 11.5 %collective-permute-start.5 = (bf16[4,48,768]{2,1,0:T(8,128)(2,1)S(1)}, bf16[4,48,768]{2,1,0:T(8,128)(2,1)S(1)}, u32[]{:S(2)}, u32[]{:S(2)}) collective-permute-start(bf16[4,48,768]{2,1,0:T(8,128)(2,1)S(1)} %pad_maximum_fusion.1.refs_0_), channel_id=1, source_target_pairs={{0,4},{1,5},{2,6},{3,7},{4,8},{5,9},{6,10},{7,11},{8,12},{9,13},{1... | collective-permute-start | bytes 884744 | tf_op jit(solution)/shard_map/weight_gather/ppermute | solution.py:53
  15.3 9.8 %collective-permute-start.8 = (bf16[4,48,768]{2,1,0:T(8,128)(2,1)S(1)}, bf16[4,48,768]{2,1,0:T(8,128)(2,1)S(1)}, u32[]{:S(2)}, u32[]{:S(2)}) collective-permute-start(bf16[4,48,768]{2,1,0:T(8,128)(2,1)S(1)} %pad_maximum_fusion.1.refs_0_), channel_id=1, source_target_pairs={{0,28},{1,29},{2,30},{3,31},{4,0},{5,1},{6,2},{7,3},{8,4},{9,5},{1... | collective-permute-start | bytes 884744 | tf_op jit(solution)/shard_map/weight_gather/ppermute | solution.py:53
  25.1 7.7 %collective-permute-start.6 = (bf16[4,48,768]{2,1,0:T(8,128)(2,1)S(1)}, bf16[4,48,768]{2,1,0:T(8,128)(2,1)S(1)}, u32[]{:S(2)}, u32[]{:S(2)}) collective-permute-start(bf16[4,48,768]{2,1,0:T(8,128)(2,1)S(1)} %collective-permute-done.5.refs_6_), channel_id=1, source_target_pairs={{0,4},{1,5},{2,6},{3,7},{4,8},{5,9},{6,10},{7,11},{8,12},{9,13},{1... | collective-permute-start | bytes 884744 | tf_op jit(solution)/shard_map/weight_gather/ppermute | solution.py:53
  25.1 7.7 %collective-permute-start.9 = (bf16[4,48,768]{2,1,0:T(8,128)(2,1)S(1)}, bf16[4,48,768]{2,1,0:T(8,128)(2,1)}, u32[]{:S(2)}, u32[]{:S(2)}) collective-permute-start(bf16[4,48,768]{2,1,0:T(8,128)(2,1)S(1)} %collective-permute-done.8.refs_1_), channel_id=1, source_target_pairs={{0,28},{1,29},{2,30},{3,31},{4,0},{5,1},{6,2},{7,3},{8,4},{9,5},{1... | collective-permute-start | bytes 884744 | tf_op jit(solution)/shard_map/weight_gather/ppermute | solution.py:53
  32.8 8.9 %collective-permute-start.7 = (bf16[4,48,768]{2,1,0:T(8,128)(2,1)S(1)}, bf16[4,48,768]{2,1,0:T(8,128)(2,1)S(1)}, u32[]{:S(2)}, u32[]{:S(2)}) collective-permute-start(bf16[4,48,768]{2,1,0:T(8,128)(2,1)S(1)} %collective-permute-done.6.refs_5_), channel_id=1, source_target_pairs={{0,4},{1,5},{2,6},{3,7},{4,8},{5,9},{6,10},{7,11},{8,12},{9,13},{1... | collective-permute-start | bytes 884744 | tf_op jit(solution)/shard_map/weight_gather/ppermute | solution.py:53
  32.9 8.9 %collective-permute-start.10 = (bf16[4,48,768]{2,1,0:T(8,128)(2,1)}, bf16[4,48,768]{2,1,0:T(8,128)(2,1)S(1)}, u32[]{:S(2)}, u32[]{:S(2)}) collective-permute-start(bf16[4,48,768]{2,1,0:T(8,128)(2,1)} %collective-permute-done.9.refs_2_), channel_id=1, source_target_pairs={{0,28},{1,29},{2,30},{3,31},{4,0},{5,1},{6,2},{7,3},{8,4},{9,5},{1... | collective-permute-start | bytes 884744 | tf_op jit(solution)/shard_map/weight_gather/ppermute | solution.py:53
  41.8 5.3 %collective-permute-start.11 = (bf16[256,3072]{1,0:T(8,128)(2,1)}, bf16[256,3072]{1,0:T(8,128)(2,1)S(1)}, u32[]{:S(2)}, u32[]{:S(2)}) collective-permute-start(bf16[256,3072]{1,0:T(8,128)(2,1)} %collective-permute-done.4.b2), channel_id=1, source_target_pairs={{0,1},{1,0},{2,3},{3,2},{4,5},{5,4},{6,7},{7,6},{8,9},{9,8},{10,11... | collective-permute-start | bytes 4718600 | tf_op jit(solution)/shard_map/weight_grad/ppermute | solution.py:53
  43.8 17.4 %collective-permute-start.12 = (bf16[4,48,768]{2,1,0:T(8,128)(2,1)S(1)}, bf16[4,48,768]{2,1,0:T(8,128)(2,1)S(1)}, u32[]{:S(2)}, u32[]{:S(2)}) collective-permute-start(bf16[4,48,768]{2,1,0:T(8,128)(2,1)S(1)} %pad_maximum_fusion.1.refs_0_), channel_id=1, source_target_pairs={{0,128},{1,129},{2,130},{3,131},{4,132},{5,133},{6,134},{7,135},{8... | collective-permute-start | bytes 884744 | tf_op jit(solution)/shard_map/start/ppermute | solution.py:53
  56.6 65.1 %all-to-all-start = ((bf16[8,8,48,768]{3,2,1,0:T(8,128)(2,1)}), bf16[8,8,48,768]{3,2,1,0:T(8,128)(2,1)}, u32[]{:S(2)}, u32[]{:S(2)}) async-start(bf16[8,8,48,768]{3,2,1,0:T(8,128)(2,1)} %bitcast.25), calls=%async_computation | async-start | bytes 9437184 | tf_op jit(solution)/shard_map/grad_scatter/all_to_all | solution.py:170
  61.2 35.6 %copy-start.14 = (bf16[4,48,768]{2,1,0:T(8,128)(2,1)}, bf16[4,48,768]{2,1,0:T(8,128)(2,1)S(1)}, u32[]{:S(2)}) copy-start(bf16[4,48,768]{2,1,0:T(8,128)(2,1)S(1)} %collective-permute-done.12.refs_9_) | copy-start | bytes 884740
  61.2 10.1 %collective-permute-start.13 = (bf16[4,48,768]{2,1,0:T(8,128)(2,1)S(1)}, bf16[4,48,768]{2,1,0:T(8,128)(2,1)S(1)}, u32[]{:S(2)}, u32[]{:S(2)}) collective-permute-start(bf16[4,48,768]{2,1,0:T(8,128)(2,1)S(1)} %collective-permute-done.12.refs_9_), channel_id=1, source_target_pairs={{0,4},{1,5},{2,6},{3,7},{4,8},{5,9},{6,10},{7,11},{8,12},{9,13},{1... | collective-permute-start | bytes 884744 | tf_op jit(solution)/shard_map/weight_gather/ppermute | solution.py:53
  61.3 10.1 %collective-permute-start.14 = (bf16[4,48,768]{2,1,0:T(8,128)(2,1)S(1)}, bf16[4,48,768]{2,1,0:T(8,128)(2,1)S(1)}, u32[]{:S(2)}, u32[]{:S(2)}) collective-permute-start(bf16[4,48,768]{2,1,0:T(8,128)(2,1)S(1)} %collective-permute-done.12.refs_9_), channel_id=1, source_target_pairs={{0,28},{1,29},{2,30},{3,31},{4,0},{5,1},{6,2},{7,3},{8,4},{9,5},{1... | collective-permute-start | bytes 884744 | tf_op jit(solution)/shard_map/weight_gather/ppermute | solution.py:53
  64.8 9.7 %collective-permute-start.15 = (bf16[2,48,768]{2,1,0:T(8,128)(2,1)S(1)}, bf16[2,48,768]{2,1,0:T(8,128)(2,1)S(1)}, u32[]{:S(2)}, u32[]{:S(2)}) collective-permute-start(bf16[2,48,768]{2,1,0:T(8,128)(2,1)S(1)} %slice.15), channel_id=1, source_target_pairs={{0,4},{1,5},{2,6},{3,7},{4,8},{5,9},{6,10},{7,11},{8,12},{9,13},{1... | collective-permute-start | bytes 442376 | tf_op jit(solution)/shard_map/weight_gather/ppermute | solution.py:53
  64.9 9.6 %collective-permute-start.16 = (bf16[2,48,768]{2,1,0:T(8,128)(2,1)S(1)}, bf16[2,48,768]{2,1,0:T(8,128)(2,1)S(1)}, u32[]{:S(2)}, u32[]{:S(2)}) collective-permute-start(bf16[2,48,768]{2,1,0:T(8,128)(2,1)S(1)} %slice.16), channel_id=1, source_target_pairs={{0,28},{1,29},{2,30},{3,31},{4,0},{5,1},{6,2},{7,3},{8,4},{9,5},{1... | collective-permute-start | bytes 442376 | tf_op jit(solution)/shard_map/weight_gather/ppermute | solution.py:53
  74.5 8.8 %collective-permute-start.19 = (bf16[4,48,768]{2,1,0:T(8,128)(2,1)S(1)}, bf16[4,48,768]{2,1,0:T(8,128)(2,1)S(1)}, u32[]{:S(2)}, u32[]{:S(2)}) collective-permute-start(bf16[4,48,768]{2,1,0:T(8,128)(2,1)S(1)} %collective-permute-done.13.refs_15_), channel_id=1, source_target_pairs={{0,4},{1,5},{2,6},{3,7},{4,8},{5,9},{6,10},{7,11},{8,12},{9,13},{1... | collective-permute-start | bytes 884744 | tf_op jit(solution)/shard_map/weight_gather/ppermute | solution.py:53
  76.3 7.5 %collective-permute-start.17 = (bf16[4,48,768]{2,1,0:T(8,128)(2,1)S(1)}, bf16[4,48,768]{2,1,0:T(8,128)(2,1)S(1)}, u32[]{:S(2)}, u32[]{:S(2)}) collective-permute-start(bf16[4,48,768]{2,1,0:T(8,128)(2,1)S(1)} %collective-permute-done.14.refs_10_), channel_id=1, source_target_pairs={{0,28},{1,29},{2,30},{3,31},{4,0},{5,1},{6,2},{7,3},{8,4},{9,5},{1... | collective-permute-start | bytes 884744 | tf_op jit(solution)/shard_map/weight_gather/ppermute | solution.py:53
  83.3 7.8 %collective-permute-start.20 = (bf16[4,48,768]{2,1,0:T(8,128)(2,1)S(1)}, bf16[4,48,768]{2,1,0:T(8,128)(2,1)S(1)}, u32[]{:S(2)}, u32[]{:S(2)}) collective-permute-start(bf16[4,48,768]{2,1,0:T(8,128)(2,1)S(1)} %collective-permute-done.19.refs_14_), channel_id=1, source_target_pairs={{0,4},{1,5},{2,6},{3,7},{4,8},{5,9},{6,10},{7,11},{8,12},{9,13},{1... | collective-permute-start | bytes 884744 | tf_op jit(solution)/shard_map/weight_gather/ppermute | solution.py:53
  83.8 7.4 %collective-permute-start.18 = (bf16[4,48,768]{2,1,0:T(8,128)(2,1)S(1)}, bf16[4,48,768]{2,1,0:T(8,128)(2,1)S(1)}, u32[]{:S(2)}, u32[]{:S(2)}) collective-permute-start(bf16[4,48,768]{2,1,0:T(8,128)(2,1)S(1)} %collective-permute-done.17.refs_11_), channel_id=1, source_target_pairs={{0,28},{1,29},{2,30},{3,31},{4,0},{5,1},{6,2},{7,3},{8,4},{9,5},{1... | collective-permute-start | bytes 884744 | tf_op jit(solution)/shard_map/weight_gather/ppermute | solution.py:53
  91.2 5.7 %collective-permute-start.21 = (bf16[2,48,768]{2,1,0:T(8,128)(2,1)S(1)}, bf16[2,48,768]{2,1,0:T(8,128)(2,1)S(1)}, u32[]{:S(2)}, u32[]{:S(2)}) collective-permute-start(bf16[2,48,768]{2,1,0:T(8,128)(2,1)S(1)} %slice.20), channel_id=1, source_target_pairs={{0,4},{1,5},{2,6},{3,7},{4,8},{5,9},{6,10},{7,11},{8,12},{9,13},{1... | collective-permute-start | bytes 442376 | tf_op jit(solution)/shard_map/weight_gather/ppermute | solution.py:53
  91.3 5.6 %collective-permute-start.22 = (bf16[2,48,768]{2,1,0:T(8,128)(2,1)S(1)}, bf16[2,48,768]{2,1,0:T(8,128)(2,1)S(1)}, u32[]{:S(2)}, u32[]{:S(2)}) collective-permute-start(bf16[2,48,768]{2,1,0:T(8,128)(2,1)S(1)} %slice.21), channel_id=1, source_target_pairs={{0,28},{1,29},{2,30},{3,31},{4,0},{5,1},{6,2},{7,3},{8,4},{9,5},{1... | collective-permute-start | bytes 442376 | tf_op jit(solution)/shard_map/weight_gather/ppermute | solution.py:53
  109.0 6.9 %collective-permute-start.23 = (bf16[256,3072]{1,0:T(8,128)(2,1)}, bf16[256,3072]{1,0:T(8,128)(2,1)S(1)}, u32[]{:S(2)}, u32[]{:S(2)}) collective-permute-start(bf16[256,3072]{1,0:T(8,128)(2,1)} %get-tuple-element.34), channel_id=1, source_target_pairs={{0,1},{1,0},{2,3},{3,2},{4,5},{5,4},{6,7},{7,6},{8,9},{9,8},{10,11... | collective-permute-start | bytes 4718600 | tf_op jit(solution)/shard_map/stream/ppermute | solution.py:53
  112.7 6.4 %collective-permute-start.24 = (bf16[256,3072]{1,0:T(8,128)(2,1)}, bf16[256,3072]{1,0:T(8,128)(2,1)S(1)}, u32[]{:S(2)}, u32[]{:S(2)}) collective-permute-start(bf16[256,3072]{1,0:T(8,128)(2,1)} %get-tuple-element.35), channel_id=1, source_target_pairs={{0,1},{1,0},{2,3},{3,2},{4,5},{5,4},{6,7},{7,6},{8,9},{9,8},{10,11... | collective-permute-start | bytes 4718600 | tf_op jit(solution)/shard_map/stream/ppermute | solution.py:53
  119.1 37.4 %collective-permute-start.25 = (bf16[256,3072]{1,0:T(8,128)(2,1)}, bf16[256,3072]{1,0:T(8,128)(2,1)}, u32[]{:S(2)}, u32[]{:S(2)}) collective-permute-start(bf16[256,3072]{1,0:T(8,128)(2,1)} %add_convert_fusion), channel_id=1, source_target_pairs={{0,2},{1,3},{2,0},{3,1},{4,6},{5,7},{6,4},{7,5},{8,10},{9,11},{10,... | collective-permute-start | bytes 4718600 | tf_op jit(solution)/shard_map/stream/ppermute | solution.py:53
  124.6 31.9 %copy-start.3 = (bf16[256,3072]{1,0:T(8,128)(2,1)S(1)}, bf16[256,3072]{1,0:T(8,128)(2,1)}, u32[]{:S(2)}) copy-start(bf16[256,3072]{1,0:T(8,128)(2,1)} %get-tuple-element.32) | copy-start | bytes 4718596
  124.6 31.9 %copy-start.10 = (f32[1,3072]{1,0:T(1,128)S(1)}, f32[1,3072]{1,0:T(1,128)}, u32[]{:S(2)}) copy-start(f32[1,3072]{1,0:T(1,128)} %param.7) | copy-start | bytes 36868
  148.6 14.8 %all-to-all-start.2 = ((f32[32,1,128]{2,1,0:T(1,128)}), f32[32,1,128]{2,1,0:T(1,128)S(1)}, u32[]{:S(2)}, u32[]{:S(2)}) async-start(f32[32,1,128]{2,1,0:T(1,128)} %broadcast_in_dim.4), calls=%async_computation.2 | async-start | bytes 32768 | tf_op jit(solution)/shard_map/norm/all_to_all | solution.py:58
  (19 other events, 257.4 us)

commit v6 on v5

--- a/solution.py
+++ b/solution.py
@@ -194,13 +194,13 @@
 
     with jax.named_scope("norm"):
         local = jnp.sum(owner_grad * owner_grad)
-        local = gather(jnp.full((1, 128), local, F32), ("xa", "xb", "z"), 32)
+        local = gather(jnp.full((1, 128), local, F32), ("yl", "xa", "xb", "yh", "c"), 32)
         stream = add(p0, r1, q2)
         stream_out = stream.astype(BF16)
         branch_out = (gate * stream).astype(BF16)
         local, stream_out, branch_out = lax.optimization_barrier((local, stream_out, branch_out))
         local = jnp.sum(local.reshape(32, 128), axis=0, keepdims=True)
-        norm_sq = jnp.sum(gather(local, ("yl", "yh", "c"), 8), axis=0)[:1, :1]
+        norm_sq = jnp.sum(gather(local, ("z",), 8), axis=0)[:1, :1]
 
     factor = jnp.minimum(1.0, max_norm / (jnp.sqrt(norm_sq) + 1e-06))
     clipped = factor * owner_grad

time: 178 us -> 177 us (level)
  starting transfers between devices: 54.4 us -> 58.7 us
  blocking collectives: 34 us -> 31.1 us
    all_to_all x1, starting transfers between devices: 6.22 us -> 10.5 us  [gather(): return lax.all_to_all(copies, axes, 0, 0, tiled=True)]
    all_to_all x1, blocking collectives: 11.8 us -> 8.89 us  [gather(): return lax.all_to_all(copies, axes, 0, 0, tiled=True)]
  transfers between devices with their start and end apart: 28 -> 28, of which waited for: 13 -> 12; matrix products, arithmetic and copies ran while one was open for 9% -> 9% of each run, Pallas kernels for 10% -> 10%
where the time goes in v6:
time: 177 us
  starting transfers between devices  58.7 us (33%)
  waiting for transfers between devices  46.4 us (26%)
  blocking collectives  31.1 us (18%)
  Pallas kernels  18.2 us (10%)
  other arithmetic  15.1 us (9%)
  local copies, waits for them, and re-layouts  6.13 us (3%)
    ppermute x26, waiting for transfers between devices, send(): return lax.ppermute(value, AXES, perm)  43.7 us
    ppermute x26, starting transfers between devices, send(): return lax.ppermute(value, AXES, perm)  43.6 us
    all_to_all x1, blocking collectives, body(): owner_grad = add(*lax.all_to_all(total, ('z',), 0, 0, tiled=True))  22.2 us
    pallas_call x1, Pallas kernels, stream_parts(): pl.pallas_call(stream_kernel, grid_spec=pltpu.PrefetchScalarGridSpec(num_...  10.9 us
    all_to_all x1, starting transfers between devices, gather(): return lax.all_to_all(copies, axes, 0, 0, tiled=True)  10.5 us
    all_to_all x1, blocking collectives, gather(): return lax.all_to_all(copies, axes, 0, 0, tiled=True)  8.89 us
    pallas_call x1, Pallas kernels, weight_grad(): pl.pallas_call(grad_kernel, grid=(D // tile,), in_specs=[pl.BlockSpec((TO...  7.39 us
    all_to_all x1, starting transfers between devices, body(): lax.all_to_all(grad.reshape(8, NZ, OWN, WIDTH), ('xb', 'yl', 'xa'), 0, 0,...  4.6 us
  transfers between devices with their start and end apart: 28, of which 12 were waited for; matrix products, arithmetic and copies ran while one was open for 9% of the time, Pallas kernels for 10%

profile of v6, /device:TPU:1, one launch (start us, length us, event | category | flops | bytes accessed | tf_op | source)
XLA Modules:
  0.0 176.8 jit_solution(17883444942444503105)
XLA Ops:
  0.6 3.3 %collective-permute-start.3 = (bf16[256,3072]{1,0:T(8,128)(2,1)}, bf16[256,3072]{1,0:T(8,128)(2,1)S(1)}, u32[]{:S(2)}, u32[]{:S(2)}) collective-permute-start(bf16[256,3072]{1,0:T(8,128)(2,1)} %b0.1), channel_id=1, source_target_pairs={{0,1},{1,0},{2,3},{3,2},{4,5},{5,4},{6,7},{7,6},{8,9},{9,8},{10,11... | collective-permute-start | bytes 4718600 | tf_op jit(solution)/shard_map/start/ppermute | solution.py:53
  7.4 2.5 %collective-permute-start.1 = (bf16[48,768]{1,0:T(8,128)(2,1)S(1)}, bf16[48,768]{1,0:T(8,128)(2,1)S(1)}, u32[]{:S(2)}, u32[]{:S(2)}) collective-permute-start(bf16[48,768]{1,0:T(8,128)(2,1)S(1)} %convert_element_type.110), channel_id=1, source_target_pairs={{0,64},{1,65},{2,66},{3,67},{4,68},{5,69},{6,70},{7,71},{8,72},{9,... | collective-permute-start | bytes 221192 | tf_op jit(solution)/shard_map/start/ppermute | solution.py:53
  15.3 4.0 %collective-permute-start.8 = (bf16[4,48,768]{2,1,0:T(8,128)(2,1)S(1)}, bf16[4,48,768]{2,1,0:T(8,128)(2,1)S(1)}, u32[]{:S(2)}, u32[]{:S(2)}) collective-permute-start(bf16[4,48,768]{2,1,0:T(8,128)(2,1)S(1)} %pad_maximum_fusion.1.refs_0_), channel_id=1, source_target_pairs={{0,28},{1,29},{2,30},{3,31},{4,0},{5,1},{6,2},{7,3},{8,4},{9,5},{1... | collective-permute-start | bytes 884744 | tf_op jit(solution)/shard_map/weight_gather/ppermute | solution.py:53
  19.3 5.8 %collective-permute-done.5.refs_6_ = bf16[4,48,768]{2,1,0:T(8,128)(2,1)S(1)} collective-permute-done((bf16[4,48,768]{2,1,0:T(8,128)(2,1)S(1)}, bf16[4,48,768]{2,1,0:T(8,128)(2,1)S(1)}, u32[]{:S(2)}, u32[]{:S(2)}) %collective-permute-start.5) | collective-permute-done | bytes 294944 | tf_op jit(solution)/shard_map/weight_gather/ppermute | solution.py:53
  25.1 2.7 %collective-permute-start.9 = (bf16[4,48,768]{2,1,0:T(8,128)(2,1)S(1)}, bf16[4,48,768]{2,1,0:T(8,128)(2,1)}, u32[]{:S(2)}, u32[]{:S(2)}) collective-permute-start(bf16[4,48,768]{2,1,0:T(8,128)(2,1)S(1)} %collective-permute-done.8.refs_1_), channel_id=1, source_target_pairs={{0,28},{1,29},{2,30},{3,31},{4,0},{5,1},{6,2},{7,3},{8,4},{9,5},{1... | collective-permute-start | bytes 884744 | tf_op jit(solution)/shard_map/weight_gather/ppermute | solution.py:53
  27.8 5.0 %collective-permute-done.6.refs_5_ = bf16[4,48,768]{2,1,0:T(8,128)(2,1)S(1)} collective-permute-done((bf16[4,48,768]{2,1,0:T(8,128)(2,1)S(1)}, bf16[4,48,768]{2,1,0:T(8,128)(2,1)S(1)}, u32[]{:S(2)}, u32[]{:S(2)}) %collective-permute-start.6) | collective-permute-done | bytes 294944 | tf_op jit(solution)/shard_map/weight_gather/ppermute | solution.py:53
  32.9 2.7 %collective-permute-start.10 = (bf16[4,48,768]{2,1,0:T(8,128)(2,1)}, bf16[4,48,768]{2,1,0:T(8,128)(2,1)S(1)}, u32[]{:S(2)}, u32[]{:S(2)}) collective-permute-start(bf16[4,48,768]{2,1,0:T(8,128)(2,1)} %collective-permute-done.9.refs_2_), channel_id=1, source_target_pairs={{0,28},{1,29},{2,30},{3,31},{4,0},{5,1},{6,2},{7,3},{8,4},{9,5},{1... | collective-permute-start | bytes 884744 | tf_op jit(solution)/shard_map/weight_gather/ppermute | solution.py:53
  37.1 4.6 %collective-permute-done.4.b2 = bf16[256,3072]{1,0:T(8,128)(2,1)} collective-permute-done((bf16[256,3072]{1,0:T(8,128)(2,1)}, bf16[256,3072]{1,0:T(8,128)(2,1)}, u32[]{:S(2)}, u32[]{:S(2)}) %collective-permute-start.4) | collective-permute-done | bytes 1572896 | tf_op jit(solution)/shard_map/start/ppermute | solution.py:53
  43.9 3.1 %collective-permute-done.11.b3 = bf16[256,3072]{1,0:T(8,128)(2,1)S(1)} collective-permute-done((bf16[256,3072]{1,0:T(8,128)(2,1)}, bf16[256,3072]{1,0:T(8,128)(2,1)S(1)}, u32[]{:S(2)}, u32[]{:S(2)}) %collective-permute-start.11) | collective-permute-done | bytes 1572896 | tf_op jit(solution)/shard_map/weight_grad/ppermute | solution.py:53
  47.0 7.4 %weight_grad.1 = bf16[2,2,2,8,48,768]{5,4,3,2,1,0:T(8,128)(2,1)S(1)} custom-call(bf16[256,3072]{1,0:T(8,128)(2,1)S(1)} %copy-done.2, bf16[256,3072]{1,0:T(8,128)(2,1)S(1)} %collective-permute-done.3.b1, bf16[256,3072]{1,0:T(8,128)(2,1)} %collective-permute-done.4.b2, bf16[256,3072]{1,0:T(8,128)(2,1)S(1)} %collective-permute-done.11.b3, ...), custom_call_target="tpu_custom_call" | custom-call | flops 4831838208 | bytes 16777216 | tf_op jit(solution)/shard_map/weight_grad/weight_grad/pallas_call | solution.py:85
  54.4 2.2 %copy-done = bf16[2,2,2,8,48,768]{5,4,3,2,1,0:T(8,128)(2,1)} copy-done((bf16[2,2,2,8,48,768]{5,4,3,2,1,0:T(8,128)(2,1)}, bf16[2,2,2,8,48,768]{5,4,3,2,1,0:T(8,128)(2,1)S(1)}, u32[]{:S(2)}) %copy-start) | copy-done | bytes 4718616
  56.6 4.6 %all-to-all-start = ((bf16[8,8,48,768]{3,2,1,0:T(8,128)(2,1)}), bf16[8,8,48,768]{3,2,1,0:T(8,128)(2,1)}, u32[]{:S(2)}, u32[]{:S(2)}) async-start(bf16[8,8,48,768]{3,2,1,0:T(8,128)(2,1)} %bitcast.25), calls=%async_computation | async-start | bytes 9437184 | tf_op jit(solution)/shard_map/grad_scatter/all_to_all | solution.py:170
  61.3 3.5 %collective-permute-start.14 = (bf16[4,48,768]{2,1,0:T(8,128)(2,1)S(1)}, bf16[4,48,768]{2,1,0:T(8,128)(2,1)S(1)}, u32[]{:S(2)}, u32[]{:S(2)}) collective-permute-start(bf16[4,48,768]{2,1,0:T(8,128)(2,1)S(1)} %collective-permute-done.12.refs_9_), channel_id=1, source_target_pairs={{0,28},{1,29},{2,30},{3,31},{4,0},{5,1},{6,2},{7,3},{8,4},{9,5},{1... | collective-permute-start | bytes 884744 | tf_op jit(solution)/shard_map/weight_gather/ppermute | solution.py:53
  64.9 2.7 %collective-permute-start.16 = (bf16[2,48,768]{2,1,0:T(8,128)(2,1)S(1)}, bf16[2,48,768]{2,1,0:T(8,128)(2,1)S(1)}, u32[]{:S(2)}, u32[]{:S(2)}) collective-permute-start(bf16[2,48,768]{2,1,0:T(8,128)(2,1)S(1)} %slice.16), channel_id=1, source_target_pairs={{0,28},{1,29},{2,30},{3,31},{4,0},{5,1},{6,2},{7,3},{8,4},{9,5},{1... | collective-permute-start | bytes 442376 | tf_op jit(solution)/shard_map/weight_gather/ppermute | solution.py:53
  67.6 3.7 %collective-permute-done.13.refs_15_ = bf16[4,48,768]{2,1,0:T(8,128)(2,1)S(1)} collective-permute-done((bf16[4,48,768]{2,1,0:T(8,128)(2,1)S(1)}, bf16[4,48,768]{2,1,0:T(8,128)(2,1)S(1)}, u32[]{:S(2)}, u32[]{:S(2)}) %collective-permute-start.13) | collective-permute-done | bytes 294944 | tf_op jit(solution)/shard_map/weight_gather/ppermute | solution.py:53
  71.4 3.2 %collective-permute-done.15.refs_7_ = bf16[2,48,768]{2,1,0:T(8,128)(2,1)S(1)} collective-permute-done((bf16[2,48,768]{2,1,0:T(8,128)(2,1)S(1)}, bf16[2,48,768]{2,1,0:T(8,128)(2,1)S(1)}, u32[]{:S(2)}, u32[]{:S(2)}) %collective-permute-start.15) | collective-permute-done | bytes 147488 | tf_op jit(solution)/shard_map/weight_gather/ppermute | solution.py:53
  77.3 6.0 %collective-permute-done.19.refs_14_ = bf16[4,48,768]{2,1,0:T(8,128)(2,1)S(1)} collective-permute-done((bf16[4,48,768]{2,1,0:T(8,128)(2,1)S(1)}, bf16[4,48,768]{2,1,0:T(8,128)(2,1)S(1)}, u32[]{:S(2)}, u32[]{:S(2)}) %collective-permute-start.19) | collective-permute-done | bytes 294944 | tf_op jit(solution)/shard_map/weight_gather/ppermute | solution.py:53
  83.8 2.2 %collective-permute-start.18 = (bf16[4,48,768]{2,1,0:T(8,128)(2,1)S(1)}, bf16[4,48,768]{2,1,0:T(8,128)(2,1)S(1)}, u32[]{:S(2)}, u32[]{:S(2)}) collective-permute-start(bf16[4,48,768]{2,1,0:T(8,128)(2,1)S(1)} %collective-permute-done.17.refs_11_), channel_id=1, source_target_pairs={{0,28},{1,29},{2,30},{3,31},{4,0},{5,1},{6,2},{7,3},{8,4},{9,5},{1... | collective-permute-start | bytes 884744 | tf_op jit(solution)/shard_map/weight_gather/ppermute | solution.py:53
  86.0 5.1 %collective-permute-done.20.refs_13_ = bf16[4,48,768]{2,1,0:T(8,128)(2,1)S(1)} collective-permute-done((bf16[4,48,768]{2,1,0:T(8,128)(2,1)S(1)}, bf16[4,48,768]{2,1,0:T(8,128)(2,1)S(1)}, u32[]{:S(2)}, u32[]{:S(2)}) %collective-permute-start.20) | collective-permute-done | bytes 294944 | tf_op jit(solution)/shard_map/weight_gather/ppermute | solution.py:53
  91.3 2.7 %collective-permute-start.22 = (bf16[2,48,768]{2,1,0:T(8,128)(2,1)S(1)}, bf16[2,48,768]{2,1,0:T(8,128)(2,1)S(1)}, u32[]{:S(2)}, u32[]{:S(2)}) collective-permute-start(bf16[2,48,768]{2,1,0:T(8,128)(2,1)S(1)} %slice.21), channel_id=1, source_target_pairs={{0,28},{1,29},{2,30},{3,31},{4,0},{5,1},{6,2},{7,3},{8,4},{9,5},{1... | collective-permute-start | bytes 442376 | tf_op jit(solution)/shard_map/weight_gather/ppermute | solution.py:53
  94.6 2.3 %collective-permute-done.21.refs_16_ = bf16[2,48,768]{2,1,0:T(8,128)(2,1)S(1)} collective-permute-done((bf16[2,48,768]{2,1,0:T(8,128)(2,1)S(1)}, bf16[2,48,768]{2,1,0:T(8,128)(2,1)S(1)}, u32[]{:S(2)}, u32[]{:S(2)}) %collective-permute-start.21) | collective-permute-done | bytes 147488 | tf_op jit(solution)/shard_map/weight_gather/ppermute | solution.py:53
  98.1 10.9 %stream_parts.1 = (bf16[256,3072]{1,0:T(8,128)(2,1)}, bf16[256,3072]{1,0:T(8,128)(2,1)}, bf16[256,3072]{1,0:T(8,128)(2,1)}, bf16[256,3072]{1,0:T(8,128)(2,1)}) custom-call(s32[3]{0:T(128)} %pad_add_fusion.here, bf16[1024,768]{1,0:T(8,128)(2,1)} %copy-done.1, bf16[4,48,768]{2,1,0:T(8,128)(2,1)} %copy-done.5, bf16[4,48,768]{2,1,0:T(8,128)(2,1)} %copy-done.12, ...), custom_call_target="tpu_custom_call" | custom-call | flops 4831838208 | bytes 16777216 | tf_op jit(solution)/shard_map/stream/stream_parts/pallas_call | solution.py:123
  109.0 3.7 %collective-permute-start.23 = (bf16[256,3072]{1,0:T(8,128)(2,1)}, bf16[256,3072]{1,0:T(8,128)(2,1)S(1)}, u32[]{:S(2)}, u32[]{:S(2)}) collective-permute-start(bf16[256,3072]{1,0:T(8,128)(2,1)} %get-tuple-element.34), channel_id=1, source_target_pairs={{0,1},{1,0},{2,3},{3,2},{4,5},{5,4},{6,7},{7,6},{8,9},{9,8},{10,11... | collective-permute-start | bytes 4718600 | tf_op jit(solution)/shard_map/stream/ppermute | solution.py:53
  112.8 3.1 %collective-permute-done.23 = bf16[256,3072]{1,0:T(8,128)(2,1)S(1)} collective-permute-done((bf16[256,3072]{1,0:T(8,128)(2,1)}, bf16[256,3072]{1,0:T(8,128)(2,1)S(1)}, u32[]{:S(2)}, u32[]{:S(2)}) %collective-permute-start.23) | collective-permute-done | bytes 1572896 | tf_op jit(solution)/shard_map/stream/ppermute | solution.py:53
  115.9 3.1 %add_convert_fusion = bf16[256,3072]{1,0:T(8,128)(2,1)} fusion(bf16[256,3072]{1,0:T(8,128)(2,1)S(1)} %collective-permute-done.23, bf16[256,3072]{1,0:T(8,128)(2,1)} %get-tuple-element.33), kind=kLoop, calls=%fused_computation.2 | loop fusion | flops 3145728 | bytes 4718592 | tf_op jit(solution)/shard_map/stream/convert_element_type | solution.py:187
  119.1 2.6 %collective-permute-start.25 = (bf16[256,3072]{1,0:T(8,128)(2,1)}, bf16[256,3072]{1,0:T(8,128)(2,1)}, u32[]{:S(2)}, u32[]{:S(2)}) collective-permute-start(bf16[256,3072]{1,0:T(8,128)(2,1)} %add_convert_fusion), channel_id=1, source_target_pairs={{0,2},{1,3},{2,0},{3,1},{4,6},{5,7},{6,4},{7,5},{8,10},{9,11},{10,... | collective-permute-start | bytes 4718600 | tf_op jit(solution)/shard_map/stream/ppermute | solution.py:53
  121.7 2.9 %fusion.1 = bf16[8,48,768]{2,1,0:T(8,128)(2,1)S(1)} fusion(bf16[8,8,48,768]{3,2,1,0:T(8,128)(2,1)} %all-to-all-done), kind=kLoop, calls=%fused_computation.6 | loop fusion | flops 4718592 | bytes 5308416 | tf_op jit(solution)/shard_map/grad_scatter/convert_element_type | solution.py:192
  124.6 22.2 %all_to_all.20 = bf16[8,48,768]{2,1,0:T(8,128)(2,1)S(1)} all-to-all(bf16[8,48,768]{2,1,0:T(8,128)(2,1)S(1)} %fusion.1), channel_id=1, replica_groups=mesh['yl'=2,'xa'=2,'xb'=2,'z'=8,'yh'=2,'c'=2] {'z'}, dimensions={0} | all-to-all | bytes 1179648 | tf_op jit(solution)/shard_map/grad_scatter/all_to_all | solution.py:193
  148.6 10.5 %all-to-all-start.2 = ((f32[32,1,128]{2,1,0:T(1,128)}), f32[32,1,128]{2,1,0:T(1,128)S(1)}, u32[]{:S(2)}, u32[]{:S(2)}) async-start(f32[32,1,128]{2,1,0:T(1,128)} %broadcast_in_dim.4), calls=%async_computation.2 | async-start | bytes 32768 | tf_op jit(solution)/shard_map/norm/all_to_all | solution.py:58
  159.1 4.1 %multiply_convert_fusion = (bf16[256,3072]{1,0:T(8,128)(2,1)}, bf16[256,3072]{1,0:T(8,128)(2,1)}) fusion(bf16[256,3072]{1,0:T(8,128)(2,1)} %collective-permute-done.25, bf16[256,3072]{1,0:T(8,128)(2,1)S(1)} %collective-permute-done.24, bf16[256,3072]{1,0:T(8,128)(2,1)S(1)} %copy-done.3, f32[3072]{0:T(1024)S(1)} %bitcast.30), kind=kLoop, calls=%fused_computation | loop fusion | flops 6291456 | bytes 7876608 | tf_op jit(solution)/shard_map/norm/convert_element_type | solution.py:200
  163.2 2.7 %all-to-all-done.2 = f32[32,1,128]{2,1,0:T(1,128)S(1)} async-done(((f32[32,1,128]{2,1,0:T(1,128)}), f32[32,1,128]{2,1,0:T(1,128)S(1)}, u32[]{:S(2)}, u32[]{:S(2)}) %all-to-all-start.2) | async-done | bytes 16416 | tf_op jit(solution)/shard_map/norm/all_to_all | solution.py:58
  166.0 8.9 %all_to_all.21 = f32[8,1,128]{2,1,0:T(1,128)S(1)} all-to-all(f32[8,1,128]{2,1,0:T(1,128)S(1)} %broadcast_in_dim.10), channel_id=1, replica_groups=mesh['yl'=2,'xa'=2,'xb'=2,'z'=8,'yh'=2,'c'=2] {'z'}, dimensions={0} | all-to-all | bytes 8192 | tf_op jit(solution)/shard_map/norm/all_to_all | solution.py:58
  (93 shorter events, 21.8 us)
Async XLA Ops:
  0.6 13.0 %collective-permute-start.3 = (bf16[256,3072]{1,0:T(8,128)(2,1)}, bf16[256,3072]{1,0:T(8,128)(2,1)S(1)}, u32[]{:S(2)}, u32[]{:S(2)}) collective-permute-start(bf16[256,3072]{1,0:T(8,128)(2,1)} %b0.1), channel_id=1, source_target_pairs={{0,1},{1,0},{2,3},{3,2},{4,5},{5,4},{6,7},{7,6},{8,9},{9,8},{10,11... | collective-permute-start | bytes 4718600 | tf_op jit(solution)/shard_map/start/ppermute | solution.py:53
  4.0 37.8 %collective-permute-start.4 = (bf16[256,3072]{1,0:T(8,128)(2,1)}, bf16[256,3072]{1,0:T(8,128)(2,1)}, u32[]{:S(2)}, u32[]{:S(2)}) collective-permute-start(bf16[256,3072]{1,0:T(8,128)(2,1)} %b0.1), channel_id=1, source_target_pairs={{0,2},{1,3},{2,0},{3,1},{4,6},{5,7},{6,4},{7,5},{8,10},{9,11},{10,... | collective-permute-start | bytes 4718600 | tf_op jit(solution)/shard_map/start/ppermute | solution.py:53
  6.1 5.8 %collective-permute-start.2 = (bf16[48,768]{1,0:T(8,128)(2,1)S(1)}, bf16[48,768]{1,0:T(8,128)(2,1)S(1)}, u32[]{:S(2)}, u32[]{:S(2)}) collective-permute-start(bf16[48,768]{1,0:T(8,128)(2,1)S(1)} %convert_element_type.110), channel_id=1, source_target_pairs={{0,32},{1,33},{2,34},{3,35},{4,36},{5,37},{6,38},{7,39},{8,40},{9,... | collective-permute-start | bytes 221192 | tf_op jit(solution)/shard_map/start/ppermute | solution.py:53
  7.4 6.2 %collective-permute-start.1 = (bf16[48,768]{1,0:T(8,128)(2,1)S(1)}, bf16[48,768]{1,0:T(8,128)(2,1)S(1)}, u32[]{:S(2)}, u32[]{:S(2)}) collective-permute-start(bf16[48,768]{1,0:T(8,128)(2,1)S(1)} %convert_element_type.110), channel_id=1, source_target_pairs={{0,64},{1,65},{2,66},{3,67},{4,68},{5,69},{6,70},{7,71},{8,72},{9,... | collective-permute-start | bytes 221192 | tf_op jit(solution)/shard_map/start/ppermute | solution.py:53
  9.8 3.7 %collective-permute-start = (bf16[48,768]{1,0:T(8,128)(2,1)S(1)}, bf16[48,768]{1,0:T(8,128)(2,1)S(1)}, u32[]{:S(2)}, u32[]{:S(2)}) collective-permute-start(bf16[48,768]{1,0:T(8,128)(2,1)S(1)} %convert_element_type.110), channel_id=1, source_target_pairs={{0,96},{1,97},{2,98},{3,99},{4,100},{5,101},{6,102},{7,103},{8,104... | collective-permute-start | bytes 221192 | tf_op jit(solution)/shard_map/start/ppermute | solution.py:53
  13.6 30.2 %copy-start.5 = (bf16[4,48,768]{2,1,0:T(8,128)(2,1)}, bf16[4,48,768]{2,1,0:T(8,128)(2,1)S(1)}, u32[]{:S(2)}) copy-start(bf16[4,48,768]{2,1,0:T(8,128)(2,1)S(1)} %pad_maximum_fusion.1.refs_0_) | copy-start | bytes 884740
  13.6 11.5 %collective-permute-start.5 = (bf16[4,48,768]{2,1,0:T(8,128)(2,1)S(1)}, bf16[4,48,768]{2,1,0:T(8,128)(2,1)S(1)}, u32[]{:S(2)}, u32[]{:S(2)}) collective-permute-start(bf16[4,48,768]{2,1,0:T(8,128)(2,1)S(1)} %pad_maximum_fusion.1.refs_0_), channel_id=1, source_target_pairs={{0,4},{1,5},{2,6},{3,7},{4,8},{5,9},{6,10},{7,11},{8,12},{9,13},{1... | collective-permute-start | bytes 884744 | tf_op jit(solution)/shard_map/weight_gather/ppermute | solution.py:53
  15.3 9.8 %collective-permute-start.8 = (bf16[4,48,768]{2,1,0:T(8,128)(2,1)S(1)}, bf16[4,48,768]{2,1,0:T(8,128)(2,1)S(1)}, u32[]{:S(2)}, u32[]{:S(2)}) collective-permute-start(bf16[4,48,768]{2,1,0:T(8,128)(2,1)S(1)} %pad_maximum_fusion.1.refs_0_), channel_id=1, source_target_pairs={{0,28},{1,29},{2,30},{3,31},{4,0},{5,1},{6,2},{7,3},{8,4},{9,5},{1... | collective-permute-start | bytes 884744 | tf_op jit(solution)/shard_map/weight_gather/ppermute | solution.py:53
  25.1 7.7 %collective-permute-start.6 = (bf16[4,48,768]{2,1,0:T(8,128)(2,1)S(1)}, bf16[4,48,768]{2,1,0:T(8,128)(2,1)S(1)}, u32[]{:S(2)}, u32[]{:S(2)}) collective-permute-start(bf16[4,48,768]{2,1,0:T(8,128)(2,1)S(1)} %collective-permute-done.5.refs_6_), channel_id=1, source_target_pairs={{0,4},{1,5},{2,6},{3,7},{4,8},{5,9},{6,10},{7,11},{8,12},{9,13},{1... | collective-permute-start | bytes 884744 | tf_op jit(solution)/shard_map/weight_gather/ppermute | solution.py:53
  25.1 7.7 %collective-permute-start.9 = (bf16[4,48,768]{2,1,0:T(8,128)(2,1)S(1)}, bf16[4,48,768]{2,1,0:T(8,128)(2,1)}, u32[]{:S(2)}, u32[]{:S(2)}) collective-permute-start(bf16[4,48,768]{2,1,0:T(8,128)(2,1)S(1)} %collective-permute-done.8.refs_1_), channel_id=1, source_target_pairs={{0,28},{1,29},{2,30},{3,31},{4,0},{5,1},{6,2},{7,3},{8,4},{9,5},{1... | collective-permute-start | bytes 884744 | tf_op jit(solution)/shard_map/weight_gather/ppermute | solution.py:53
  32.8 8.9 %collective-permute-start.7 = (bf16[4,48,768]{2,1,0:T(8,128)(2,1)S(1)}, bf16[4,48,768]{2,1,0:T(8,128)(2,1)S(1)}, u32[]{:S(2)}, u32[]{:S(2)}) collective-permute-start(bf16[4,48,768]{2,1,0:T(8,128)(2,1)S(1)} %collective-permute-done.6.refs_5_), channel_id=1, source_target_pairs={{0,4},{1,5},{2,6},{3,7},{4,8},{5,9},{6,10},{7,11},{8,12},{9,13},{1... | collective-permute-start | bytes 884744 | tf_op jit(solution)/shard_map/weight_gather/ppermute | solution.py:53
  32.9 8.9 %collective-permute-start.10 = (bf16[4,48,768]{2,1,0:T(8,128)(2,1)}, bf16[4,48,768]{2,1,0:T(8,128)(2,1)S(1)}, u32[]{:S(2)}, u32[]{:S(2)}) collective-permute-start(bf16[4,48,768]{2,1,0:T(8,128)(2,1)} %collective-permute-done.9.refs_2_), channel_id=1, source_target_pairs={{0,28},{1,29},{2,30},{3,31},{4,0},{5,1},{6,2},{7,3},{8,4},{9,5},{1... | collective-permute-start | bytes 884744 | tf_op jit(solution)/shard_map/weight_gather/ppermute | solution.py:53
  41.8 5.3 %collective-permute-start.11 = (bf16[256,3072]{1,0:T(8,128)(2,1)}, bf16[256,3072]{1,0:T(8,128)(2,1)S(1)}, u32[]{:S(2)}, u32[]{:S(2)}) collective-permute-start(bf16[256,3072]{1,0:T(8,128)(2,1)} %collective-permute-done.4.b2), channel_id=1, source_target_pairs={{0,1},{1,0},{2,3},{3,2},{4,5},{5,4},{6,7},{7,6},{8,9},{9,8},{10,11... | collective-permute-start | bytes 4718600 | tf_op jit(solution)/shard_map/weight_grad/ppermute | solution.py:53
  43.8 17.4 %collective-permute-start.12 = (bf16[4,48,768]{2,1,0:T(8,128)(2,1)S(1)}, bf16[4,48,768]{2,1,0:T(8,128)(2,1)S(1)}, u32[]{:S(2)}, u32[]{:S(2)}) collective-permute-start(bf16[4,48,768]{2,1,0:T(8,128)(2,1)S(1)} %pad_maximum_fusion.1.refs_0_), channel_id=1, source_target_pairs={{0,128},{1,129},{2,130},{3,131},{4,132},{5,133},{6,134},{7,135},{8... | collective-permute-start | bytes 884744 | tf_op jit(solution)/shard_map/start/ppermute | solution.py:53
  56.6 65.1 %all-to-all-start = ((bf16[8,8,48,768]{3,2,1,0:T(8,128)(2,1)}), bf16[8,8,48,768]{3,2,1,0:T(8,128)(2,1)}, u32[]{:S(2)}, u32[]{:S(2)}) async-start(bf16[8,8,48,768]{3,2,1,0:T(8,128)(2,1)} %bitcast.25), calls=%async_computation | async-start | bytes 9437184 | tf_op jit(solution)/shard_map/grad_scatter/all_to_all | solution.py:170
  61.2 35.6 %copy-start.14 = (bf16[4,48,768]{2,1,0:T(8,128)(2,1)}, bf16[4,48,768]{2,1,0:T(8,128)(2,1)S(1)}, u32[]{:S(2)}) copy-start(bf16[4,48,768]{2,1,0:T(8,128)(2,1)S(1)} %collective-permute-done.12.refs_9_) | copy-start | bytes 884740
  61.2 10.1 %collective-permute-start.13 = (bf16[4,48,768]{2,1,0:T(8,128)(2,1)S(1)}, bf16[4,48,768]{2,1,0:T(8,128)(2,1)S(1)}, u32[]{:S(2)}, u32[]{:S(2)}) collective-permute-start(bf16[4,48,768]{2,1,0:T(8,128)(2,1)S(1)} %collective-permute-done.12.refs_9_), channel_id=1, source_target_pairs={{0,4},{1,5},{2,6},{3,7},{4,8},{5,9},{6,10},{7,11},{8,12},{9,13},{1... | collective-permute-start | bytes 884744 | tf_op jit(solution)/shard_map/weight_gather/ppermute | solution.py:53
  61.3 10.1 %collective-permute-start.14 = (bf16[4,48,768]{2,1,0:T(8,128)(2,1)S(1)}, bf16[4,48,768]{2,1,0:T(8,128)(2,1)S(1)}, u32[]{:S(2)}, u32[]{:S(2)}) collective-permute-start(bf16[4,48,768]{2,1,0:T(8,128)(2,1)S(1)} %collective-permute-done.12.refs_9_), channel_id=1, source_target_pairs={{0,28},{1,29},{2,30},{3,31},{4,0},{5,1},{6,2},{7,3},{8,4},{9,5},{1... | collective-permute-start | bytes 884744 | tf_op jit(solution)/shard_map/weight_gather/ppermute | solution.py:53
  64.8 9.7 %collective-permute-start.15 = (bf16[2,48,768]{2,1,0:T(8,128)(2,1)S(1)}, bf16[2,48,768]{2,1,0:T(8,128)(2,1)S(1)}, u32[]{:S(2)}, u32[]{:S(2)}) collective-permute-start(bf16[2,48,768]{2,1,0:T(8,128)(2,1)S(1)} %slice.15), channel_id=1, source_target_pairs={{0,4},{1,5},{2,6},{3,7},{4,8},{5,9},{6,10},{7,11},{8,12},{9,13},{1... | collective-permute-start | bytes 442376 | tf_op jit(solution)/shard_map/weight_gather/ppermute | solution.py:53
  64.9 9.6 %collective-permute-start.16 = (bf16[2,48,768]{2,1,0:T(8,128)(2,1)S(1)}, bf16[2,48,768]{2,1,0:T(8,128)(2,1)S(1)}, u32[]{:S(2)}, u32[]{:S(2)}) collective-permute-start(bf16[2,48,768]{2,1,0:T(8,128)(2,1)S(1)} %slice.16), channel_id=1, source_target_pairs={{0,28},{1,29},{2,30},{3,31},{4,0},{5,1},{6,2},{7,3},{8,4},{9,5},{1... | collective-permute-start | bytes 442376 | tf_op jit(solution)/shard_map/weight_gather/ppermute | solution.py:53
  74.5 8.8 %collective-permute-start.19 = (bf16[4,48,768]{2,1,0:T(8,128)(2,1)S(1)}, bf16[4,48,768]{2,1,0:T(8,128)(2,1)S(1)}, u32[]{:S(2)}, u32[]{:S(2)}) collective-permute-start(bf16[4,48,768]{2,1,0:T(8,128)(2,1)S(1)} %collective-permute-done.13.refs_15_), channel_id=1, source_target_pairs={{0,4},{1,5},{2,6},{3,7},{4,8},{5,9},{6,10},{7,11},{8,12},{9,13},{1... | collective-permute-start | bytes 884744 | tf_op jit(solution)/shard_map/weight_gather/ppermute | solution.py:53
  76.3 7.5 %collective-permute-start.17 = (bf16[4,48,768]{2,1,0:T(8,128)(2,1)S(1)}, bf16[4,48,768]{2,1,0:T(8,128)(2,1)S(1)}, u32[]{:S(2)}, u32[]{:S(2)}) collective-permute-start(bf16[4,48,768]{2,1,0:T(8,128)(2,1)S(1)} %collective-permute-done.14.refs_10_), channel_id=1, source_target_pairs={{0,28},{1,29},{2,30},{3,31},{4,0},{5,1},{6,2},{7,3},{8,4},{9,5},{1... | collective-permute-start | bytes 884744 | tf_op jit(solution)/shard_map/weight_gather/ppermute | solution.py:53
  83.3 7.8 %collective-permute-start.20 = (bf16[4,48,768]{2,1,0:T(8,128)(2,1)S(1)}, bf16[4,48,768]{2,1,0:T(8,128)(2,1)S(1)}, u32[]{:S(2)}, u32[]{:S(2)}) collective-permute-start(bf16[4,48,768]{2,1,0:T(8,128)(2,1)S(1)} %collective-permute-done.19.refs_14_), channel_id=1, source_target_pairs={{0,4},{1,5},{2,6},{3,7},{4,8},{5,9},{6,10},{7,11},{8,12},{9,13},{1... | collective-permute-start | bytes 884744 | tf_op jit(solution)/shard_map/weight_gather/ppermute | solution.py:53
  83.8 7.4 %collective-permute-start.18 = (bf16[4,48,768]{2,1,0:T(8,128)(2,1)S(1)}, bf16[4,48,768]{2,1,0:T(8,128)(2,1)S(1)}, u32[]{:S(2)}, u32[]{:S(2)}) collective-permute-start(bf16[4,48,768]{2,1,0:T(8,128)(2,1)S(1)} %collective-permute-done.17.refs_11_), channel_id=1, source_target_pairs={{0,28},{1,29},{2,30},{3,31},{4,0},{5,1},{6,2},{7,3},{8,4},{9,5},{1... | collective-permute-start | bytes 884744 | tf_op jit(solution)/shard_map/weight_gather/ppermute | solution.py:53
  91.2 5.7 %collective-permute-start.21 = (bf16[2,48,768]{2,1,0:T(8,128)(2,1)S(1)}, bf16[2,48,768]{2,1,0:T(8,128)(2,1)S(1)}, u32[]{:S(2)}, u32[]{:S(2)}) collective-permute-start(bf16[2,48,768]{2,1,0:T(8,128)(2,1)S(1)} %slice.20), channel_id=1, source_target_pairs={{0,4},{1,5},{2,6},{3,7},{4,8},{5,9},{6,10},{7,11},{8,12},{9,13},{1... | collective-permute-start | bytes 442376 | tf_op jit(solution)/shard_map/weight_gather/ppermute | solution.py:53
  91.3 5.6 %collective-permute-start.22 = (bf16[2,48,768]{2,1,0:T(8,128)(2,1)S(1)}, bf16[2,48,768]{2,1,0:T(8,128)(2,1)S(1)}, u32[]{:S(2)}, u32[]{:S(2)}) collective-permute-start(bf16[2,48,768]{2,1,0:T(8,128)(2,1)S(1)} %slice.21), channel_id=1, source_target_pairs={{0,28},{1,29},{2,30},{3,31},{4,0},{5,1},{6,2},{7,3},{8,4},{9,5},{1... | collective-permute-start | bytes 442376 | tf_op jit(solution)/shard_map/weight_gather/ppermute | solution.py:53
  109.0 6.9 %collective-permute-start.23 = (bf16[256,3072]{1,0:T(8,128)(2,1)}, bf16[256,3072]{1,0:T(8,128)(2,1)S(1)}, u32[]{:S(2)}, u32[]{:S(2)}) collective-permute-start(bf16[256,3072]{1,0:T(8,128)(2,1)} %get-tuple-element.34), channel_id=1, source_target_pairs={{0,1},{1,0},{2,3},{3,2},{4,5},{5,4},{6,7},{7,6},{8,9},{9,8},{10,11... | collective-permute-start | bytes 4718600 | tf_op jit(solution)/shard_map/stream/ppermute | solution.py:53
  112.7 6.4 %collective-permute-start.24 = (bf16[256,3072]{1,0:T(8,128)(2,1)}, bf16[256,3072]{1,0:T(8,128)(2,1)S(1)}, u32[]{:S(2)}, u32[]{:S(2)}) collective-permute-start(bf16[256,3072]{1,0:T(8,128)(2,1)} %get-tuple-element.35), channel_id=1, source_target_pairs={{0,1},{1,0},{2,3},{3,2},{4,5},{5,4},{6,7},{7,6},{8,9},{9,8},{10,11... | collective-permute-start | bytes 4718600 | tf_op jit(solution)/shard_map/stream/ppermute | solution.py:53
  119.1 40.0 %collective-permute-start.25 = (bf16[256,3072]{1,0:T(8,128)(2,1)}, bf16[256,3072]{1,0:T(8,128)(2,1)}, u32[]{:S(2)}, u32[]{:S(2)}) collective-permute-start(bf16[256,3072]{1,0:T(8,128)(2,1)} %add_convert_fusion), channel_id=1, source_target_pairs={{0,2},{1,3},{2,0},{3,1},{4,6},{5,7},{6,4},{7,5},{8,10},{9,11},{10,... | collective-permute-start | bytes 4718600 | tf_op jit(solution)/shard_map/stream/ppermute | solution.py:53
  124.6 34.5 %copy-start.3 = (bf16[256,3072]{1,0:T(8,128)(2,1)S(1)}, bf16[256,3072]{1,0:T(8,128)(2,1)}, u32[]{:S(2)}) copy-start(bf16[256,3072]{1,0:T(8,128)(2,1)} %get-tuple-element.32) | copy-start | bytes 4718596
  124.6 34.5 %copy-start.10 = (f32[1,3072]{1,0:T(1,128)S(1)}, f32[1,3072]{1,0:T(1,128)}, u32[]{:S(2)}) copy-start(f32[1,3072]{1,0:T(1,128)} %param.7) | copy-start | bytes 36868
  148.6 17.3 %all-to-all-start.2 = ((f32[32,1,128]{2,1,0:T(1,128)}), f32[32,1,128]{2,1,0:T(1,128)S(1)}, u32[]{:S(2)}, u32[]{:S(2)}) async-start(f32[32,1,128]{2,1,0:T(1,128)} %broadcast_in_dim.4), calls=%async_computation.2 | async-start | bytes 32768 | tf_op jit(solution)/shard_map/norm/all_to_all | solution.py:58
  (19 other events, 254.4 us)
